TPU v7x, 256 devices: a whole 4x4x8 slice. The times are simulated.
256 devices in a mesh: ctx: 8 (over x, core), tp: 32 (over z, y).
Axes of the slice: x: 4, y: 4, z: 8, core: 2. Of those that a mesh axis runs over, the one named last changes fastest.
Arguments:
- streams: bfloat16 [16384, 3, 4096], P('ctx', None, 'tp'), may hold values from -6 to 6
- short_filter: float32 [3, 3, 4096], P(None, None, 'tp'), may hold values from -4 to 4
- residue: float32 [16, 4096], P(None, 'tp'), may hold values from -1.5 to 1.5
- decay_rate: float32 [16, 4096], P(None, 'tp'), may hold values from 1.8310547e-05 to 0.1
- skip_gain: float32 [4096], P('tp'), may hold values from -4 to 4
- out_weight: bfloat16 [4096, 4096], P(None, 'tp'), may hold values from -0.09375 to 0.09375
Outputs:
- projected: bfloat16 [16384, 4096], P('ctx', 'tp')
All inputs are finite; a program needn't handle non-finite values.
Results may differ from a plain program's by a relative error of at most 0.0065.
Values may be sent and summed in bfloat16 or wider, within the bound.
No kernel may reach another device: no remote copies, remote signals or barrier semaphores. Data moves between devices by JAX's collectives and lax.ppermute only.
A program may use at most 128 MiB of HBM per device.

v0:
```python
import math

import jax
import jax.numpy as jnp
from jax import lax
from jax.sharding import PartitionSpec as P

HIGHEST = lax.Precision.HIGHEST
TWO_PI = 2.0 * math.pi


def from_behind(value, axis, steps):
    count = lax.axis_size(axis)
    first, last = (max(0, -steps), min(count, count - steps))
    return lax.ppermute(value, axis, [(source, source + steps) for source in range(first, last)])


def featurize(streams, short_filter):
    tap_count = short_filter.shape[0]
    row_count = streams.shape[0]
    tails = streams[row_count - (tap_count - 1) :]
    earlier = from_behind(tails, "ctx", 1)
    padded = jnp.concatenate([earlier, streams], axis=0).astype(jnp.float32)
    feat = jnp.zeros(streams.shape, jnp.float32)
    for tap_index in range(tap_count):
        feat = feat + short_filter[tap_index][None] * padded[tap_index : tap_index + row_count]
    return feat


def angle_table(first, second, period):
    phase = first[:, None] * second[None, :] % period
    return TWO_PI * phase.astype(jnp.float32) / period


def spectral(signal_cols, residue_cols, rate_cols, seq_len):
    fast_len = 128
    slow_len = 2 * seq_len // fast_len
    live_len = seq_len // fast_len
    fft_len = 2 * seq_len
    group_count = signal_cols.shape[0]
    blocks = signal_cols.reshape(group_count, live_len, fast_len)
    slow_in = jnp.arange(live_len, dtype=jnp.int32)
    slow_out = jnp.arange(slow_len, dtype=jnp.int32)
    fast_index = jnp.arange(fast_len, dtype=jnp.int32)
    first_angle = angle_table(slow_in, slow_out, slow_len)
    first_cos = jnp.cos(first_angle)
    first_sin = jnp.sin(first_angle)
    section_re = jnp.einsum("cmn,mk->ckn", blocks, first_cos, precision=HIGHEST)
    section_im = -jnp.einsum("cmn,mk->ckn", blocks, first_sin, precision=HIGHEST)
    twiddle = angle_table(slow_out, fast_index, fft_len)
    twid_cos = jnp.cos(twiddle)[None]
    twid_sin = jnp.sin(twiddle)[None]
    turned_re = section_re * twid_cos + section_im * twid_sin
    turned_im = section_im * twid_cos - section_re * twid_sin
    second_angle = angle_table(fast_index, fast_index, fast_len)
    second_cos = jnp.cos(second_angle)
    second_sin = jnp.sin(second_angle)
    freq_re = jnp.einsum("ckn,nq->ckq", turned_re, second_cos, precision=HIGHEST) + jnp.einsum(
        "ckn,nq->ckq", turned_im, second_sin, precision=HIGHEST
    )
    freq_im = jnp.einsum("ckn,nq->ckq", turned_im, second_cos, precision=HIGHEST) - jnp.einsum(
        "ckn,nq->ckq", turned_re, second_sin, precision=HIGHEST
    )
    frequency = slow_out[:, None] + slow_len * fast_index[None, :]
    theta = TWO_PI * frequency.astype(jnp.float32) / fft_len
    parity = (1 - 2 * (frequency % 2)).astype(jnp.float32)[None]
    half_sin = jnp.sin(0.5 * theta)[None]
    full_sin = jnp.sin(theta)[None]

    def add_mode(mode_index, carried):
        spec_re, spec_im = carried
        rate_row = lax.dynamic_index_in_dim(rate_cols, mode_index, 0, keepdims=False)[:, None, None]
        residue_row = lax.dynamic_index_in_dim(residue_cols, mode_index, 0, keepdims=False)[
            :, None, None
        ]
        mode_weight = residue_row * jnp.sqrt(2.0 * rate_row)
        decay = jnp.exp(-rate_row)
        numer = 1.0 - jnp.exp(-rate_row * seq_len) * parity
        denom_re = -jnp.expm1(-rate_row) + 2.0 * decay * half_sin * half_sin
        denom_im = decay * full_sin
        factor = mode_weight * numer / (denom_re * denom_re + denom_im * denom_im)
        return (spec_re + factor * denom_re, spec_im - factor * denom_im)

    empty = jnp.zeros((group_count, slow_len, fast_len), jnp.float32)
    spec_re, spec_im = lax.fori_loop(0, rate_cols.shape[0], add_mode, (empty, empty))
    prod_re = freq_re * spec_re - freq_im * spec_im
    prod_im = freq_re * spec_im + freq_im * spec_re
    back_re = jnp.einsum("ckq,qn->ckn", prod_re, second_cos, precision=HIGHEST) - jnp.einsum(
        "ckq,qn->ckn", prod_im, second_sin, precision=HIGHEST
    )
    back_im = jnp.einsum("ckq,qn->ckn", prod_im, second_cos, precision=HIGHEST) + jnp.einsum(
        "ckq,qn->ckn", prod_re, second_sin, precision=HIGHEST
    )
    unturn_re = back_re * twid_cos - back_im * twid_sin
    unturn_im = back_im * twid_cos + back_re * twid_sin
    result = jnp.einsum("ckn,mk->cmn", unturn_re, first_cos, precision=HIGHEST) - jnp.einsum(
        "ckn,mk->cmn", unturn_im, first_sin, precision=HIGHEST
    )
    return (result / fft_len).reshape(group_count, seq_len)


def shards(streams, short_filter, residue, decay_rate, skip_gain, out_weight):
    feat = featurize(streams, short_filter)
    signal = feat[:, 1, :] * feat[:, 2, :]
    signal_cols = signal.T
    chan_count, local_len = signal_cols.shape
    group_total = lax.axis_size("ctx")
    per_group = chan_count // group_total
    by_channel = lax.all_to_all(signal_cols, "ctx", split_axis=0, concat_axis=1, tiled=True)
    offset = lax.axis_index("ctx") * per_group
    residue_cols = lax.dynamic_slice_in_dim(residue, offset, per_group, 1)
    rate_cols = lax.dynamic_slice_in_dim(decay_rate, offset, per_group, 1)
    filtered = spectral(by_channel, residue_cols, rate_cols, local_len * group_total)
    mixed_cols = lax.all_to_all(filtered, "ctx", split_axis=1, concat_axis=0, tiled=True)
    conv = mixed_cols.T + skip_gain[None, :] * signal
    gated = (feat[:, 0, :] * conv).astype(jnp.bfloat16)
    summed = jnp.dot(
        lax.all_gather(gated, "tp", axis=1, tiled=True),
        out_weight,
        preferred_element_type=jnp.float32,
    )
    return summed.astype(jnp.bfloat16)


def solution(mesh):
    in_specs = (
        P("ctx", None, "tp"),
        P(None, None, "tp"),
        P(None, "tp"),
        P(None, "tp"),
        P("tp"),
        P(None, "tp"),
    )
    out_specs = P("ctx", "tp")
    return jax.shard_map(shards, mesh=mesh, in_specs=in_specs, out_specs=out_specs, check_vma=False)
```

profile of v0, /device:TPU:2, one launch (start us, length us, event | category | flops | bytes accessed | tf_op | source)
XLA Modules:
  0.0 368.1 jit_solution(8982667567525190956)
XLA Ops:
  21.0 5.8 %all-to-all-start = ((f32[8,16,2048]{2,1,0:T(8,128)}), f32[8,16,2048]{2,1,0:T(8,128)}, u32[]{:S(2)}, u32[]{:S(2)}) async-start(f32[8,16,2048]{2,1,0:T(8,128)} %bitcast.113), calls=%async_computation | async-start | bytes 2097152 | tf_op jit(solution)/shard_map/all_to_all | solution.py:109
  26.8 126.9 %while.19 = (s32[]{:T(128)}, f32[16,256,128]{2,1,0:T(8,128)S(1)}, f32[16,256,128]{2,1,0:T(8,128)}, f32[16,16]{1,0:T(8,128)}, f32[16,16]{1,0:T(8,128)}, /*index=5*/s32[128]{0:T(128)S(1)}, s32[]{:T(128)}, s32[]{:T(128)}) while((s32[]{:T(128)}, f32[16,256,128]{2,1,0:T(8,128)S(1)}, ...), condition=%wide.region_1.2_spmd.clone.clone.clone.clone, body=%wide.region_0.1_spmd.clone.clone.clone.clone.sunk | while | flops 9535587 | bytes 9177131 | solution.py:85
  29.6 4.2 %fusion.169 = (f32[16,256,128]{2,1,0:T(8,128)}, f32[16,256,128]{2,1,0:T(8,128)S(1)}) fusion(f32[16,256,128]{2,1,0:T(8,128)} %get-tuple-element.336, f32[256,128]{1,0:T(8,128)S(1)} %get-tuple-element.317, f32[16]{0:T(128)S(1)} %get-tuple-element.319, f32[256,128]{1,0:T(8,128)S(1)} %get-tuple-element.320, f32[16]{0:T(128)} %broadcast_multiply_fusion.2, ...), kind=kLoop, calls=%fused_computation.7.clone.1 | loop fusion | flops 8912896 | bytes 8782145 | tf_op jit(solution)/shard_map/while/body/eval_jaxpr/sub | solution.py:82
  36.7 5.1 %fusion.169 = (f32[16,256,128]{2,1,0:T(8,128)}, f32[16,256,128]{2,1,0:T(8,128)S(1)}) fusion(f32[16,256,128]{2,1,0:T(8,128)} %get-tuple-element.336, f32[256,128]{1,0:T(8,128)S(1)} %get-tuple-element.317, f32[16]{0:T(128)S(1)} %get-tuple-element.319, f32[256,128]{1,0:T(8,128)S(1)} %get-tuple-element.320, f32[16]{0:T(128)} %broadcast_multiply_fusion.2, ...), kind=kLoop, calls=%fused_computation.7.clone.1 | loop fusion | flops 8912896 | bytes 8782145 | tf_op jit(solution)/shard_map/while/body/eval_jaxpr/sub | solution.py:82
  44.7 5.1 %fusion.169 = (f32[16,256,128]{2,1,0:T(8,128)}, f32[16,256,128]{2,1,0:T(8,128)S(1)}) fusion(f32[16,256,128]{2,1,0:T(8,128)} %get-tuple-element.336, f32[256,128]{1,0:T(8,128)S(1)} %get-tuple-element.317, f32[16]{0:T(128)S(1)} %get-tuple-element.319, f32[256,128]{1,0:T(8,128)S(1)} %get-tuple-element.320, f32[16]{0:T(128)} %broadcast_multiply_fusion.2, ...), kind=kLoop, calls=%fused_computation.7.clone.1 | loop fusion | flops 8912896 | bytes 8782145 | tf_op jit(solution)/shard_map/while/body/eval_jaxpr/sub | solution.py:82
  52.6 5.1 %fusion.169 = (f32[16,256,128]{2,1,0:T(8,128)}, f32[16,256,128]{2,1,0:T(8,128)S(1)}) fusion(f32[16,256,128]{2,1,0:T(8,128)} %get-tuple-element.336, f32[256,128]{1,0:T(8,128)S(1)} %get-tuple-element.317, f32[16]{0:T(128)S(1)} %get-tuple-element.319, f32[256,128]{1,0:T(8,128)S(1)} %get-tuple-element.320, f32[16]{0:T(128)} %broadcast_multiply_fusion.2, ...), kind=kLoop, calls=%fused_computation.7.clone.1 | loop fusion | flops 8912896 | bytes 8782145 | tf_op jit(solution)/shard_map/while/body/eval_jaxpr/sub | solution.py:82
  60.6 5.1 %fusion.169 = (f32[16,256,128]{2,1,0:T(8,128)}, f32[16,256,128]{2,1,0:T(8,128)S(1)}) fusion(f32[16,256,128]{2,1,0:T(8,128)} %get-tuple-element.336, f32[256,128]{1,0:T(8,128)S(1)} %get-tuple-element.317, f32[16]{0:T(128)S(1)} %get-tuple-element.319, f32[256,128]{1,0:T(8,128)S(1)} %get-tuple-element.320, f32[16]{0:T(128)} %broadcast_multiply_fusion.2, ...), kind=kLoop, calls=%fused_computation.7.clone.1 | loop fusion | flops 8912896 | bytes 8782145 | tf_op jit(solution)/shard_map/while/body/eval_jaxpr/sub | solution.py:82
  68.6 5.1 %fusion.169 = (f32[16,256,128]{2,1,0:T(8,128)}, f32[16,256,128]{2,1,0:T(8,128)S(1)}) fusion(f32[16,256,128]{2,1,0:T(8,128)} %get-tuple-element.336, f32[256,128]{1,0:T(8,128)S(1)} %get-tuple-element.317, f32[16]{0:T(128)S(1)} %get-tuple-element.319, f32[256,128]{1,0:T(8,128)S(1)} %get-tuple-element.320, f32[16]{0:T(128)} %broadcast_multiply_fusion.2, ...), kind=kLoop, calls=%fused_computation.7.clone.1 | loop fusion | flops 8912896 | bytes 8782145 | tf_op jit(solution)/shard_map/while/body/eval_jaxpr/sub | solution.py:82
  76.5 5.1 %fusion.169 = (f32[16,256,128]{2,1,0:T(8,128)}, f32[16,256,128]{2,1,0:T(8,128)S(1)}) fusion(f32[16,256,128]{2,1,0:T(8,128)} %get-tuple-element.336, f32[256,128]{1,0:T(8,128)S(1)} %get-tuple-element.317, f32[16]{0:T(128)S(1)} %get-tuple-element.319, f32[256,128]{1,0:T(8,128)S(1)} %get-tuple-element.320, f32[16]{0:T(128)} %broadcast_multiply_fusion.2, ...), kind=kLoop, calls=%fused_computation.7.clone.1 | loop fusion | flops 8912896 | bytes 8782145 | tf_op jit(solution)/shard_map/while/body/eval_jaxpr/sub | solution.py:82
  84.5 5.1 %fusion.169 = (f32[16,256,128]{2,1,0:T(8,128)}, f32[16,256,128]{2,1,0:T(8,128)S(1)}) fusion(f32[16,256,128]{2,1,0:T(8,128)} %get-tuple-element.336, f32[256,128]{1,0:T(8,128)S(1)} %get-tuple-element.317, f32[16]{0:T(128)S(1)} %get-tuple-element.319, f32[256,128]{1,0:T(8,128)S(1)} %get-tuple-element.320, f32[16]{0:T(128)} %broadcast_multiply_fusion.2, ...), kind=kLoop, calls=%fused_computation.7.clone.1 | loop fusion | flops 8912896 | bytes 8782145 | tf_op jit(solution)/shard_map/while/body/eval_jaxpr/sub | solution.py:82
  92.5 5.1 %fusion.169 = (f32[16,256,128]{2,1,0:T(8,128)}, f32[16,256,128]{2,1,0:T(8,128)S(1)}) fusion(f32[16,256,128]{2,1,0:T(8,128)} %get-tuple-element.336, f32[256,128]{1,0:T(8,128)S(1)} %get-tuple-element.317, f32[16]{0:T(128)S(1)} %get-tuple-element.319, f32[256,128]{1,0:T(8,128)S(1)} %get-tuple-element.320, f32[16]{0:T(128)} %broadcast_multiply_fusion.2, ...), kind=kLoop, calls=%fused_computation.7.clone.1 | loop fusion | flops 8912896 | bytes 8782145 | tf_op jit(solution)/shard_map/while/body/eval_jaxpr/sub | solution.py:82
  100.4 5.1 %fusion.169 = (f32[16,256,128]{2,1,0:T(8,128)}, f32[16,256,128]{2,1,0:T(8,128)S(1)}) fusion(f32[16,256,128]{2,1,0:T(8,128)} %get-tuple-element.336, f32[256,128]{1,0:T(8,128)S(1)} %get-tuple-element.317, f32[16]{0:T(128)S(1)} %get-tuple-element.319, f32[256,128]{1,0:T(8,128)S(1)} %get-tuple-element.320, f32[16]{0:T(128)} %broadcast_multiply_fusion.2, ...), kind=kLoop, calls=%fused_computation.7.clone.1 | loop fusion | flops 8912896 | bytes 8782145 | tf_op jit(solution)/shard_map/while/body/eval_jaxpr/sub | solution.py:82
  108.4 5.1 %fusion.169 = (f32[16,256,128]{2,1,0:T(8,128)}, f32[16,256,128]{2,1,0:T(8,128)S(1)}) fusion(f32[16,256,128]{2,1,0:T(8,128)} %get-tuple-element.336, f32[256,128]{1,0:T(8,128)S(1)} %get-tuple-element.317, f32[16]{0:T(128)S(1)} %get-tuple-element.319, f32[256,128]{1,0:T(8,128)S(1)} %get-tuple-element.320, f32[16]{0:T(128)} %broadcast_multiply_fusion.2, ...), kind=kLoop, calls=%fused_computation.7.clone.1 | loop fusion | flops 8912896 | bytes 8782145 | tf_op jit(solution)/shard_map/while/body/eval_jaxpr/sub | solution.py:82
  116.3 5.1 %fusion.169 = (f32[16,256,128]{2,1,0:T(8,128)}, f32[16,256,128]{2,1,0:T(8,128)S(1)}) fusion(f32[16,256,128]{2,1,0:T(8,128)} %get-tuple-element.336, f32[256,128]{1,0:T(8,128)S(1)} %get-tuple-element.317, f32[16]{0:T(128)S(1)} %get-tuple-element.319, f32[256,128]{1,0:T(8,128)S(1)} %get-tuple-element.320, f32[16]{0:T(128)} %broadcast_multiply_fusion.2, ...), kind=kLoop, calls=%fused_computation.7.clone.1 | loop fusion | flops 8912896 | bytes 8782145 | tf_op jit(solution)/shard_map/while/body/eval_jaxpr/sub | solution.py:82
  124.3 5.1 %fusion.169 = (f32[16,256,128]{2,1,0:T(8,128)}, f32[16,256,128]{2,1,0:T(8,128)S(1)}) fusion(f32[16,256,128]{2,1,0:T(8,128)} %get-tuple-element.336, f32[256,128]{1,0:T(8,128)S(1)} %get-tuple-element.317, f32[16]{0:T(128)S(1)} %get-tuple-element.319, f32[256,128]{1,0:T(8,128)S(1)} %get-tuple-element.320, f32[16]{0:T(128)} %broadcast_multiply_fusion.2, ...), kind=kLoop, calls=%fused_computation.7.clone.1 | loop fusion | flops 8912896 | bytes 8782145 | tf_op jit(solution)/shard_map/while/body/eval_jaxpr/sub | solution.py:82
  132.2 5.1 %fusion.169 = (f32[16,256,128]{2,1,0:T(8,128)}, f32[16,256,128]{2,1,0:T(8,128)S(1)}) fusion(f32[16,256,128]{2,1,0:T(8,128)} %get-tuple-element.336, f32[256,128]{1,0:T(8,128)S(1)} %get-tuple-element.317, f32[16]{0:T(128)S(1)} %get-tuple-element.319, f32[256,128]{1,0:T(8,128)S(1)} %get-tuple-element.320, f32[16]{0:T(128)} %broadcast_multiply_fusion.2, ...), kind=kLoop, calls=%fused_computation.7.clone.1 | loop fusion | flops 8912896 | bytes 8782145 | tf_op jit(solution)/shard_map/while/body/eval_jaxpr/sub | solution.py:82
  140.2 5.1 %fusion.169 = (f32[16,256,128]{2,1,0:T(8,128)}, f32[16,256,128]{2,1,0:T(8,128)S(1)}) fusion(f32[16,256,128]{2,1,0:T(8,128)} %get-tuple-element.336, f32[256,128]{1,0:T(8,128)S(1)} %get-tuple-element.317, f32[16]{0:T(128)S(1)} %get-tuple-element.319, f32[256,128]{1,0:T(8,128)S(1)} %get-tuple-element.320, f32[16]{0:T(128)} %broadcast_multiply_fusion.2, ...), kind=kLoop, calls=%fused_computation.7.clone.1 | loop fusion | flops 8912896 | bytes 8782145 | tf_op jit(solution)/shard_map/while/body/eval_jaxpr/sub | solution.py:82
  148.1 5.1 %fusion.169 = (f32[16,256,128]{2,1,0:T(8,128)}, f32[16,256,128]{2,1,0:T(8,128)S(1)}) fusion(f32[16,256,128]{2,1,0:T(8,128)} %get-tuple-element.336, f32[256,128]{1,0:T(8,128)S(1)} %get-tuple-element.317, f32[16]{0:T(128)S(1)} %get-tuple-element.319, f32[256,128]{1,0:T(8,128)S(1)} %get-tuple-element.320, f32[16]{0:T(128)} %broadcast_multiply_fusion.2, ...), kind=kLoop, calls=%fused_computation.7.clone.1 | loop fusion | flops 8912896 | bytes 8782145 | tf_op jit(solution)/shard_map/while/body/eval_jaxpr/sub | solution.py:82
  154.2 2.8 copy.13
  159.4 3.6 fusion.66
  172.4 2.8 multiply_add_fusion.1
  188.8 19.4 %all_to_all.35 = f32[16,8,2048]{2,0,1:T(8,128)S(1)} all-to-all(f32[16,8,2048]{2,0,1:T(8,128)S(1)} %copy.16), channel_id=1, replica_groups=mesh['ctx'=8,'tp'=32] {'ctx'}, dimensions={1} | all-to-all | bytes 2097152 | tf_op jit(solution)/shard_map/all_to_all | solution.py:114
  209.3 142.7 %all-gather.2.cloned.1.call-done = bf16[2048,4096]{0,1:T(8,128)(2,1)} async-done(((bf16[2048,128]{0,1:T(8,128)(2,1)}), bf16[2048,4096]{0,1:T(8,128)(2,1)}) %all-gather.2.cloned.1.call-update) | async-done | bytes 16777232 | tf_op jit(solution)/shard_map/all_gather | solution.py:118
  352.1 9.0 %convolution_convert_fusion = bf16[2048,128]{1,0:T(8,128)(2,1)} fusion(bf16[2048,4096]{0,1:T(8,128)(2,1)} %all-gather.2.cloned.1.call-done, bf16[4096,128]{1,0:T(8,128)(2,1)S(1)} %copy-done), kind=kOutput, calls=%fused_computation.36 | convolution fusion | flops 2147745792 | bytes 18350080 | tf_op jit(solution)/shard_map/dot_general | solution.py:117
  (123 shorter events, 87.1 us)
Async XLA Ops:
  6.5 345.6 %copy-start = (bf16[4096,128]{1,0:T(8,128)(2,1)S(1)}, bf16[4096,128]{1,0:T(8,128)(2,1)}, u32[]{:S(2)}) copy-start(bf16[4096,128]{1,0:T(8,128)(2,1)} %param.13) | copy-start | bytes 3145732
  7.5 6.7 %collective-permute-start = (bf16[2,3,128]{0,2,1:T(8,128)(2,1)S(1)}, bf16[2,3,128]{0,2,1:T(8,128)(2,1)S(1)}, u32[]{:S(2)}, u32[]{:S(2)}) collective-permute-start(bf16[2,3,128]{0,2,1:T(8,128)(2,1)S(1)} %copy.11), channel_id=1, source_target_pairs={{0,32},{32,64},{64,96},{96,128},{128,160},{160,192},{192,224},{1,3... | collective-permute-start | bytes 4616 | tf_op jit(solution)/shard_map/ppermute | solution.py:15
  18.2 1.7 copy-start.2
  21.0 133.2 %all-to-all-start = ((f32[8,16,2048]{2,1,0:T(8,128)}), f32[8,16,2048]{2,1,0:T(8,128)}, u32[]{:S(2)}, u32[]{:S(2)}) async-start(f32[8,16,2048]{2,1,0:T(8,128)} %bitcast.113), calls=%async_computation | async-start | bytes 2097152 | tf_op jit(solution)/shard_map/all_to_all | solution.py:109
  26.7 325.3 %all-gather.2.cloned.1.call-start = ((), (), s32[]{:S(2)}) async-start(), calls=%async_computation.2 | async-start | bytes 17301504 | tf_op jit(solution)/shard_map/all_gather | solution.py:118
  159.4 3.6 copy-start.4
  169.9 2.5 copy-start.1
  188.1 20.0 %copy-start.3 = (f32[2048,3,128]{0,2,1:T(8,128)S(1)}, f32[2048,3,128]{0,2,1:T(8,128)}, u32[]{:S(2)}) copy-start(f32[2048,3,128]{0,2,1:T(8,128)} %copy-done.2) | copy-start | bytes 9437188
  188.1 20.0 %copy-start.5 = (f32[128]{0:T(128)S(1)}, f32[128]{0:T(128)}, u32[]{:S(2)}) copy-start(f32[128]{0:T(128)} %param.12) | copy-start | bytes 1540
Sparse Core Ops, SparseCore 0:
  209.5 142.5 all-gather.1
where the time goes:
time: 375 us; the launch traced here: 368 us
  waiting for transfers between devices  143 us (38%)
  other arithmetic  133 us (35%)
  matrix products  37.4 us (10%)
  blocking collectives  19.4 us (5%)
  between operations  13.8 us (4%)
  local copies, waits for them, and re-layouts  13.3 us (4%)
  starting transfers between devices  7.69 us (2%)
    all_gather x1, waiting for transfers between devices, shards(): lax.all_gather(gated, 'tp', axis=1, tiled=True)  143 us
    sub x16, other arithmetic, add_mode(): return (spec_re + factor * denom_re, spec_im - factor * denom_im)  80.5 us
    all_to_all x1, blocking collectives, shards(): lax.all_to_all(filtered, 'ctx', split_axis=1, concat_axis=0, tiled=True)  19.4 us
    mul x16, other arithmetic, add_mode(): denom_im = decay * full_sin  13.9 us
    exp x16, other arithmetic, add_mode(): numer = 1.0 - jnp.exp(-rate_row * seq_len) * parity  11.7 us
    mul x16, other arithmetic, add_mode(): denom_re = -jnp.expm1(-rate_row) + 2.0 * decay * half_sin * half_sin  9.58 us
    exp x16, other arithmetic, add_mode(): decay = jnp.exp(-rate_row)  9.44 us
    dot_general x1, matrix products, shards(): jnp.dot(lax.all_gather(gated, 'tp', axis=1, tiled=True), out_weight, pref...  8.98 us
  transfers between devices with their start and end apart: 3, of which 1 were waited for; matrix products, arithmetic and copies ran while one was open for 36% of the time, Pallas kernels for 0%

commit v1 on v0

v1 whole, which is shorter than its diff:
```python
import jax
import jax.numpy as jnp
from jax import lax
from jax.experimental import pallas as pl
from jax.experimental.pallas import tpu as pltpu
from jax.sharding import Mesh, PartitionSpec as P

CTX = ("x", "core")
SUB = 8
PAD = 8
UNROLL = 8
PIECES = 2
ROW_TILE = 256


def shifted(value, axis, steps):
    count = lax.axis_size(axis)
    return lax.ppermute(value, axis, [(at, (at + steps) % count) for at in range(count)])


def from_behind(value, axis, steps):
    count = lax.axis_size(axis)
    return lax.ppermute(value, axis, [(at, at + steps) for at in range(count - steps)])


def wide(row):
    return jnp.broadcast_to(row, (SUB, row.shape[-1]))


def added(parts):
    while len(parts) > 1:
        pairs = [a + b for a, b in zip(parts[0::2], parts[1::2])]
        parts = pairs + parts[2 * len(pairs) :]
    return parts[0]


def unpack_stream(stream_ref, which, padded_ref):
    rows = stream_ref.shape[1]
    padded_ref[0:PAD, :] = jnp.zeros((PAD, padded_ref.shape[1]), jnp.float32)
    tile = 256

    def body(at, _):
        start = pl.multiple_of(at * tile, tile)
        block = stream_ref[which, pl.ds(start, tile), :].astype(jnp.float32)
        padded_ref[pl.ds(pl.multiple_of(PAD + at * tile, 8), tile), :] = block
        return 0

    lax.fori_loop(0, rows // tile, body, 0)


def state_kernel(stream_ref, taps_ref, rate_ref, signal_ref, start_ref, packed_ref, key_ref, val_ref):
    rows = stream_ref.shape[1]
    steps = rows // SUB
    order, chans = rate_ref.shape
    unpack_stream(stream_ref, 1, key_ref)
    unpack_stream(stream_ref, 2, val_ref)
    decay = [wide(jnp.exp(-rate_ref[r : r + 1, :])) for r in range(order)]
    key_taps = [wide(taps_ref[j, 1:2, :]) for j in range(3)]
    val_taps = [wide(taps_ref[j, 2:3, :]) for j in range(3)]
    block = lax.broadcasted_iota(jnp.int32, (SUB, chans), 0)

    def row(ref, step):
        return ref[pl.ds(PAD + step, SUB, stride=steps), :]

    def advance(step, carried, masked):
        k2, k1, v2, v1, *states = carried
        k0 = row(key_ref, step)
        v0 = row(val_ref, step)
        key = key_taps[0] * k2 + key_taps[1] * k1 + key_taps[2] * k0
        val = val_taps[0] * v2 + val_taps[1] * v1 + val_taps[2] * v0
        signal = key * val
        if masked:
            signal = jnp.where(block == 0, 0.0, signal)
        signal_ref[step] = signal
        states = [a * h + signal for a, h in zip(decay, states)]
        return [k1, k0, v1, v0, *states]

    carried = [row(key_ref, -2), row(key_ref, -1), row(val_ref, -2), row(val_ref, -1)]
    carried += [jnp.zeros((SUB, chans), jnp.float32)] * order
    for step in range(UNROLL):
        carried = advance(step, carried, step < 2)

    def body(at, carried):
        carried = list(carried)
        for step in range(UNROLL):
            carried = advance(at * UNROLL + step, carried, False)
        return tuple(carried)

    states = lax.fori_loop(1, steps // UNROLL, body, tuple(carried))[4:]
    for r in range(order):
        rate = wide(rate_ref[r : r + 1, :])
        total = states[r]
        for back in (1, 2, 4):
            gain = jnp.where(block >= back, jnp.exp(-rate * (steps * back)), 0.0)
            total = total + gain * pltpu.roll(total, back, 0)
        packed_ref[r : r + 1, :] = total[SUB - 1 : SUB, :]
        start_ref[r] = jnp.where(block == 0, 0.0, pltpu.roll(total, 1, 0))
    for s in range(3):
        head = stream_ref[s, 0:16, :].astype(jnp.float32)
        tail = stream_ref[s, rows - 16 : rows, :].astype(jnp.float32)
        packed_ref[order + 2 * s : order + 2 * s + 2, :] = head[0:2, :]
        packed_ref[order + 6 + 2 * s : order + 8 + 2 * s, :] = tail[14:16, :]
    packed_ref[order + 12 :, :] = jnp.zeros((packed_ref.shape[0] - order - 12, chans), jnp.float32)


def local_kernel(
    stream_ref, taps_ref, residue_ref, rate_ref, skip_ref, signal_ref, start_ref, query_ref, conv_ref, raw_ref
):
    rows = stream_ref.shape[1]
    steps = rows // SUB
    order, chans = rate_ref.shape
    unpack_stream(stream_ref, 0, raw_ref)
    decay = [wide(jnp.exp(-rate_ref[r : r + 1, :])) for r in range(order)]
    weight = [
        wide(residue_ref[r : r + 1, :] * jnp.sqrt(2.0 * rate_ref[r : r + 1, :])) for r in range(order)
    ]
    taps = [wide(taps_ref[j, 0:1, :]) for j in range(3)]
    skip = wide(skip_ref[0:1, :])

    def row(step):
        return raw_ref[pl.ds(PAD + step, SUB, stride=steps), :]

    def body(at, carried):
        q2, q1, *states = carried
        for inner in range(UNROLL):
            step = at * UNROLL + inner
            q0 = row(step)
            query_ref[step] = taps[0] * q2 + taps[1] * q1 + taps[2] * q0
            q2, q1 = q1, q0
            signal = signal_ref[step]
            states = [a * h + signal for a, h in zip(decay, states)]
            parts = [w * h for w, h in zip(weight, states)]
            parts.append(skip * signal)
            conv_ref[step] = added(parts)
        return (q2, q1, *states)

    first = (row(-2), row(-1), *[start_ref[r] for r in range(order)])
    lax.fori_loop(0, steps // UNROLL, body, first)


def gate_kernel(
    taps_ref, residue_ref, rate_ref, skip_ref, query_ref, conv_ref, own_ref, *rest
):
    *past_refs, out_ref, nat_ref = rest
    rows, chans = out_ref.shape
    steps = rows // SUB
    order = rate_ref.shape[0]
    rate = rate_ref[...]
    decay = jnp.exp(-rate)
    weight = residue_ref[...] * jnp.sqrt(2.0 * rate)
    tap = [[taps_ref[j, s : s + 1, :] for s in range(3)] for j in range(3)]

    def head_feat(now_ref, past_ref, s):
        at = order + 2 * s
        x0, x1 = now_ref[at : at + 1, :], now_ref[at + 1 : at + 2, :]
        at = order + 6 + 2 * s
        if past_ref is None:
            m2 = m1 = jnp.zeros_like(x0)
        else:
            m2, m1 = past_ref[at : at + 1, :], past_ref[at + 1 : at + 2, :]
        first = tap[0][s] * m2 + tap[1][s] * m1 + tap[2][s] * x0
        second = tap[0][s] * m1 + tap[1][s] * x0 + tap[2][s] * x1
        return first, second

    refs = [own_ref, *past_refs, None]

    def head_signal(at):
        k0, k1 = head_feat(refs[at], refs[at + 1], 1)
        v0, v1 = head_feat(refs[at], refs[at + 1], 2)
        return k0 * v0, k1 * v1

    whole = jnp.exp(-rate * rows)
    lead0 = jnp.exp(-rate * (rows - 1))
    lead1 = jnp.exp(-rate * (rows - 2))
    state = jnp.zeros((order, chans), jnp.float32)
    for at in range(len(past_refs), 0, -1):
        s0, s1 = head_signal(at)
        state = whole * state + refs[at][0:order, :] + lead0 * s0 + lead1 * s1
    s0, s1 = head_signal(0)
    at0 = decay * state + s0
    at1 = decay * at0 + s1
    skip = skip_ref[0:1, :]
    conv0 = jnp.sum(weight * at0, axis=0, keepdims=True) + skip * s0
    conv1 = jnp.sum(weight * at1, axis=0, keepdims=True) + skip * s1
    q0, q1 = head_feat(refs[0], refs[1], 0)

    block = lax.broadcasted_iota(jnp.int32, (SUB, chans), 0).astype(jnp.float32)
    begin = weight * at1
    decays = [wide(decay[r : r + 1, :]) for r in range(order)]
    terms = [
        wide(begin[r : r + 1, :]) * jnp.exp(-wide(rate[r : r + 1, :]) * (block * steps - 1.0))
        for r in range(order)
    ]

    def body(at, terms):
        for inner in range(UNROLL):
            step = at * UNROLL + inner
            parts = [conv_ref[step], *terms]
            nat_ref[pl.ds(step, SUB, stride=steps), :] = query_ref[step] * added(parts)
            terms = [p * a for p, a in zip(terms, decays)]
        return tuple(terms)

    lax.fori_loop(0, steps // UNROLL, body, tuple(terms))
    nat_ref[0:1, :] = q0 * conv0
    nat_ref[1:2, :] = q1 * conv1
    tile = 256

    def finish(at, _):
        span = pl.ds(pl.multiple_of(at * tile, tile), tile)
        out_ref[span, :] = nat_ref[span, :].astype(jnp.bfloat16)
        return 0

    lax.fori_loop(0, rows // tile, finish, 0)


def project_kernel(place_ref, *refs):
    here, f1, f2, f3, b1, b2, b3, f4, b4, w0, w1, w2, w3, own, p1, p2, p3, weight = refs
    rows = here.shape[0]
    count = w0.shape[0]
    depth = w0.shape[1]
    place = place_ref[0]
    for j in range(count):
        source = lax.rem(place - j + count, count)
        for s, piece in enumerate((w0, w1, w2, w3)):
            weight[j * depth : (j + 1) * depth, s * depth : (s + 1) * depth] = piece[source]
    for start in range(0, rows, ROW_TILE):
        span = slice(start, start + ROW_TILE)
        half = rows // 2
        far = f4[start : start + ROW_TILE, :] if start < half else b4[start - half : start - half + ROW_TILE, :]
        left = jnp.concatenate(
            [here[span, :], f1[span, :], f2[span, :], f3[span, :], far, b3[span, :], b2[span, :], b1[span, :]],
            axis=1,
        )
        total = jnp.dot(left, weight[...], preferred_element_type=jnp.float32)
        own[span, :] = total[:, 0:depth]
        for s, part in enumerate((p1, p2, p3)):
            part[span, :] = total[:, (s + 1) * depth : (s + 2) * depth].astype(jnp.bfloat16)


def call(kernel, shapes, scratch, flops, args, name):
    size = sum(a.size * a.dtype.itemsize for a in args) + sum(
        s.size * jnp.dtype(s.dtype).itemsize for s in jax.tree.leaves(shapes)
    )
    return pl.pallas_call(
        kernel,
        out_shape=shapes,
        scratch_shapes=scratch,
        compiler_params=pltpu.CompilerParams(vmem_limit_bytes=40 * 1024 * 1024),
        cost_estimate=pl.CostEstimate(flops=flops, bytes_accessed=size, transcendentals=0),
        name=name,
    )(*args)


def shards(streams, short_filter, residue, decay_rate, skip_gain, out_weight):
    f32, bf16 = jnp.float32, jnp.bfloat16
    rows, _, chans = streams.shape
    order = residue.shape[0]
    steps = rows // SUB
    z_size, y_size = lax.axis_size("z"), lax.axis_size("y")
    z_at, y_at = lax.axis_index("z"), lax.axis_index("y")
    shape = jax.ShapeDtypeStruct
    skip = skip_gain[None, :]

    by_owner = out_weight.reshape(z_size, y_size, chans, chans)
    weights = []
    for s in range(y_size):
        rows_of = lax.dynamic_index_in_dim(by_owner, (y_at + s) % y_size, 1, keepdims=False)
        weights.append(rows_of if s == 0 else shifted(rows_of, "y", s))

    planes = jnp.transpose(streams, (1, 0, 2))
    plane = pltpu.VMEM((PAD + rows, chans), f32)
    by_step = shape((steps, SUB, chans), f32)
    signal, start, packed = call(
        state_kernel,
        (by_step, shape((order, SUB, chans), f32), shape((order + 16, chans), f32)),
        [plane, plane],
        rows * chans * 44,
        (planes, short_filter, decay_rate),
        "states",
    )
    past = [from_behind(packed, CTX, s) for s in range(1, 8)]
    query, conv = call(
        local_kernel,
        (by_step, by_step),
        [plane],
        rows * chans * 70,
        (planes, short_filter, residue, decay_rate, skip, signal, start),
        "local_conv",
    )
    gated = call(
        gate_kernel,
        shape((rows, chans), bf16),
        [pltpu.VMEM((rows, chans), f32)],
        rows * chans * 34,
        (short_filter, residue, decay_rate, skip, query, conv, packed, *past),
        "gate",
    )

    place = z_at.astype(jnp.int32).reshape(1)
    count = rows // PIECES
    results = []
    for piece in range(PIECES):
        here = gated[piece * count : (piece + 1) * count]
        ahead, behind = [here], [here]
        for _ in range(3):
            ahead.append(shifted(ahead[-1], "z", 1))
            behind.append(shifted(behind[-1], "z", -1))
        f4 = shifted(ahead[3][: count // 2], "z", 1)
        b4 = shifted(behind[3][count // 2 :], "z", -1)
        part = shape((count, chans), bf16)
        smem = pl.BlockSpec(memory_space=pltpu.SMEM)
        vmem = pl.BlockSpec(memory_space=pltpu.VMEM)
        own, *parts = pl.pallas_call(
            project_kernel,
            out_shape=(shape((count, chans), f32), part, part, part),
            in_specs=[smem] + [vmem] * 13,
            out_specs=(vmem,) * 4,
            scratch_shapes=[pltpu.VMEM((z_size * chans, y_size * chans), bf16)],
            compiler_params=pltpu.CompilerParams(vmem_limit_bytes=40 * 1024 * 1024),
            cost_estimate=pl.CostEstimate(
                flops=2 * count * z_size * y_size * chans * chans,
                bytes_accessed=16 * count * chans * 2,
                transcendentals=0,
            ),
            name="project",
        )(place, *ahead, *behind[1:], f4, b4, *weights)
        total = own
        for s in range(1, y_size):
            total = total + shifted(parts[s - 1], "y", -s).astype(f32)
        results.append(total.astype(bf16))
    return jnp.concatenate(results, axis=0)


def solution(mesh):
    ctx_size, tp_size = mesh.devices.shape
    fine = Mesh(mesh.devices.reshape(ctx_size // 2, 2, tp_size // 4, 4), ("x", "core", "z", "y"))
    tp = ("z", "y")
    in_specs = (
        P(CTX, None, tp),
        P(None, None, tp),
        P(None, tp),
        P(None, tp),
        P(tp),
        P(None, tp),
    )
    return jax.shard_map(shards, mesh=fine, in_specs=in_specs, out_specs=P(CTX, tp), check_vma=False)
```

time: 375 us -> 112 us (0.30); the launches traced: 368 us -> 111 us
  other arithmetic: 133 us -> 1.09 us
  waiting for transfers between devices: 143 us -> 33.5 us
  starting transfers between devices: 7.69 us -> 53.2 us
  matrix products: 37.4 us -> 0 us
  blocking collectives: 19.4 us -> 0 us
  between operations: 13.8 us -> 0.28 us
  Pallas kernels: 0 us -> 12.4 us
    all_gather x1 -> x0, waiting for transfers between devices: 143 us -> none  [shards(): lax.all_gather(gated, 'tp', axis=1, tiled=True)]
    sub x16 -> x0, other arithmetic: 80.5 us -> none  [add_mode(): return (spec_re + factor * denom_re, spec_im - factor * denom_im)]
    ppermute x1 -> x32, starting transfers between devices: 1.92 us -> 53.2 us  [the longest x25 40 us: shifted(): lax.ppermute(value, axis, [(at, (at + steps) % count) for at in range(cou...]
    dot_general x13 -> x0, matrix products: 37.4 us -> none  [the longest x1 8.98 us: shards(): jnp.dot(lax.all_gather(gated, 'tp', axis=1, tiled=True), out_weight, pref...]
    ppermute x1 -> x32, waiting for transfers between devices: 0.01 us -> 33.5 us  [the longest x25 33.4 us: shifted(): lax.ppermute(value, axis, [(at, (at + steps) % count) for at in range(cou...]
    mul x50 -> x0, other arithmetic: 25.8 us -> none  [the longest x16 13.9 us: add_mode(): denom_im = decay * full_sin]
    exp x32 -> x0, other arithmetic: 21.1 us -> none  [the longest x16 11.7 us: add_mode(): numer = 1.0 - jnp.exp(-rate_row * seq_len) * parity]
    all_to_all x1 -> x0, blocking collectives: 19.4 us -> none  [shards(): lax.all_to_all(filtered, 'ctx', split_axis=1, concat_axis=0, tiled=True)]
  transfers between devices with their start and end apart: 3 -> 32, of which waited for: 1 -> 13; matrix products, arithmetic and copies ran while one was open for 36% -> 3% of each run, Pallas kernels for 0% -> 7%
where the time goes in v1:
time: 112 us; the launch traced here: 111 us
  starting transfers between devices  53.2 us (48%)
  waiting for transfers between devices  33.5 us (30%)
  Pallas kernels  12.4 us (11%)
  local copies, waits for them, and re-layouts  10.5 us (9%)
    ppermute x25, starting transfers between devices, shifted(): lax.ppermute(value, axis, [(at, (at + steps) % count) for at in range(cou...  40 us
    ppermute x25, waiting for transfers between devices, shifted(): lax.ppermute(value, axis, [(at, (at + steps) % count) for at in range(cou...  33.4 us
    ppermute x7, starting transfers between devices, from_behind(): lax.ppermute(value, axis, [(at, at + steps) for at in range(count - steps)])  13.2 us
    pallas_call x3, Pallas kernels, call(): pl.pallas_call(kernel, out_shape=shapes, scratch_shapes=scratch, compiler...  7.64 us
    unnamed x26, local copies, waits for them, and re-layouts  7.07 us
    pallas_call x2, Pallas kernels, shards(): pl.pallas_call(project_kernel, out_shape=(shape((count, chans), f32), par...  4.77 us
  transfers between devices with their start and end apart: 32, of which 13 were waited for; matrix products, arithmetic and copies ran while one was open for 3% of the time, Pallas kernels for 7%

profile of v1, /device:TPU:2, one launch (start us, length us, event | category | flops | bytes accessed | tf_op | source)
XLA Modules:
  0.0 110.9 jit_solution(8408398128141659396)
XLA Ops:
  2.8 2.7 %states.1 = (f32[256,8,128]{2,1,0:T(8,128)S(1)}, f32[16,8,128]{2,1,0:T(8,128)S(1)}, f32[32,128]{1,0:T(8,128)S(1)}) custom-call(bf16[3,2048,128]{2,1,0:T(8,128)(2,1)S(1)} %bitcast.20, f32[3,3,128]{2,1,0:T(4,128)S(1)} %copy-done.2, f32[16,128]{1,0:T(8,128)S(1)} %copy-done.1), custom_call_target="tpu_custom_call" | custom-call | flops 11534336 | bytes 2716160 | tf_op jit(solution)/shard_map/states/pallas_call | solution.py:244
  6.8 4.7 %collective-permute-start.4 = (f32[32,128]{1,0:T(8,128)S(1)}, f32[32,128]{1,0:T(8,128)S(1)}, u32[]{:S(2)}, u32[]{:S(2)}) collective-permute-start(f32[32,128]{1,0:T(8,128)S(1)} %get-tuple-element.22.own_ref), channel_id=1, source_target_pairs={{0,160},{32,192},{64,224},{1,161},{33,193},{65,225},{2,162},{34,19... | collective-permute-start | bytes 49160 | tf_op jit(solution)/shard_map/ppermute | solution.py:23
  14.2 2.5 %collective-permute-start.1 = (f32[32,128]{1,0:T(8,128)S(1)}, f32[32,128]{1,0:T(8,128)S(1)}, u32[]{:S(2)}, u32[]{:S(2)}) collective-permute-start(f32[32,128]{1,0:T(8,128)S(1)} %get-tuple-element.22.own_ref), channel_id=1, source_target_pairs={{0,64},{32,96},{64,128},{96,160},{128,192},{160,224},{1,65},{33,97... | collective-permute-start | bytes 49160 | tf_op jit(solution)/shard_map/ppermute | solution.py:23
  16.7 2.1 %collective-permute-start = (f32[32,128]{1,0:T(8,128)S(1)}, f32[32,128]{1,0:T(8,128)S(1)}, u32[]{:S(2)}, u32[]{:S(2)}) collective-permute-start(f32[32,128]{1,0:T(8,128)S(1)} %get-tuple-element.22.own_ref), channel_id=1, source_target_pairs={{0,32},{32,64},{64,96},{96,128},{128,160},{160,192},{192,224},{1,3... | collective-permute-start | bytes 49160 | tf_op jit(solution)/shard_map/ppermute | solution.py:23
  18.8 3.4 %local_conv.1 = (f32[256,8,128]{2,1,0:T(8,128)S(1)}, f32[256,8,128]{2,1,0:T(8,128)S(1)}) custom-call(bf16[3,2048,128]{2,1,0:T(8,128)(2,1)S(1)} %bitcast.21, f32[3,3,128]{2,1,0:T(4,128)S(1)} %copy-done.2, f32[16,128]{1,0:T(8,128)S(1)} %copy-done.3, f32[16,128]{1,0:T(8,128)S(1)} %copy-done.1, f32[1,128]{1,0:T(1,128)S(1)} %bitcast.22, ...), custom_call_target="tpu_custom_call" | custom-call | flops 18350080 | bytes 4805632 | tf_op jit(solution)/shard_map/local_conv/pallas_call | solution.py:244
  23.9 5.9 %collective-permute-start.10 = (bf16[1024,128]{1,0:T(8,128)(2,1)S(1)}, bf16[1024,128]{1,0:T(8,128)(2,1)S(1)}, u32[]{:S(2)}, u32[]{:S(2)}) collective-permute-start(bf16[1024,128]{1,0:T(8,128)(2,1)S(1)} %get-tuple-element.35.refs_0_), channel_id=1, source_target_pairs={{0,28},{4,0},{8,4},{12,8},{16,12},{20,16},{24,20},{28,24},{1,29},{... | collective-permute-start | bytes 786440 | tf_op jit(solution)/shard_map/ppermute | solution.py:18
  29.8 3.2 %collective-permute-start.24 = (bf16[1024,128]{1,0:T(8,128)(2,1)S(1)}, bf16[1024,128]{1,0:T(8,128)(2,1)S(1)}, u32[]{:S(2)}, u32[]{:S(2)}) collective-permute-start(bf16[1024,128]{1,0:T(8,128)(2,1)S(1)} %get-tuple-element.36.refs_0_), channel_id=1, source_target_pairs={{0,28},{4,0},{8,4},{12,8},{16,12},{20,16},{24,20},{28,24},{1,29},{... | collective-permute-start | bytes 786440 | tf_op jit(solution)/shard_map/ppermute | solution.py:18
  33.0 3.5 %collective-permute-done.10.refs_4_ = bf16[1024,128]{1,0:T(8,128)(2,1)S(1)} collective-permute-done((bf16[1024,128]{1,0:T(8,128)(2,1)S(1)}, bf16[1024,128]{1,0:T(8,128)(2,1)S(1)}, u32[]{:S(2)}, u32[]{:S(2)}) %collective-permute-start.10) | collective-permute-done | bytes 262176 | tf_op jit(solution)/shard_map/ppermute | solution.py:18
  36.5 3.7 %collective-permute-start.11 = (bf16[1024,128]{1,0:T(8,128)(2,1)S(1)}, bf16[1024,128]{1,0:T(8,128)(2,1)S(1)}, u32[]{:S(2)}, u32[]{:S(2)}) collective-permute-start(bf16[1024,128]{1,0:T(8,128)(2,1)S(1)} %collective-permute-done.10.refs_4_), channel_id=1, source_target_pairs={{0,28},{4,0},{8,4},{12,8},{16,12},{20,16},{24,20},{28,24},{1,29},{... | collective-permute-start | bytes 786440 | tf_op jit(solution)/shard_map/ppermute | solution.py:18
  42.1 3.7 %collective-permute-start.25 = (bf16[1024,128]{1,0:T(8,128)(2,1)S(1)}, bf16[1024,128]{1,0:T(8,128)(2,1)S(1)}, u32[]{:S(2)}, u32[]{:S(2)}) collective-permute-start(bf16[1024,128]{1,0:T(8,128)(2,1)S(1)} %collective-permute-done.24.refs_4_), channel_id=1, source_target_pairs={{0,28},{4,0},{8,4},{12,8},{16,12},{20,16},{24,20},{28,24},{1,29},{... | collective-permute-start | bytes 786440 | tf_op jit(solution)/shard_map/ppermute | solution.py:18
  47.7 3.7 %collective-permute-start.12 = (bf16[1024,128]{1,0:T(8,128)(2,1)S(1)}, bf16[1024,128]{1,0:T(8,128)(2,1)S(1)}, u32[]{:S(2)}, u32[]{:S(2)}) collective-permute-start(bf16[1024,128]{1,0:T(8,128)(2,1)S(1)} %collective-permute-done.11.refs_5_), channel_id=1, source_target_pairs={{0,28},{4,0},{8,4},{12,8},{16,12},{20,16},{24,20},{28,24},{1,29},{... | collective-permute-start | bytes 786440 | tf_op jit(solution)/shard_map/ppermute | solution.py:18
  53.5 3.1 %collective-permute-start.17 = (bf16[8,128,128]{2,1,0:T(8,128)(2,1)S(1)}, bf16[8,128,128]{2,1,0:T(8,128)(2,1)S(1)}, u32[]{:S(2)}, u32[]{:S(2)}) collective-permute-start(bf16[8,128,128]{2,1,0:T(8,128)(2,1)S(1)} %get-tuple-element.31), channel_id=1, source_target_pairs={{0,3},{1,0},{2,1},{3,2},{4,7},{5,4},{6,5},{7,6},{8,11},{9,8},{10,9... | collective-permute-start | bytes 786440 | tf_op jit(solution)/shard_map/ppermute | solution.py:18
  60.3 3.4 %collective-permute-done.22.refs_2_ = bf16[1024,128]{1,0:T(8,128)(2,1)} collective-permute-done((bf16[1024,128]{1,0:T(8,128)(2,1)S(1)}, bf16[1024,128]{1,0:T(8,128)(2,1)}, u32[]{:S(2)}, u32[]{:S(2)}) %collective-permute-start.22) | collective-permute-done | bytes 262176 | tf_op jit(solution)/shard_map/ppermute | solution.py:18
  64.0 2.4 %collective-permute-done.9.refs_3_ = bf16[1024,128]{1,0:T(8,128)(2,1)S(1)} collective-permute-done((bf16[1024,128]{1,0:T(8,128)(2,1)S(1)}, bf16[1024,128]{1,0:T(8,128)(2,1)S(1)}, u32[]{:S(2)}, u32[]{:S(2)}) %collective-permute-start.9) | collective-permute-done | bytes 262176 | tf_op jit(solution)/shard_map/ppermute | solution.py:18
  67.8 3.2 %collective-permute-start.14 = (bf16[512,128]{1,0:T(8,128)(2,1)}, bf16[512,128]{1,0:T(8,128)(2,1)S(1)}, u32[]{:S(2)}, u32[]{:S(2)}) collective-permute-start(bf16[512,128]{1,0:T(8,128)(2,1)} %slice.26), channel_id=1, source_target_pairs={{0,28},{4,0},{8,4},{12,8},{16,12},{20,16},{24,20},{28,24},{1,29},{... | collective-permute-start | bytes 393224 | tf_op jit(solution)/shard_map/ppermute | solution.py:18
  71.7 2.1 %collective-permute-done.14.refs_8_ = bf16[512,128]{1,0:T(8,128)(2,1)S(1)} collective-permute-done((bf16[512,128]{1,0:T(8,128)(2,1)}, bf16[512,128]{1,0:T(8,128)(2,1)S(1)}, u32[]{:S(2)}, u32[]{:S(2)}) %collective-permute-start.14) | collective-permute-done | bytes 131104 | tf_op jit(solution)/shard_map/ppermute | solution.py:18
  73.8 4.4 %collective-permute-done.13.refs_7_ = bf16[512,128]{1,0:T(8,128)(2,1)} collective-permute-done((bf16[512,128]{1,0:T(8,128)(2,1)}, bf16[512,128]{1,0:T(8,128)(2,1)}, u32[]{:S(2)}, u32[]{:S(2)}) %collective-permute-start.13) | collective-permute-done | bytes 131104 | tf_op jit(solution)/shard_map/ppermute | solution.py:18
  81.1 2.4 %project.2 = (f32[1024,128]{1,0:T(8,128)S(1)}, bf16[1024,128]{1,0:T(8,128)(2,1)S(1)}, bf16[1024,128]{1,0:T(8,128)(2,1)S(1)}, bf16[1024,128]{1,0:T(8,128)(2,1)S(1)}) custom-call(s32[1]{0:T(128)} %bitcast.place_ref, bf16[1024,128]{1,0:T(8,128)(2,1)S(1)} %get-tuple-element.35.refs_0_, bf16[1024,128]{1,0:T(8,128)(2,1)S(1)} %collective-permute-done.7.refs_1_, ...), custom_call_target="tpu_custom_call" | custom-call | flops 1073741824 | bytes 4194304 | tf_op jit(solution)/shard_map/project/pallas_call | solution.py:313
  83.5 3.1 %collective-permute-start.18 = (bf16[1024,128]{1,0:T(8,128)(2,1)S(1)}, bf16[1024,128]{1,0:T(8,128)(2,1)S(1)}, u32[]{:S(2)}, u32[]{:S(2)}) collective-permute-start(bf16[1024,128]{1,0:T(8,128)(2,1)S(1)} %get-tuple-element.24), channel_id=1, source_target_pairs={{0,3},{1,0},{2,1},{3,2},{4,7},{5,4},{6,5},{7,6},{8,11},{9,8},{10,9... | collective-permute-start | bytes 786440 | tf_op jit(solution)/shard_map/ppermute | solution.py:18
  90.4 2.8 %collective-permute-done.28.refs_8_ = bf16[512,128]{1,0:T(8,128)(2,1)S(1)} collective-permute-done((bf16[512,128]{1,0:T(8,128)(2,1)S(1)}, bf16[512,128]{1,0:T(8,128)(2,1)S(1)}, u32[]{:S(2)}, u32[]{:S(2)}) %collective-permute-start.28) | collective-permute-done | bytes 131104 | tf_op jit(solution)/shard_map/ppermute | solution.py:18
  94.6 2.4 %project.3 = (f32[1024,128]{1,0:T(8,128)S(1)}, bf16[1024,128]{1,0:T(8,128)(2,1)S(1)}, bf16[1024,128]{1,0:T(8,128)(2,1)S(1)}, bf16[1024,128]{1,0:T(8,128)(2,1)S(1)}) custom-call(s32[1]{0:T(128)} %bitcast.place_ref, bf16[1024,128]{1,0:T(8,128)(2,1)S(1)} %get-tuple-element.36.refs_0_, bf16[1024,128]{1,0:T(8,128)(2,1)S(1)} %collective-permute-done.21.refs_1_, ...), custom_call_target="tpu_custom_call" | custom-call | flops 1073741824 | bytes 4194304 | tf_op jit(solution)/shard_map/project/pallas_call | solution.py:313
  96.9 2.3 %collective-permute-start.29 = (bf16[1024,128]{1,0:T(8,128)(2,1)S(1)}, bf16[1024,128]{1,0:T(8,128)(2,1)S(1)}, u32[]{:S(2)}, u32[]{:S(2)}) collective-permute-start(bf16[1024,128]{1,0:T(8,128)(2,1)S(1)} %get-tuple-element.28), channel_id=1, source_target_pairs={{0,3},{1,0},{2,1},{3,2},{4,7},{5,4},{6,5},{7,6},{8,11},{9,8},{10,9... | collective-permute-start | bytes 786440 | tf_op jit(solution)/shard_map/ppermute | solution.py:18
  101.1 5.0 %collective-permute-done.29 = bf16[1024,128]{1,0:T(8,128)(2,1)S(1)} collective-permute-done((bf16[1024,128]{1,0:T(8,128)(2,1)S(1)}, bf16[1024,128]{1,0:T(8,128)(2,1)S(1)}, u32[]{:S(2)}, u32[]{:S(2)}) %collective-permute-start.29) | collective-permute-done | bytes 262176 | tf_op jit(solution)/shard_map/ppermute | solution.py:18
  107.3 2.7 %collective-permute-done.31 = bf16[1024,128]{1,0:T(8,128)(2,1)S(1)} collective-permute-done((bf16[1024,128]{1,0:T(8,128)(2,1)S(1)}, bf16[1024,128]{1,0:T(8,128)(2,1)S(1)}, u32[]{:S(2)}, u32[]{:S(2)}) %collective-permute-start.31) | collective-permute-done | bytes 262176 | tf_op jit(solution)/shard_map/ppermute | solution.py:18
  (80 shorter events, 32.1 us)
Async XLA Ops:
  6.2 10.5 %collective-permute-start.5 = (f32[32,128]{1,0:T(8,128)S(1)}, f32[32,128]{1,0:T(8,128)S(1)}, u32[]{:S(2)}, u32[]{:S(2)}) collective-permute-start(f32[32,128]{1,0:T(8,128)S(1)} %get-tuple-element.22.own_ref), channel_id=1, source_target_pairs={{0,192},{32,224},{1,193},{33,225},{2,194},{34,226},{3,195},{35,227... | collective-permute-start | bytes 49160 | tf_op jit(solution)/shard_map/ppermute | solution.py:23
  6.8 15.4 %collective-permute-start.4 = (f32[32,128]{1,0:T(8,128)S(1)}, f32[32,128]{1,0:T(8,128)S(1)}, u32[]{:S(2)}, u32[]{:S(2)}) collective-permute-start(f32[32,128]{1,0:T(8,128)S(1)} %get-tuple-element.22.own_ref), channel_id=1, source_target_pairs={{0,160},{32,192},{64,224},{1,161},{33,193},{65,225},{2,162},{34,19... | collective-permute-start | bytes 49160 | tf_op jit(solution)/shard_map/ppermute | solution.py:23
  11.6 10.7 %collective-permute-start.3 = (f32[32,128]{1,0:T(8,128)S(1)}, f32[32,128]{1,0:T(8,128)S(1)}, u32[]{:S(2)}, u32[]{:S(2)}) collective-permute-start(f32[32,128]{1,0:T(8,128)S(1)} %get-tuple-element.22.own_ref), channel_id=1, source_target_pairs={{0,128},{32,160},{64,192},{96,224},{1,129},{33,161},{65,193},{97,2... | collective-permute-start | bytes 49160 | tf_op jit(solution)/shard_map/ppermute | solution.py:23
  12.9 9.4 %collective-permute-start.2 = (f32[32,128]{1,0:T(8,128)S(1)}, f32[32,128]{1,0:T(8,128)S(1)}, u32[]{:S(2)}, u32[]{:S(2)}) collective-permute-start(f32[32,128]{1,0:T(8,128)S(1)} %get-tuple-element.22.own_ref), channel_id=1, source_target_pairs={{0,96},{32,128},{64,160},{96,192},{128,224},{1,97},{33,129},{65,16... | collective-permute-start | bytes 49160 | tf_op jit(solution)/shard_map/ppermute | solution.py:23
  23.9 12.6 %collective-permute-start.10 = (bf16[1024,128]{1,0:T(8,128)(2,1)S(1)}, bf16[1024,128]{1,0:T(8,128)(2,1)S(1)}, u32[]{:S(2)}, u32[]{:S(2)}) collective-permute-start(bf16[1024,128]{1,0:T(8,128)(2,1)S(1)} %get-tuple-element.35.refs_0_), channel_id=1, source_target_pairs={{0,28},{4,0},{8,4},{12,8},{16,12},{20,16},{24,20},{28,24},{1,29},{... | collective-permute-start | bytes 786440 | tf_op jit(solution)/shard_map/ppermute | solution.py:18
  29.8 10.4 %collective-permute-start.7 = (bf16[1024,128]{1,0:T(8,128)(2,1)S(1)}, bf16[1024,128]{1,0:T(8,128)(2,1)S(1)}, u32[]{:S(2)}, u32[]{:S(2)}) collective-permute-start(bf16[1024,128]{1,0:T(8,128)(2,1)S(1)} %get-tuple-element.35.refs_0_), channel_id=1, source_target_pairs={{0,4},{4,8},{8,12},{12,16},{16,20},{20,24},{24,28},{28,0},{1,5},{5... | collective-permute-start | bytes 786440 | tf_op jit(solution)/shard_map/ppermute | solution.py:18
  29.8 12.3 %collective-permute-start.24 = (bf16[1024,128]{1,0:T(8,128)(2,1)S(1)}, bf16[1024,128]{1,0:T(8,128)(2,1)S(1)}, u32[]{:S(2)}, u32[]{:S(2)}) collective-permute-start(bf16[1024,128]{1,0:T(8,128)(2,1)S(1)} %get-tuple-element.36.refs_0_), channel_id=1, source_target_pairs={{0,28},{4,0},{8,4},{12,8},{16,12},{20,16},{24,20},{28,24},{1,29},{... | collective-permute-start | bytes 786440 | tf_op jit(solution)/shard_map/ppermute | solution.py:18
  36.5 11.2 %collective-permute-start.11 = (bf16[1024,128]{1,0:T(8,128)(2,1)S(1)}, bf16[1024,128]{1,0:T(8,128)(2,1)S(1)}, u32[]{:S(2)}, u32[]{:S(2)}) collective-permute-start(bf16[1024,128]{1,0:T(8,128)(2,1)S(1)} %collective-permute-done.10.refs_4_), channel_id=1, source_target_pairs={{0,28},{4,0},{8,4},{12,8},{16,12},{20,16},{24,20},{28,24},{1,29},{... | collective-permute-start | bytes 786440 | tf_op jit(solution)/shard_map/ppermute | solution.py:18
  40.2 13.2 %collective-permute-start.21 = (bf16[1024,128]{1,0:T(8,128)(2,1)S(1)}, bf16[1024,128]{1,0:T(8,128)(2,1)S(1)}, u32[]{:S(2)}, u32[]{:S(2)}) collective-permute-start(bf16[1024,128]{1,0:T(8,128)(2,1)S(1)} %get-tuple-element.36.refs_0_), channel_id=1, source_target_pairs={{0,4},{4,8},{8,12},{12,16},{16,20},{20,24},{24,28},{28,0},{1,5},{5... | collective-permute-start | bytes 786440 | tf_op jit(solution)/shard_map/ppermute | solution.py:18
  40.2 13.2 %collective-permute-start.8 = (bf16[1024,128]{1,0:T(8,128)(2,1)S(1)}, bf16[1024,128]{1,0:T(8,128)(2,1)S(1)}, u32[]{:S(2)}, u32[]{:S(2)}) collective-permute-start(bf16[1024,128]{1,0:T(8,128)(2,1)S(1)} %collective-permute-done.7.refs_1_), channel_id=1, source_target_pairs={{0,4},{4,8},{8,12},{12,16},{16,20},{20,24},{24,28},{28,0},{1,5},{5... | collective-permute-start | bytes 786440 | tf_op jit(solution)/shard_map/ppermute | solution.py:18
  42.1 14.5 %collective-permute-start.25 = (bf16[1024,128]{1,0:T(8,128)(2,1)S(1)}, bf16[1024,128]{1,0:T(8,128)(2,1)S(1)}, u32[]{:S(2)}, u32[]{:S(2)}) collective-permute-start(bf16[1024,128]{1,0:T(8,128)(2,1)S(1)} %collective-permute-done.24.refs_4_), channel_id=1, source_target_pairs={{0,28},{4,0},{8,4},{12,8},{16,12},{20,16},{24,20},{28,24},{1,29},{... | collective-permute-start | bytes 786440 | tf_op jit(solution)/shard_map/ppermute | solution.py:18
  47.7 10.3 %collective-permute-start.12 = (bf16[1024,128]{1,0:T(8,128)(2,1)S(1)}, bf16[1024,128]{1,0:T(8,128)(2,1)S(1)}, u32[]{:S(2)}, u32[]{:S(2)}) collective-permute-start(bf16[1024,128]{1,0:T(8,128)(2,1)S(1)} %collective-permute-done.11.refs_5_), channel_id=1, source_target_pairs={{0,28},{4,0},{8,4},{12,8},{16,12},{20,16},{24,20},{28,24},{1,29},{... | collective-permute-start | bytes 786440 | tf_op jit(solution)/shard_map/ppermute | solution.py:18
  53.4 10.3 %collective-permute-start.22 = (bf16[1024,128]{1,0:T(8,128)(2,1)S(1)}, bf16[1024,128]{1,0:T(8,128)(2,1)}, u32[]{:S(2)}, u32[]{:S(2)}) collective-permute-start(bf16[1024,128]{1,0:T(8,128)(2,1)S(1)} %collective-permute-done.21.refs_1_), channel_id=1, source_target_pairs={{0,4},{4,8},{8,12},{12,16},{16,20},{20,24},{24,28},{28,0},{1,5},{5... | collective-permute-start | bytes 786440 | tf_op jit(solution)/shard_map/ppermute | solution.py:18
  53.4 13.0 %collective-permute-start.9 = (bf16[1024,128]{1,0:T(8,128)(2,1)S(1)}, bf16[1024,128]{1,0:T(8,128)(2,1)S(1)}, u32[]{:S(2)}, u32[]{:S(2)}) collective-permute-start(bf16[1024,128]{1,0:T(8,128)(2,1)S(1)} %collective-permute-done.8.refs_2_), channel_id=1, source_target_pairs={{0,4},{4,8},{8,12},{12,16},{16,20},{20,24},{24,28},{28,0},{1,5},{5... | collective-permute-start | bytes 786440 | tf_op jit(solution)/shard_map/ppermute | solution.py:18
  53.5 13.5 %collective-permute-start.17 = (bf16[8,128,128]{2,1,0:T(8,128)(2,1)S(1)}, bf16[8,128,128]{2,1,0:T(8,128)(2,1)S(1)}, u32[]{:S(2)}, u32[]{:S(2)}) collective-permute-start(bf16[8,128,128]{2,1,0:T(8,128)(2,1)S(1)} %get-tuple-element.31), channel_id=1, source_target_pairs={{0,3},{1,0},{2,1},{3,2},{4,7},{5,4},{6,5},{7,6},{8,11},{9,8},{10,9... | collective-permute-start | bytes 786440 | tf_op jit(solution)/shard_map/ppermute | solution.py:18
  56.6 14.4 %collective-permute-start.16 = (bf16[8,128,128]{2,1,0:T(8,128)(2,1)S(1)}, bf16[8,128,128]{2,1,0:T(8,128)(2,1)S(1)}, u32[]{:S(2)}, u32[]{:S(2)}) collective-permute-start(bf16[8,128,128]{2,1,0:T(8,128)(2,1)S(1)} %get-tuple-element.32), channel_id=1, source_target_pairs={{0,2},{1,3},{2,0},{3,1},{4,6},{5,7},{6,4},{7,5},{8,10},{9,11},{10,... | collective-permute-start | bytes 786440 | tf_op jit(solution)/shard_map/ppermute | solution.py:18
  58.0 13.7 %collective-permute-start.15 = (bf16[8,128,128]{2,1,0:T(8,128)(2,1)}, bf16[8,128,128]{2,1,0:T(8,128)(2,1)}, u32[]{:S(2)}, u32[]{:S(2)}) collective-permute-start(bf16[8,128,128]{2,1,0:T(8,128)(2,1)} %get-tuple-element.33), channel_id=1, source_target_pairs={{0,1},{1,2},{2,3},{3,0},{4,5},{5,6},{6,7},{7,4},{8,9},{9,10},{10,1... | collective-permute-start | bytes 786440 | tf_op jit(solution)/shard_map/ppermute | solution.py:18
  63.7 24.5 %collective-permute-start.26 = (bf16[1024,128]{1,0:T(8,128)(2,1)S(1)}, bf16[1024,128]{1,0:T(8,128)(2,1)S(1)}, u32[]{:S(2)}, u32[]{:S(2)}) collective-permute-start(bf16[1024,128]{1,0:T(8,128)(2,1)S(1)} %collective-permute-done.25.refs_5_), channel_id=1, source_target_pairs={{0,28},{4,0},{8,4},{12,8},{16,12},{20,16},{24,20},{28,24},{1,29},{... | collective-permute-start | bytes 786440 | tf_op jit(solution)/shard_map/ppermute | solution.py:18
  66.4 21.9 %collective-permute-start.23 = (bf16[1024,128]{1,0:T(8,128)(2,1)}, bf16[1024,128]{1,0:T(8,128)(2,1)S(1)}, u32[]{:S(2)}, u32[]{:S(2)}) collective-permute-start(bf16[1024,128]{1,0:T(8,128)(2,1)} %collective-permute-done.22.refs_2_), channel_id=1, source_target_pairs={{0,4},{4,8},{8,12},{12,16},{16,20},{20,24},{24,28},{28,0},{1,5},{5... | collective-permute-start | bytes 786440 | tf_op jit(solution)/shard_map/ppermute | solution.py:18
  83.5 17.5 %collective-permute-start.18 = (bf16[1024,128]{1,0:T(8,128)(2,1)S(1)}, bf16[1024,128]{1,0:T(8,128)(2,1)S(1)}, u32[]{:S(2)}, u32[]{:S(2)}) collective-permute-start(bf16[1024,128]{1,0:T(8,128)(2,1)S(1)} %get-tuple-element.24), channel_id=1, source_target_pairs={{0,3},{1,0},{2,1},{3,2},{4,7},{5,4},{6,5},{7,6},{8,11},{9,8},{10,9... | collective-permute-start | bytes 786440 | tf_op jit(solution)/shard_map/ppermute | solution.py:18
  86.6 14.4 %collective-permute-start.19 = (bf16[1024,128]{1,0:T(8,128)(2,1)S(1)}, bf16[1024,128]{1,0:T(8,128)(2,1)S(1)}, u32[]{:S(2)}, u32[]{:S(2)}) collective-permute-start(bf16[1024,128]{1,0:T(8,128)(2,1)S(1)} %get-tuple-element.25), channel_id=1, source_target_pairs={{0,2},{1,3},{2,0},{3,1},{4,6},{5,7},{6,4},{7,5},{8,10},{9,11},{10,... | collective-permute-start | bytes 786440 | tf_op jit(solution)/shard_map/ppermute | solution.py:18
  87.2 13.8 %collective-permute-start.20 = (bf16[1024,128]{1,0:T(8,128)(2,1)S(1)}, bf16[1024,128]{1,0:T(8,128)(2,1)S(1)}, u32[]{:S(2)}, u32[]{:S(2)}) collective-permute-start(bf16[1024,128]{1,0:T(8,128)(2,1)S(1)} %get-tuple-element.26), channel_id=1, source_target_pairs={{0,1},{1,2},{2,3},{3,0},{4,5},{5,6},{6,7},{7,4},{8,9},{9,10},{10,1... | collective-permute-start | bytes 786440 | tf_op jit(solution)/shard_map/ppermute | solution.py:18
  96.9 9.2 %collective-permute-start.29 = (bf16[1024,128]{1,0:T(8,128)(2,1)S(1)}, bf16[1024,128]{1,0:T(8,128)(2,1)S(1)}, u32[]{:S(2)}, u32[]{:S(2)}) collective-permute-start(bf16[1024,128]{1,0:T(8,128)(2,1)S(1)} %get-tuple-element.28), channel_id=1, source_target_pairs={{0,3},{1,0},{2,1},{3,2},{4,7},{5,4},{6,5},{7,6},{8,11},{9,8},{10,9... | collective-permute-start | bytes 786440 | tf_op jit(solution)/shard_map/ppermute | solution.py:18
  101.0 9.0 %collective-permute-start.31 = (bf16[1024,128]{1,0:T(8,128)(2,1)S(1)}, bf16[1024,128]{1,0:T(8,128)(2,1)S(1)}, u32[]{:S(2)}, u32[]{:S(2)}) collective-permute-start(bf16[1024,128]{1,0:T(8,128)(2,1)S(1)} %get-tuple-element.30), channel_id=1, source_target_pairs={{0,1},{1,2},{2,3},{3,0},{4,5},{5,6},{6,7},{7,4},{8,9},{9,10},{10,1... | collective-permute-start | bytes 786440 | tf_op jit(solution)/shard_map/ppermute | solution.py:18
  (21 other events, 133.6 us)

commit v2 on v1

v2 whole, which is shorter than its diff:
```python
import jax
import jax.numpy as jnp
from jax import lax
from jax.experimental import pallas as pl
from jax.experimental.pallas import tpu as pltpu
from jax.sharding import Mesh, PartitionSpec as P

CTX = ("x", "core")
SUB = 8
PAD = 8
UNROLL = 8
PIECES = (1024, 1024)
VMEM_LIMIT = 16 * 1024 * 1024
ROW_TILE = 256


def shifted(value, axis, steps):
    count = lax.axis_size(axis)
    return lax.ppermute(value, axis, [(at, (at + steps) % count) for at in range(count)])


def from_behind(value, axis, steps):
    count = lax.axis_size(axis)
    return lax.ppermute(value, axis, [(at, at + steps) for at in range(count - steps)])


def wide(row):
    return jnp.broadcast_to(row, (SUB, row.shape[-1]))


def added(parts):
    while len(parts) > 1:
        pairs = [a + b for a, b in zip(parts[0::2], parts[1::2])]
        parts = pairs + parts[2 * len(pairs) :]
    return parts[0]


def unpack_stream(raw_ref, padded_ref, first=0, last=None):
    last = raw_ref.shape[0] if last is None else last
    if first == 0:
        padded_ref[0:PAD, :] = jnp.zeros((PAD, padded_ref.shape[1]), jnp.float32)
    tile = 128
    for at in range(first, last, tile):
        padded_ref[PAD + at : PAD + at + tile, :] = raw_ref[at : at + tile, :].astype(jnp.float32)


def mode_rows(taps_ref, rate_ref, residue_ref):
    taps = lambda j, s: taps_ref[j, s : s + 1, :]
    rate = rate_ref[...]
    return taps, rate, residue_ref[...] * jnp.sqrt(2.0 * rate)


def state_kernel(stream_ref, taps_ref, rate_ref, signal_ref, start_ref, packed_ref, key_ref, val_ref):
    rows = stream_ref.shape[1]
    steps = rows // SUB
    order, _, chans = start_ref.shape
    unpack_stream(stream_ref.at[1], key_ref)
    unpack_stream(stream_ref.at[2], val_ref)
    taps, rates, _ = mode_rows(taps_ref, rate_ref, rate_ref)
    fade = jnp.exp(-rates)
    decay = [wide(fade[r : r + 1, :]) for r in range(order)]
    key_taps = [wide(taps(j, 1)) for j in range(3)]
    val_taps = [wide(taps(j, 2)) for j in range(3)]
    block = lax.broadcasted_iota(jnp.int32, (SUB, chans), 0)

    def row(ref, step):
        return ref[pl.ds(PAD + step, SUB, stride=steps), :]

    def advance(step, carried, masked):
        k2, k1, v2, v1, *states = carried
        k0 = row(key_ref, step)
        v0 = row(val_ref, step)
        key = key_taps[0] * k2 + key_taps[1] * k1 + key_taps[2] * k0
        val = val_taps[0] * v2 + val_taps[1] * v1 + val_taps[2] * v0
        signal = key * val
        if masked:
            signal = jnp.where(block == 0, 0.0, signal)
        signal_ref[step] = signal
        states = [a * h + signal for a, h in zip(decay, states)]
        return [k1, k0, v1, v0, *states]

    carried = [row(key_ref, -2), row(key_ref, -1), row(val_ref, -2), row(val_ref, -1)]
    carried += [jnp.zeros((SUB, chans), jnp.float32)] * order
    for step in range(UNROLL):
        carried = advance(step, carried, step < 2)

    def body(at, carried):
        carried = list(carried)
        for step in range(UNROLL):
            carried = advance(at * UNROLL + step, carried, False)
        return tuple(carried)

    states = lax.fori_loop(1, steps // UNROLL, body, tuple(carried))[4:]
    for r in range(order):
        rate = wide(rates[r : r + 1, :])
        total = states[r]
        for back in (1, 2, 4):
            gain = jnp.where(block >= back, jnp.exp(-rate * (steps * back)), 0.0)
            total = total + gain * pltpu.roll(total, back, 0)
        packed_ref[r : r + 1, :] = total[SUB - 1 : SUB, :]
        start_ref[r] = jnp.where(block == 0, 0.0, pltpu.roll(total, 1, 0))
    heads = [
        stream_ref[0, 0:16, :].astype(jnp.float32)[0:2, :],
        key_ref[PAD : PAD + 2, :],
        val_ref[PAD : PAD + 2, :],
    ]
    tails = [
        stream_ref[0, rows - 16 : rows, :].astype(jnp.float32)[14:16, :],
        key_ref[PAD + rows - 2 : PAD + rows, :],
        val_ref[PAD + rows - 2 : PAD + rows, :],
    ]
    for s in range(3):
        packed_ref[order + 2 * s : order + 2 * s + 2, :] = heads[s]
        packed_ref[order + 6 + 2 * s : order + 8 + 2 * s, :] = tails[s]
    packed_ref[order + 12 :, :] = jnp.zeros((packed_ref.shape[0] - order - 12, chans), jnp.float32)


def local_kernel(
    stream_ref, taps_ref, rate_ref, residue_ref, skip_ref, signal_ref, start_ref, query_ref, conv_ref, raw_ref
):
    rows = stream_ref.shape[1]
    steps = rows // SUB
    order = start_ref.shape[0]
    unpack_stream(stream_ref.at[0], raw_ref)
    taps, rate, weights = mode_rows(taps_ref, rate_ref, residue_ref)
    fade = jnp.exp(-rate)
    decay = [wide(fade[r : r + 1, :]) for r in range(order)]
    weight = [wide(weights[r : r + 1, :]) for r in range(order)]
    taps = [wide(taps(j, 0)) for j in range(3)]
    skip = wide(skip_ref[0:1, :])

    def row(step):
        return raw_ref[pl.ds(PAD + step, SUB, stride=steps), :]

    def body(at, carried):
        q2, q1, *states = carried
        for inner in range(UNROLL):
            step = at * UNROLL + inner
            q0 = row(step)
            query_ref[step] = taps[0] * q2 + taps[1] * q1 + taps[2] * q0
            q2, q1 = q1, q0
            signal = signal_ref[step]
            states = [a * h + signal for a, h in zip(decay, states)]
            parts = [w * h for w, h in zip(weight, states)]
            parts.append(skip * signal)
            conv_ref[step] = added(parts)
        return (q2, q1, *states)

    carried = (row(-2), row(-1), *[start_ref[r] for r in range(order)])
    lax.fori_loop(0, steps // UNROLL, body, carried)


def pack_kernel(*refs):
    *parts, out_ref = refs
    for at, part in enumerate(parts):
        out_ref[at] = part[...]


def gate_kernel(core_ref, taps_ref, rate_ref, residue_ref, skip_ref, query_ref, conv_ref, *rest):
    *own_refs, other_ref, out_ref, nat_ref, ends_ref = rest
    rows, chans = out_ref.shape
    steps = rows // SUB
    core = core_ref[0]
    for back, own_ref in enumerate(own_refs):
        pair = 2 * (len(own_refs) - 1 - back)
        ends_ref[pair + core] = own_ref[...]
        ends_ref[pair + 1 - core] = other_ref[back]
    taps, rate, weight = mode_rows(taps_ref, rate_ref, residue_ref)
    skip = skip_ref[0:1, :]
    order = rate.shape[0]
    decay = jnp.exp(-rate)
    tap = [[taps(j, s) for s in range(3)] for j in range(3)]

    def head_feat(at, s):
        head, tail = order + 2 * s, order + 6 + 2 * s
        x0, x1 = ends_ref[at, head : head + 1, :], ends_ref[at, head + 1 : head + 2, :]
        if isinstance(at, int) and at == 0:
            m2 = m1 = jnp.zeros_like(x0)
        else:
            m2, m1 = ends_ref[at - 1, tail : tail + 1, :], ends_ref[at - 1, tail + 1 : tail + 2, :]
        first = tap[0][s] * m2 + tap[1][s] * m1 + tap[2][s] * x0
        second = tap[0][s] * m1 + tap[1][s] * x0 + tap[2][s] * x1
        return first, second

    whole = jnp.exp(-rate * rows)
    lead0 = jnp.exp(-rate * (rows - 1))
    lead1 = jnp.exp(-rate * (rows - 2))
    running = jnp.zeros((order, chans), jnp.float32)
    last = ends_ref.shape[0]
    for at in range(last):
        k0, k1 = head_feat(at, 1)
        v0, v1 = head_feat(at, 2)
        h0, h1 = head_feat(at, 0)
        now = (running, k0 * v0, k1 * v1, h0, h1)
        if at == last - 2:
            state, s0, s1, q0, q1 = now
        elif at == last - 1:
            state, s0, s1, q0, q1 = [
                jnp.where(core == 1, new, old) for new, old in zip(now, (state, s0, s1, q0, q1))
            ]
        running = whole * running + ends_ref[at, 0:order, :] + lead0 * now[1] + lead1 * now[2]
    at0 = decay * state + s0
    at1 = decay * at0 + s1
    conv0 = jnp.sum(weight * at0, axis=0, keepdims=True) + skip * s0
    conv1 = jnp.sum(weight * at1, axis=0, keepdims=True) + skip * s1

    block = lax.broadcasted_iota(jnp.int32, (SUB, chans), 0).astype(jnp.float32)
    begin = weight * at1
    decays = [wide(decay[r : r + 1, :]) for r in range(order)]
    terms = [
        wide(begin[r : r + 1, :]) * jnp.exp(-wide(rate[r : r + 1, :]) * (block * steps - 1.0))
        for r in range(order)
    ]

    def body(at, terms):
        for inner in range(UNROLL):
            step = at * UNROLL + inner
            nat_ref[pl.ds(step, SUB, stride=steps), :] = query_ref[step] * added([conv_ref[step], *terms])
            terms = [p * a for p, a in zip(terms, decays)]
        return tuple(terms)

    lax.fori_loop(0, steps // UNROLL, body, tuple(terms))
    nat_ref[0:1, :] = q0 * conv0
    nat_ref[1:2, :] = q1 * conv1
    tile = 128
    for at in range(0, rows, tile):
        out_ref[at : at + tile, :] = nat_ref[at : at + tile, :].astype(jnp.bfloat16)


def pick_kernel(turn_ref, by_owner_ref, *out_refs):
    count = by_owner_ref.shape[1]
    for s, out_ref in enumerate(out_refs):
        out_ref[...] = by_owner_ref[:, lax.rem(turn_ref[0] + s + 1, count)]


def weight_kernel(turn_ref, by_owner_ref, *refs):
    *pieces, weight = refs
    count, _, depth, _ = by_owner_ref.shape
    for j in range(count):
        source = lax.rem(turn_ref[1] - j + count, count)
        rows = slice(j * depth, (j + 1) * depth)
        weight[rows, 0:depth] = by_owner_ref[source, turn_ref[0]]
        for s, piece in enumerate(pieces):
            weight[rows, (s + 1) * depth : (s + 2) * depth] = piece[source]


def project_kernel(here, f1, f2, f3, b1, b2, b3, far, weight, own, p1, p2, p3):
    rows, depth = here.shape
    for start in range(0, rows, ROW_TILE):
        span = slice(start, start + ROW_TILE)
        order = (here, f1, f2, f3, far, b3, b2, b1)
        left = jnp.concatenate([piece[span, :] for piece in order], axis=1)
        total = jnp.dot(left, weight[...], preferred_element_type=jnp.float32)
        own[span, :] = total[:, 0:depth]
        for s, part in enumerate((p1, p2, p3)):
            part[span, :] = total[:, (s + 1) * depth : (s + 2) * depth].astype(jnp.bfloat16)


def call(kernel, shapes, scratch, flops, args, name, limit=VMEM_LIMIT, **more):
    size = sum(a.size * a.dtype.itemsize for a in args) + sum(
        s.size * jnp.dtype(s.dtype).itemsize for s in jax.tree.leaves(shapes)
    )
    return pl.pallas_call(
        kernel,
        out_shape=shapes,
        scratch_shapes=scratch,
        compiler_params=pltpu.CompilerParams(vmem_limit_bytes=limit),
        cost_estimate=pl.CostEstimate(flops=flops, bytes_accessed=size, transcendentals=0),
        name=name,
        **more,
    )(*args)


def shards(streams, short_filter, residue, decay_rate, skip_gain, out_weight):
    f32, bf16 = jnp.float32, jnp.bfloat16
    rows, _, chans = streams.shape
    order = residue.shape[0]
    steps = rows // SUB
    z_size, y_size = lax.axis_size("z"), lax.axis_size("y")
    z_at, y_at = lax.axis_index("z"), lax.axis_index("y")
    shape = jax.ShapeDtypeStruct

    smem = pl.BlockSpec(memory_space=pltpu.SMEM)
    vmem = pl.BlockSpec(memory_space=pltpu.VMEM)
    planes = jnp.transpose(streams, (1, 0, 2))
    plane = pltpu.VMEM((PAD + rows, chans), f32)
    by_step = shape((steps, SUB, chans), f32)
    modes = (short_filter, decay_rate, residue, skip_gain[None, :])
    signal, start, packed = call(
        state_kernel,
        (by_step, shape((order, SUB, chans), f32), shape((order + 16, chans), f32)),
        [plane, plane],
        rows * chans * 44,
        (planes, short_filter, decay_rate),
        "states",
    )
    own_ends = [packed] + [from_behind(packed, "x", s) for s in range(1, lax.axis_size("x"))]
    feat, conv = call(
        local_kernel,
        (by_step, by_step),
        [plane],
        rows * chans * 70,
        (planes, *modes, signal, start),
        "local_conv",
    )
    own_ends, conv = lax.optimization_barrier((own_ends, conv))
    ends = call(
        pack_kernel, shape((len(own_ends), *packed.shape), f32), [], 8 * packed.size, own_ends, "pack"
    )
    other_ends = shifted(ends, "core", 1)
    gated = call(
        gate_kernel,
        shape((rows, chans), bf16),
        [pltpu.VMEM((rows, chans), f32), pltpu.VMEM((2 * len(own_ends), *packed.shape), f32)],
        rows * chans * 34,
        (
            lax.axis_index("core").astype(jnp.int32).reshape(1),
            *modes,
            feat,
            conv,
            *own_ends,
            other_ends,
        ),
        "gate",
        in_specs=[smem] + [vmem] * (7 + len(own_ends)),
        out_specs=vmem,
    )

    bounds = [0]
    for count in PIECES:
        bounds.append(bounds[-1] + count)
    here = [gated[lo:hi] for lo, hi in zip(bounds, bounds[1:])]
    ahead, behind = [[h] for h in here], [[h] for h in here]

    def after(value, *others):
        return lax.optimization_barrier((value, *others))[0]

    def hop(piece, number):
        if number < 3 or piece == 0:
            ahead[piece].append(shifted(ahead[piece][-1], "z", 1))
        if number < 3 or piece == 1:
            behind[piece].append(shifted(behind[piece][-1], "z", -1))

    for number in range(4):
        hop(0, number)
        hop(1, number)
    turn = jnp.stack([y_at, z_at]).astype(jnp.int32)
    by_owner = out_weight.reshape(z_size, y_size, chans, chans)
    block = shape((z_size, chans, chans), bf16)
    sources = call(
        pick_kernel,
        (block,) * (y_size - 1),
        [],
        out_weight.size,
        (turn, after(by_owner, gated)),
        "pick",
        in_specs=[smem, vmem],
        out_specs=(vmem,) * (y_size - 1),
    )
    ties = (ahead[0][1], ahead[0][2], ahead[1][2])
    weights = [shifted(after(w, tie), "y", s + 1) for s, (w, tie) in enumerate(zip(sources, ties))]
    weight = call(
        weight_kernel,
        shape((z_size * chans, y_size * chans), bf16),
        [],
        out_weight.size,
        (turn, by_owner, *weights),
        "weights",
        in_specs=[smem] + [vmem] * y_size,
        out_specs=vmem,
    )
    ahead[0][0] = after(ahead[0][0], behind[1][3])

    def project(piece):
        count = PIECES[piece]
        part = shape((count, chans), bf16)
        own, *parts = call(
            project_kernel,
            (shape((count, chans), f32), part, part, part),
            [],
            2 * count * z_size * y_size * chans * chans,
            (*ahead[piece][:4], *behind[piece][1:4], (ahead, behind)[piece][piece][4], weight),
            "project",
        )
        total = own
        for s in range(1, y_size):
            total = total + shifted(parts[s - 1], "y", -s).astype(f32)
        return total.astype(bf16)

    return jnp.concatenate([project(piece) for piece in range(len(PIECES))], axis=0)


def solution(mesh):
    ctx_size, tp_size = mesh.devices.shape
    fine = Mesh(mesh.devices.reshape(ctx_size // 2, 2, tp_size // 4, 4), ("x", "core", "z", "y"))
    tp = ("z", "y")
    in_specs = (
        P(CTX, None, tp),
        P(None, None, tp),
        P(None, tp),
        P(None, tp),
        P(tp),
        P(None, tp),
    )
    return jax.shard_map(shards, mesh=fine, in_specs=in_specs, out_specs=P(CTX, tp), check_vma=False)
```

time: 112 us -> 95.1 us (0.85)
  the two profiles are of different devices: /device:TPU:2 before, /device:TPU:8 now
where the time goes in v2:
time: 95.1 us; the launch traced here: 94.8 us
  starting transfers between devices  45.7 us (48%)
  waiting for transfers between devices  33.5 us (35%)
  Pallas kernels  11.3 us (12%)
  local copies, waits for them, and re-layouts  2.87 us (3%)
  other arithmetic  1.15 us (1%)
    ppermute x24, starting transfers between devices, shifted(): lax.ppermute(value, axis, [(at, (at + steps) % count) for at in range(cou...  36.4 us
    ppermute x24, waiting for transfers between devices, shifted(): lax.ppermute(value, axis, [(at, (at + steps) % count) for at in range(cou...  33.5 us
    pallas_call x8, Pallas kernels, call(): pl.pallas_call(kernel, out_shape=shapes, scratch_shapes=scratch, compiler...  11.3 us
    ppermute x3, starting transfers between devices, from_behind(): lax.ppermute(value, axis, [(at, at + steps) for at in range(count - steps)])  9.32 us
    unnamed x16, local copies, waits for them, and re-layouts  2.83 us
  transfers between devices with their start and end apart: 27, of which 13 were waited for; matrix products, arithmetic and copies ran while one was open for 0% of the time, Pallas kernels for 8%

profile of v2, /device:TPU:8, one launch (start us, length us, event | category | flops | bytes accessed | tf_op | source)
XLA Modules:
  0.0 94.8 jit_solution(17176367406886015247)
XLA Ops:
  2.8 2.7 %states.1 = (f32[256,8,128]{2,1,0:T(8,128)S(1)}, f32[16,8,128]{2,1,0:T(8,128)S(1)}, f32[32,128]{1,0:T(8,128)S(1)}) custom-call(bf16[3,2048,128]{2,1,0:T(8,128)(2,1)S(1)} %bitcast.6, f32[3,3,128]{2,1,0:T(4,128)S(1)} %copy-done.4, f32[16,128]{1,0:T(8,128)S(1)} %copy-done.2), custom_call_target="tpu_custom_call" | custom-call | flops 11534336 | bytes 2716160 | tf_op jit(solution)/shard_map/states/pallas_call | solution.py:263
  5.5 3.4 %collective-permute-start = (f32[32,128]{1,0:T(8,128)S(1)}, f32[32,128]{1,0:T(8,128)S(1)}, u32[]{:S(2)}, u32[]{:S(2)}) collective-permute-start(f32[32,128]{1,0:T(8,128)S(1)} %get-tuple-element.37.refs_0_.rest_0_), channel_id=1, source_target_pairs={{0,64},{64,128},{128,192},{1,65},{65,129},{129,193},{2,66},{66,130... | collective-permute-start | bytes 49160 | tf_op jit(solution)/shard_map/ppermute | solution.py:24
  8.9 4.6 %collective-permute-start.1 = (f32[32,128]{1,0:T(8,128)S(1)}, f32[32,128]{1,0:T(8,128)S(1)}, u32[]{:S(2)}, u32[]{:S(2)}) collective-permute-start(f32[32,128]{1,0:T(8,128)S(1)} %get-tuple-element.37.refs_0_.rest_0_), channel_id=1, source_target_pairs={{0,128},{64,192},{1,129},{65,193},{2,130},{66,194},{3,131},{67,195... | collective-permute-start | bytes 49160 | tf_op jit(solution)/shard_map/ppermute | solution.py:24
  14.9 3.3 %local_conv.1 = (f32[256,8,128]{2,1,0:T(8,128)S(1)}, f32[256,8,128]{2,1,0:T(8,128)S(1)}) custom-call(bf16[3,2048,128]{2,1,0:T(8,128)(2,1)S(1)} %bitcast.7, f32[3,3,128]{2,1,0:T(4,128)S(1)} %copy-done.4, f32[16,128]{1,0:T(8,128)S(1)} %copy-done.2, f32[16,128]{1,0:T(8,128)S(1)} %copy-done.6, f32[1,128]{1,0:T(1,128)S(1)} %bitcast.10, ...), custom_call_target="tpu_custom_call" | custom-call | flops 18350080 | bytes 4805632 | tf_op jit(solution)/shard_map/local_conv/pallas_call | solution.py:263
  21.1 5.9 %collective-permute-start.4 = (bf16[1024,128]{1,0:T(8,128)(2,1)S(1)}, bf16[1024,128]{1,0:T(8,128)(2,1)S(1)}, u32[]{:S(2)}, u32[]{:S(2)}) collective-permute-start(bf16[1024,128]{1,0:T(8,128)(2,1)S(1)} %get-tuple-element.58.here), channel_id=1, source_target_pairs={{0,28},{4,0},{8,4},{12,8},{16,12},{20,16},{24,20},{28,24},{1,29},{... | collective-permute-start | bytes 786440 | tf_op jit(solution)/shard_map/ppermute | solution.py:19
  27.1 3.3 %collective-permute-start.10 = (bf16[1024,128]{1,0:T(8,128)(2,1)S(1)}, bf16[1024,128]{1,0:T(8,128)(2,1)S(1)}, u32[]{:S(2)}, u32[]{:S(2)}) collective-permute-start(bf16[1024,128]{1,0:T(8,128)(2,1)S(1)} %get-tuple-element.41.here), channel_id=1, source_target_pairs={{0,28},{4,0},{8,4},{12,8},{16,12},{20,16},{24,20},{28,24},{1,29},{... | collective-permute-start | bytes 786440 | tf_op jit(solution)/shard_map/ppermute | solution.py:19
  30.3 3.4 %collective-permute-done.4.b1 = bf16[1024,128]{1,0:T(8,128)(2,1)S(1)} collective-permute-done((bf16[1024,128]{1,0:T(8,128)(2,1)S(1)}, bf16[1024,128]{1,0:T(8,128)(2,1)S(1)}, u32[]{:S(2)}, u32[]{:S(2)}) %collective-permute-start.4) | collective-permute-done | bytes 262176 | tf_op jit(solution)/shard_map/ppermute | solution.py:19
  33.7 3.7 %collective-permute-start.5 = (bf16[1024,128]{1,0:T(8,128)(2,1)S(1)}, bf16[1024,128]{1,0:T(8,128)(2,1)S(1)}, u32[]{:S(2)}, u32[]{:S(2)}) collective-permute-start(bf16[1024,128]{1,0:T(8,128)(2,1)S(1)} %collective-permute-done.4.b1), channel_id=1, source_target_pairs={{0,28},{4,0},{8,4},{12,8},{16,12},{20,16},{24,20},{28,24},{1,29},{... | collective-permute-start | bytes 786440 | tf_op jit(solution)/shard_map/ppermute | solution.py:19
  38.2 4.9 %collective-permute-done.16.f1 = bf16[1024,128]{1,0:T(8,128)(2,1)S(1)} collective-permute-done((bf16[1024,128]{1,0:T(8,128)(2,1)S(1)}, bf16[1024,128]{1,0:T(8,128)(2,1)S(1)}, u32[]{:S(2)}, u32[]{:S(2)}) %collective-permute-start.16) | collective-permute-done | bytes 262176 | tf_op jit(solution)/shard_map/ppermute | solution.py:19
  43.1 1.6 %collective-permute-start.14 = (bf16[8,128,128]{2,1,0:T(8,128)(2,1)S(1)}, bf16[8,128,128]{2,1,0:T(8,128)(2,1)S(1)}, u32[]{:S(2)}, u32[]{:S(2)}) collective-permute-start(bf16[8,128,128]{2,1,0:T(8,128)(2,1)S(1)} %get-tuple-element.44), channel_id=1, source_target_pairs={{0,1},{1,2},{2,3},{3,0},{4,5},{5,6},{6,7},{7,4},{8,9},{9,10},{10,1... | collective-permute-start | bytes 786440 | tf_op jit(solution)/shard_map/ppermute | solution.py:19
  44.7 3.2 %collective-permute-start.11 = (bf16[1024,128]{1,0:T(8,128)(2,1)S(1)}, bf16[1024,128]{1,0:T(8,128)(2,1)S(1)}, u32[]{:S(2)}, u32[]{:S(2)}) collective-permute-start(bf16[1024,128]{1,0:T(8,128)(2,1)S(1)} %collective-permute-done.10.b1), channel_id=1, source_target_pairs={{0,28},{4,0},{8,4},{12,8},{16,12},{20,16},{24,20},{28,24},{1,29},{... | collective-permute-start | bytes 786440 | tf_op jit(solution)/shard_map/ppermute | solution.py:19
  48.7 2.3 %collective-permute-start.15 = (bf16[8,128,128]{2,1,0:T(8,128)(2,1)S(1)}, bf16[8,128,128]{2,1,0:T(8,128)(2,1)S(1)}, u32[]{:S(2)}, u32[]{:S(2)}) collective-permute-start(bf16[8,128,128]{2,1,0:T(8,128)(2,1)S(1)} %get-tuple-element.46), channel_id=1, source_target_pairs={{0,2},{1,3},{2,0},{3,1},{4,6},{5,7},{6,4},{7,5},{8,10},{9,11},{10,... | collective-permute-start | bytes 786440 | tf_op jit(solution)/shard_map/ppermute | solution.py:19
  51.0 2.2 %collective-permute-done.17.f2 = bf16[1024,128]{1,0:T(8,128)(2,1)S(1)} collective-permute-done((bf16[1024,128]{1,0:T(8,128)(2,1)S(1)}, bf16[1024,128]{1,0:T(8,128)(2,1)S(1)}, u32[]{:S(2)}, u32[]{:S(2)}) %collective-permute-start.17) | collective-permute-done | bytes 262176 | tf_op jit(solution)/shard_map/ppermute | solution.py:19
  53.8 2.8 %collective-permute-done.6.b3 = bf16[1024,128]{1,0:T(8,128)(2,1)S(1)} collective-permute-done((bf16[1024,128]{1,0:T(8,128)(2,1)S(1)}, bf16[1024,128]{1,0:T(8,128)(2,1)S(1)}, u32[]{:S(2)}, u32[]{:S(2)}) %collective-permute-start.6) | collective-permute-done | bytes 262176 | tf_op jit(solution)/shard_map/ppermute | solution.py:19
  56.6 3.7 %collective-permute-start.23 = (bf16[1024,128]{1,0:T(8,128)(2,1)S(1)}, bf16[1024,128]{1,0:T(8,128)(2,1)S(1)}, u32[]{:S(2)}, u32[]{:S(2)}) collective-permute-start(bf16[1024,128]{1,0:T(8,128)(2,1)S(1)} %collective-permute-done.6.b3), channel_id=1, source_target_pairs={{0,28},{4,0},{8,4},{12,8},{16,12},{20,16},{24,20},{28,24},{1,29},{... | collective-permute-start | bytes 786440 | tf_op jit(solution)/shard_map/ppermute | solution.py:19
  60.3 3.3 %collective-permute-done.9.f3 = bf16[1024,128]{1,0:T(8,128)(2,1)S(1)} collective-permute-done((bf16[1024,128]{1,0:T(8,128)(2,1)S(1)}, bf16[1024,128]{1,0:T(8,128)(2,1)S(1)}, u32[]{:S(2)}, u32[]{:S(2)}) %collective-permute-start.9) | collective-permute-done | bytes 262176 | tf_op jit(solution)/shard_map/ppermute | solution.py:19
  64.4 4.9 %collective-permute-done.22.f3 = bf16[1024,128]{1,0:T(8,128)(2,1)S(1)} collective-permute-done((bf16[1024,128]{1,0:T(8,128)(2,1)S(1)}, bf16[1024,128]{1,0:T(8,128)(2,1)S(1)}, u32[]{:S(2)}, u32[]{:S(2)}) %collective-permute-start.22) | collective-permute-done | bytes 262176 | tf_op jit(solution)/shard_map/ppermute | solution.py:19
  70.5 1.7 %collective-permute-start.26 = (bf16[1024,128]{1,0:T(8,128)(2,1)S(1)}, bf16[1024,128]{1,0:T(8,128)(2,1)S(1)}, u32[]{:S(2)}, u32[]{:S(2)}) collective-permute-start(bf16[1024,128]{1,0:T(8,128)(2,1)S(1)} %get-tuple-element.56), channel_id=1, source_target_pairs={{0,1},{1,2},{2,3},{3,0},{4,5},{5,6},{6,7},{7,4},{8,9},{9,10},{10,1... | collective-permute-start | bytes 786440 | tf_op jit(solution)/shard_map/ppermute | solution.py:19
  73.1 2.4 %collective-permute-start.24 = (bf16[1024,128]{1,0:T(8,128)(2,1)S(1)}, bf16[1024,128]{1,0:T(8,128)(2,1)S(1)}, u32[]{:S(2)}, u32[]{:S(2)}) collective-permute-start(bf16[1024,128]{1,0:T(8,128)(2,1)S(1)} %get-tuple-element.54), channel_id=1, source_target_pairs={{0,3},{1,0},{2,1},{3,2},{4,7},{5,4},{6,5},{7,6},{8,11},{9,8},{10,9... | collective-permute-start | bytes 786440 | tf_op jit(solution)/shard_map/ppermute | solution.py:19
  76.9 3.4 %collective-permute-start.20 = (bf16[1024,128]{1,0:T(8,128)(2,1)S(1)}, bf16[1024,128]{1,0:T(8,128)(2,1)S(1)}, u32[]{:S(2)}, u32[]{:S(2)}) collective-permute-start(bf16[1024,128]{1,0:T(8,128)(2,1)S(1)} %get-tuple-element.51), channel_id=1, source_target_pairs={{0,2},{1,3},{2,0},{3,1},{4,6},{5,7},{6,4},{7,5},{8,10},{9,11},{10,... | collective-permute-start | bytes 786440 | tf_op jit(solution)/shard_map/ppermute | solution.py:19
  80.3 3.5 %collective-permute-start.19 = (bf16[1024,128]{1,0:T(8,128)(2,1)S(1)}, bf16[1024,128]{1,0:T(8,128)(2,1)S(1)}, u32[]{:S(2)}, u32[]{:S(2)}) collective-permute-start(bf16[1024,128]{1,0:T(8,128)(2,1)S(1)} %get-tuple-element.50), channel_id=1, source_target_pairs={{0,3},{1,0},{2,1},{3,2},{4,7},{5,4},{6,5},{7,6},{8,11},{9,8},{10,9... | collective-permute-start | bytes 786440 | tf_op jit(solution)/shard_map/ppermute | solution.py:19
  83.9 4.0 %collective-permute-done.24 = bf16[1024,128]{1,0:T(8,128)(2,1)S(1)} collective-permute-done((bf16[1024,128]{1,0:T(8,128)(2,1)S(1)}, bf16[1024,128]{1,0:T(8,128)(2,1)S(1)}, u32[]{:S(2)}, u32[]{:S(2)}) %collective-permute-start.24) | collective-permute-done | bytes 262176 | tf_op jit(solution)/shard_map/ppermute | solution.py:19
  89.0 2.9 %collective-permute-done.20 = bf16[1024,128]{1,0:T(8,128)(2,1)S(1)} collective-permute-done((bf16[1024,128]{1,0:T(8,128)(2,1)S(1)}, bf16[1024,128]{1,0:T(8,128)(2,1)S(1)}, u32[]{:S(2)}, u32[]{:S(2)}) %collective-permute-start.20) | collective-permute-done | bytes 262176 | tf_op jit(solution)/shard_map/ppermute | solution.py:19
  91.9 1.9 %collective-permute-done.19 = bf16[1024,128]{1,0:T(8,128)(2,1)S(1)} collective-permute-done((bf16[1024,128]{1,0:T(8,128)(2,1)S(1)}, bf16[1024,128]{1,0:T(8,128)(2,1)S(1)}, u32[]{:S(2)}, u32[]{:S(2)}) %collective-permute-start.19) | collective-permute-done | bytes 262176 | tf_op jit(solution)/shard_map/ppermute | solution.py:19
  (59 shorter events, 15.5 us)
Async XLA Ops:
  5.5 12.7 %collective-permute-start = (f32[32,128]{1,0:T(8,128)S(1)}, f32[32,128]{1,0:T(8,128)S(1)}, u32[]{:S(2)}, u32[]{:S(2)}) collective-permute-start(f32[32,128]{1,0:T(8,128)S(1)} %get-tuple-element.37.refs_0_.rest_0_), channel_id=1, source_target_pairs={{0,64},{64,128},{128,192},{1,65},{65,129},{129,193},{2,66},{66,130... | collective-permute-start | bytes 49160 | tf_op jit(solution)/shard_map/ppermute | solution.py:24
  8.9 9.3 %collective-permute-start.1 = (f32[32,128]{1,0:T(8,128)S(1)}, f32[32,128]{1,0:T(8,128)S(1)}, u32[]{:S(2)}, u32[]{:S(2)}) collective-permute-start(f32[32,128]{1,0:T(8,128)S(1)} %get-tuple-element.37.refs_0_.rest_0_), channel_id=1, source_target_pairs={{0,128},{64,192},{1,129},{65,193},{2,130},{66,194},{3,131},{67,195... | collective-permute-start | bytes 49160 | tf_op jit(solution)/shard_map/ppermute | solution.py:24
  21.1 12.6 %collective-permute-start.4 = (bf16[1024,128]{1,0:T(8,128)(2,1)S(1)}, bf16[1024,128]{1,0:T(8,128)(2,1)S(1)}, u32[]{:S(2)}, u32[]{:S(2)}) collective-permute-start(bf16[1024,128]{1,0:T(8,128)(2,1)S(1)} %get-tuple-element.58.here), channel_id=1, source_target_pairs={{0,28},{4,0},{8,4},{12,8},{16,12},{20,16},{24,20},{28,24},{1,29},{... | collective-permute-start | bytes 786440 | tf_op jit(solution)/shard_map/ppermute | solution.py:19
  27.1 10.4 %collective-permute-start.7 = (bf16[1024,128]{1,0:T(8,128)(2,1)S(1)}, bf16[1024,128]{1,0:T(8,128)(2,1)S(1)}, u32[]{:S(2)}, u32[]{:S(2)}) collective-permute-start(bf16[1024,128]{1,0:T(8,128)(2,1)S(1)} %get-tuple-element.41.here), channel_id=1, source_target_pairs={{0,4},{4,8},{8,12},{12,16},{16,20},{20,24},{24,28},{28,0},{1,5},{5... | collective-permute-start | bytes 786440 | tf_op jit(solution)/shard_map/ppermute | solution.py:19
  27.1 16.0 %collective-permute-start.16 = (bf16[1024,128]{1,0:T(8,128)(2,1)S(1)}, bf16[1024,128]{1,0:T(8,128)(2,1)S(1)}, u32[]{:S(2)}, u32[]{:S(2)}) collective-permute-start(bf16[1024,128]{1,0:T(8,128)(2,1)S(1)} %get-tuple-element.58.here), channel_id=1, source_target_pairs={{0,4},{4,8},{8,12},{12,16},{16,20},{20,24},{24,28},{28,0},{1,5},{5... | collective-permute-start | bytes 786440 | tf_op jit(solution)/shard_map/ppermute | solution.py:19
  27.1 17.6 %collective-permute-start.10 = (bf16[1024,128]{1,0:T(8,128)(2,1)S(1)}, bf16[1024,128]{1,0:T(8,128)(2,1)S(1)}, u32[]{:S(2)}, u32[]{:S(2)}) collective-permute-start(bf16[1024,128]{1,0:T(8,128)(2,1)S(1)} %get-tuple-element.41.here), channel_id=1, source_target_pairs={{0,28},{4,0},{8,4},{12,8},{16,12},{20,16},{24,20},{28,24},{1,29},{... | collective-permute-start | bytes 786440 | tf_op jit(solution)/shard_map/ppermute | solution.py:19
  33.7 14.2 %collective-permute-start.5 = (bf16[1024,128]{1,0:T(8,128)(2,1)S(1)}, bf16[1024,128]{1,0:T(8,128)(2,1)S(1)}, u32[]{:S(2)}, u32[]{:S(2)}) collective-permute-start(bf16[1024,128]{1,0:T(8,128)(2,1)S(1)} %collective-permute-done.4.b1), channel_id=1, source_target_pairs={{0,28},{4,0},{8,4},{12,8},{16,12},{20,16},{24,20},{28,24},{1,29},{... | collective-permute-start | bytes 786440 | tf_op jit(solution)/shard_map/ppermute | solution.py:19
  37.5 11.2 %collective-permute-start.8 = (bf16[1024,128]{1,0:T(8,128)(2,1)S(1)}, bf16[1024,128]{1,0:T(8,128)(2,1)S(1)}, u32[]{:S(2)}, u32[]{:S(2)}) collective-permute-start(bf16[1024,128]{1,0:T(8,128)(2,1)S(1)} %collective-permute-done.7.f1), channel_id=1, source_target_pairs={{0,4},{4,8},{8,12},{12,16},{16,20},{20,24},{24,28},{28,0},{1,5},{5... | collective-permute-start | bytes 786440 | tf_op jit(solution)/shard_map/ppermute | solution.py:19
  43.1 10.1 %collective-permute-start.17 = (bf16[1024,128]{1,0:T(8,128)(2,1)S(1)}, bf16[1024,128]{1,0:T(8,128)(2,1)S(1)}, u32[]{:S(2)}, u32[]{:S(2)}) collective-permute-start(bf16[1024,128]{1,0:T(8,128)(2,1)S(1)} %collective-permute-done.16.f1), channel_id=1, source_target_pairs={{0,4},{4,8},{8,12},{12,16},{16,20},{20,24},{24,28},{28,0},{1,5},{5... | collective-permute-start | bytes 786440 | tf_op jit(solution)/shard_map/ppermute | solution.py:19
  43.1 10.1 %collective-permute-start.14 = (bf16[8,128,128]{2,1,0:T(8,128)(2,1)S(1)}, bf16[8,128,128]{2,1,0:T(8,128)(2,1)S(1)}, u32[]{:S(2)}, u32[]{:S(2)}) collective-permute-start(bf16[8,128,128]{2,1,0:T(8,128)(2,1)S(1)} %get-tuple-element.44), channel_id=1, source_target_pairs={{0,1},{1,2},{2,3},{3,0},{4,5},{5,6},{6,7},{7,4},{8,9},{9,10},{10,1... | collective-permute-start | bytes 786440 | tf_op jit(solution)/shard_map/ppermute | solution.py:19
  44.7 9.1 %collective-permute-start.11 = (bf16[1024,128]{1,0:T(8,128)(2,1)S(1)}, bf16[1024,128]{1,0:T(8,128)(2,1)S(1)}, u32[]{:S(2)}, u32[]{:S(2)}) collective-permute-start(bf16[1024,128]{1,0:T(8,128)(2,1)S(1)} %collective-permute-done.10.b1), channel_id=1, source_target_pairs={{0,28},{4,0},{8,4},{12,8},{16,12},{20,16},{24,20},{28,24},{1,29},{... | collective-permute-start | bytes 786440 | tf_op jit(solution)/shard_map/ppermute | solution.py:19
  48.7 11.6 %collective-permute-start.15 = (bf16[8,128,128]{2,1,0:T(8,128)(2,1)S(1)}, bf16[8,128,128]{2,1,0:T(8,128)(2,1)S(1)}, u32[]{:S(2)}, u32[]{:S(2)}) collective-permute-start(bf16[8,128,128]{2,1,0:T(8,128)(2,1)S(1)} %get-tuple-element.46), channel_id=1, source_target_pairs={{0,2},{1,3},{2,0},{3,1},{4,6},{5,7},{6,4},{7,5},{8,10},{9,11},{10,... | collective-permute-start | bytes 786440 | tf_op jit(solution)/shard_map/ppermute | solution.py:19
  53.2 10.5 %collective-permute-start.9 = (bf16[1024,128]{1,0:T(8,128)(2,1)S(1)}, bf16[1024,128]{1,0:T(8,128)(2,1)S(1)}, u32[]{:S(2)}, u32[]{:S(2)}) collective-permute-start(bf16[1024,128]{1,0:T(8,128)(2,1)S(1)} %collective-permute-done.8.f2), channel_id=1, source_target_pairs={{0,4},{4,8},{8,12},{12,16},{16,20},{20,24},{24,28},{28,0},{1,5},{5... | collective-permute-start | bytes 786440 | tf_op jit(solution)/shard_map/ppermute | solution.py:19
  53.2 10.5 %collective-permute-start.18 = (bf16[8,128,128]{2,1,0:T(8,128)(2,1)S(1)}, bf16[8,128,128]{2,1,0:T(8,128)(2,1)S(1)}, u32[]{:S(2)}, u32[]{:S(2)}) collective-permute-start(bf16[8,128,128]{2,1,0:T(8,128)(2,1)S(1)} %get-tuple-element.48), channel_id=1, source_target_pairs={{0,3},{1,0},{2,1},{3,2},{4,7},{5,4},{6,5},{7,6},{8,11},{9,8},{10,9... | collective-permute-start | bytes 786440 | tf_op jit(solution)/shard_map/ppermute | solution.py:19
  53.8 15.5 %collective-permute-start.22 = (bf16[1024,128]{1,0:T(8,128)(2,1)S(1)}, bf16[1024,128]{1,0:T(8,128)(2,1)S(1)}, u32[]{:S(2)}, u32[]{:S(2)}) collective-permute-start(bf16[1024,128]{1,0:T(8,128)(2,1)S(1)} %collective-permute-done.17.f2), channel_id=1, source_target_pairs={{0,4},{4,8},{8,12},{12,16},{16,20},{20,24},{24,28},{28,0},{1,5},{5... | collective-permute-start | bytes 786440 | tf_op jit(solution)/shard_map/ppermute | solution.py:19
  56.6 12.7 %collective-permute-start.23 = (bf16[1024,128]{1,0:T(8,128)(2,1)S(1)}, bf16[1024,128]{1,0:T(8,128)(2,1)S(1)}, u32[]{:S(2)}, u32[]{:S(2)}) collective-permute-start(bf16[1024,128]{1,0:T(8,128)(2,1)S(1)} %collective-permute-done.6.b3), channel_id=1, source_target_pairs={{0,28},{4,0},{8,4},{12,8},{16,12},{20,16},{24,20},{28,24},{1,29},{... | collective-permute-start | bytes 786440 | tf_op jit(solution)/shard_map/ppermute | solution.py:19
  60.3 15.3 %collective-permute-start.12 = (bf16[1024,128]{1,0:T(8,128)(2,1)S(1)}, bf16[1024,128]{1,0:T(8,128)(2,1)S(1)}, u32[]{:S(2)}, u32[]{:S(2)}) collective-permute-start(bf16[1024,128]{1,0:T(8,128)(2,1)S(1)} %collective-permute-done.11.b2), channel_id=1, source_target_pairs={{0,28},{4,0},{8,4},{12,8},{16,12},{20,16},{24,20},{28,24},{1,29},{... | collective-permute-start | bytes 786440 | tf_op jit(solution)/shard_map/ppermute | solution.py:19
  63.7 11.9 %collective-permute-start.13 = (bf16[1024,128]{1,0:T(8,128)(2,1)S(1)}, bf16[1024,128]{1,0:T(8,128)(2,1)S(1)}, u32[]{:S(2)}, u32[]{:S(2)}) collective-permute-start(bf16[1024,128]{1,0:T(8,128)(2,1)S(1)} %collective-permute-done.9.f3), channel_id=1, source_target_pairs={{0,4},{4,8},{8,12},{12,16},{16,20},{20,24},{24,28},{28,0},{1,5},{5... | collective-permute-start | bytes 786440 | tf_op jit(solution)/shard_map/ppermute | solution.py:19
  70.5 9.8 %collective-permute-start.26 = (bf16[1024,128]{1,0:T(8,128)(2,1)S(1)}, bf16[1024,128]{1,0:T(8,128)(2,1)S(1)}, u32[]{:S(2)}, u32[]{:S(2)}) collective-permute-start(bf16[1024,128]{1,0:T(8,128)(2,1)S(1)} %get-tuple-element.56), channel_id=1, source_target_pairs={{0,1},{1,2},{2,3},{3,0},{4,5},{5,6},{6,7},{7,4},{8,9},{9,10},{10,1... | collective-permute-start | bytes 786440 | tf_op jit(solution)/shard_map/ppermute | solution.py:19
  72.2 11.7 %collective-permute-start.25 = (bf16[1024,128]{1,0:T(8,128)(2,1)S(1)}, bf16[1024,128]{1,0:T(8,128)(2,1)S(1)}, u32[]{:S(2)}, u32[]{:S(2)}) collective-permute-start(bf16[1024,128]{1,0:T(8,128)(2,1)S(1)} %get-tuple-element.55), channel_id=1, source_target_pairs={{0,2},{1,3},{2,0},{3,1},{4,6},{5,7},{6,4},{7,5},{8,10},{9,11},{10,... | collective-permute-start | bytes 786440 | tf_op jit(solution)/shard_map/ppermute | solution.py:19
  73.1 14.7 %collective-permute-start.24 = (bf16[1024,128]{1,0:T(8,128)(2,1)S(1)}, bf16[1024,128]{1,0:T(8,128)(2,1)S(1)}, u32[]{:S(2)}, u32[]{:S(2)}) collective-permute-start(bf16[1024,128]{1,0:T(8,128)(2,1)S(1)} %get-tuple-element.54), channel_id=1, source_target_pairs={{0,3},{1,0},{2,1},{3,2},{4,7},{5,4},{6,5},{7,6},{8,11},{9,8},{10,9... | collective-permute-start | bytes 786440 | tf_op jit(solution)/shard_map/ppermute | solution.py:19
  76.8 12.2 %collective-permute-start.21 = (bf16[1024,128]{1,0:T(8,128)(2,1)S(1)}, bf16[1024,128]{1,0:T(8,128)(2,1)S(1)}, u32[]{:S(2)}, u32[]{:S(2)}) collective-permute-start(bf16[1024,128]{1,0:T(8,128)(2,1)S(1)} %get-tuple-element.52), channel_id=1, source_target_pairs={{0,1},{1,2},{2,3},{3,0},{4,5},{5,6},{6,7},{7,4},{8,9},{9,10},{10,1... | collective-permute-start | bytes 786440 | tf_op jit(solution)/shard_map/ppermute | solution.py:19
  76.9 15.0 %collective-permute-start.20 = (bf16[1024,128]{1,0:T(8,128)(2,1)S(1)}, bf16[1024,128]{1,0:T(8,128)(2,1)S(1)}, u32[]{:S(2)}, u32[]{:S(2)}) collective-permute-start(bf16[1024,128]{1,0:T(8,128)(2,1)S(1)} %get-tuple-element.51), channel_id=1, source_target_pairs={{0,2},{1,3},{2,0},{3,1},{4,6},{5,7},{6,4},{7,5},{8,10},{9,11},{10,... | collective-permute-start | bytes 786440 | tf_op jit(solution)/shard_map/ppermute | solution.py:19
  80.3 13.6 %collective-permute-start.19 = (bf16[1024,128]{1,0:T(8,128)(2,1)S(1)}, bf16[1024,128]{1,0:T(8,128)(2,1)S(1)}, u32[]{:S(2)}, u32[]{:S(2)}) collective-permute-start(bf16[1024,128]{1,0:T(8,128)(2,1)S(1)} %get-tuple-element.50), channel_id=1, source_target_pairs={{0,3},{1,0},{2,1},{3,2},{4,7},{5,4},{6,5},{7,6},{8,11},{9,8},{10,9... | collective-permute-start | bytes 786440 | tf_op jit(solution)/shard_map/ppermute | solution.py:19
  (11 other events, 90.5 us)

commit v3 on v2

v3 whole, which is shorter than its diff:
```python
import math

import jax
import jax.numpy as jnp
from jax import lax
from jax.experimental import pallas as pl
from jax.experimental.pallas import tpu as pltpu
from jax.sharding import Mesh, PartitionSpec as P

CTX = ("x", "core")
SUB = 8
PAD = 8
UNROLL = 8
HALF = 1024
KINDS = (2, 1, 3)
LOADS = 4
BACK = (0, 2, 1, 3)
VMEM_LIMIT = 16 * 1024 * 1024
ROW_TILE = 256


def shifted(value, axis, steps):
    count = lax.axis_size(axis)
    return lax.ppermute(value, axis, [(at, (at + steps) % count) for at in range(count)])


def swapped(value, kind):
    count = lax.axis_size("y")
    pairs = []
    for core in range(2):
        flip = kind if kind == 2 or core == 0 else 4 - kind
        pairs += [(core * count + at, core * count + (at ^ flip)) for at in range(count)]
    return lax.ppermute(value, ("core", "y"), pairs)


def peers():
    core, here = lax.axis_index("core"), lax.axis_index("y")
    return {kind: here ^ (kind + core * (4 - 2 * kind)) for kind in (1, 2, 3)}


def from_behind(value, axis, steps):
    count = lax.axis_size(axis)
    return lax.ppermute(value, axis, [(at, at + steps) for at in range(count - steps)])


def wide(row):
    return jnp.broadcast_to(row, (SUB, row.shape[-1]))


def added(parts):
    while len(parts) > 1:
        pairs = [a + b for a, b in zip(parts[0::2], parts[1::2])]
        parts = pairs + parts[2 * len(pairs) :]
    return parts[0]


def widen(raw, padded_ref, first, last):
    blocks, steps, _ = raw.shape
    for c in range(blocks):
        at = c * (steps + PAD) + PAD
        padded_ref[at + first : at + last, :] = raw[c, first:last, :].astype(jnp.float32)


def lead_in(tails, padded_ref, steps):
    blocks, count, chans = tails.shape
    padded_ref[PAD - 2 : PAD, :] = jnp.zeros((2, chans), jnp.float32)
    for c in range(1, blocks):
        at = c * (steps + PAD) + PAD
        padded_ref[at - 2 : at, :] = tails[c - 1].astype(jnp.float32)[count - 2 : count, :]


def row_of(ref, step, steps):
    return ref[pl.ds(PAD + step, SUB, stride=steps + PAD), :]


def mode_rows(param_ref):
    order = (param_ref.shape[0] - 16) // 3
    taps = lambda j, s: param_ref[3 * j + s : 3 * j + s + 1, :]
    rate, decay, weight = [param_ref[16 + order * i : 16 + order * (i + 1), :] for i in range(3)]
    return taps, param_ref[9:10, :], rate, decay, weight


def state_kernel(stream_hbm, taps_hbm, rate_hbm, residue_hbm, skip_hbm, *rest):
    signal_ref, start_ref, packed_ref, param_ref, *scratch = rest
    raw_ref, tail_ref, edge_ref, taps_ref, rate_ref, residue_ref, skip_ref, key_ref, val_ref, sems = scratch
    _, blocks, steps, chans = stream_hbm.shape
    order = rate_ref.shape[0]
    pair = pl.ds(1, 2)
    part = steps // LOADS
    sources = [
        (stream_hbm.at[pair, :, pl.ds(steps - 16, 16)], tail_ref),
        (taps_hbm, taps_ref),
        (rate_hbm, rate_ref),
        (residue_hbm, residue_ref),
        (skip_hbm, skip_ref),
        (stream_hbm.at[0, 0, pl.ds(0, 16)], edge_ref.at[0]),
        (stream_hbm.at[0, blocks - 1, pl.ds(steps - 16, 16)], edge_ref.at[1]),
    ]
    for at in range(LOADS):
        span = pl.ds(at * part, part)
        sources.append((stream_hbm.at[pair, :, span], raw_ref.at[:, :, span]))
    copies = [pltpu.make_async_copy(*pair, sems.at[i]) for i, pair in enumerate(sources)]
    small, large = copies[:-LOADS], copies[-LOADS:]
    for copy in small[:3] + large + small[3:]:
        copy.start()
    for copy in small:
        copy.wait()

    for j in range(3):
        for s in range(3):
            param_ref[3 * j + s : 3 * j + s + 1, :] = taps_ref[j, s : s + 1, :]
    param_ref[9:10, :] = skip_ref[...]
    param_ref[10:16, :] = jnp.zeros((6, chans), jnp.float32)
    rates = rate_ref[...]
    param_ref[16 : 16 + order, :] = rates
    param_ref[16 + order : 16 + 2 * order, :] = jnp.exp(-rates)
    param_ref[16 + 2 * order : 16 + 3 * order, :] = residue_ref[...] * jnp.sqrt(2.0 * rates)
    taps, _, _, fade, _ = mode_rows(param_ref)
    lead_in(tail_ref.at[0], key_ref, steps)
    lead_in(tail_ref.at[1], val_ref, steps)

    decay = [wide(fade[r : r + 1, :]) for r in range(order)]
    key_taps = [wide(taps(j, 1)) for j in range(3)]
    val_taps = [wide(taps(j, 2)) for j in range(3)]
    block = lax.broadcasted_iota(jnp.int32, (SUB, chans), 0)

    def advance(step, carried, masked):
        k2, k1, v2, v1, *states = carried
        k0 = row_of(key_ref, step, steps)
        v0 = row_of(val_ref, step, steps)
        key = key_taps[0] * k2 + key_taps[1] * k1 + key_taps[2] * k0
        val = val_taps[0] * v2 + val_taps[1] * v1 + val_taps[2] * v0
        signal = key * val
        if masked:
            signal = jnp.where(block == 0, 0.0, signal)
        signal_ref[step] = signal
        states = [a * h + signal for a, h in zip(decay, states)]
        return [k1, k0, v1, v0, *states]

    def body(at, carried):
        carried = list(carried)
        for step in range(UNROLL):
            carried = advance(at * UNROLL + step, carried, False)
        return tuple(carried)

    carried = [row_of(ref, step, steps) for ref in (key_ref, val_ref) for step in (-2, -1)]
    carried += [jnp.zeros((SUB, chans), jnp.float32)] * order
    for at in range(LOADS):
        large[at].wait()
        for which, ref in enumerate((key_ref, val_ref)):
            widen(raw_ref.at[which], ref, at * part, (at + 1) * part)
        begin = at * part // UNROLL
        if at == 0:
            for step in range(UNROLL):
                carried = advance(step, carried, step < 2)
            begin = 1
        carried = lax.fori_loop(begin, (at + 1) * part // UNROLL, body, tuple(carried))
    states = carried[4:]
    for r in range(order):
        rate = wide(rates[r : r + 1, :])
        total = states[r]
        for back in (1, 2, 4):
            gain = jnp.where(block >= back, jnp.exp(-rate * (steps * back)), 0.0)
            total = total + gain * pltpu.roll(total, back, 0)
        packed_ref[r : r + 1, :] = total[SUB - 1 : SUB, :]
        start_ref[r] = jnp.where(block == 0, 0.0, pltpu.roll(total, 1, 0))
    end = blocks * (steps + PAD)
    heads = [edge_ref[0].astype(jnp.float32)[0:2, :], key_ref[PAD : PAD + 2, :], val_ref[PAD : PAD + 2, :]]
    tails = [
        edge_ref[1].astype(jnp.float32)[14:16, :],
        key_ref[end - 2 : end, :],
        val_ref[end - 2 : end, :],
    ]
    for s in range(3):
        packed_ref[order + 2 * s : order + 2 * s + 2, :] = heads[s]
        packed_ref[order + 6 + 2 * s : order + 8 + 2 * s, :] = tails[s]
    packed_ref[order + 12 :, :] = jnp.zeros((packed_ref.shape[0] - order - 12, chans), jnp.float32)


def local_steps(first, param_ref, signal_ref, start_ref, conv_ref):
    order = start_ref.shape[0]
    _, skip, _, decay, weight = mode_rows(param_ref)
    decay = [wide(decay[r : r + 1, :]) for r in range(order)]
    weight = [wide(weight[r : r + 1, :]) for r in range(order)]
    skip = wide(skip)

    def body(at, states):
        for inner in range(UNROLL):
            step = at * UNROLL + inner
            signal = signal_ref[first + step]
            states = [a * h + signal for a, h in zip(decay, states)]
            conv_ref[step] = added([w * h for w, h in zip(weight, states)] + [skip * signal])
        return tuple(states)

    states = tuple(start_ref[r] for r in range(order))
    return lax.fori_loop(0, conv_ref.shape[0] // UNROLL, body, states)


def local_kernel(param_ref, signal_ref, start_ref, conv_ref, next_ref):
    states = local_steps(0, param_ref, signal_ref, start_ref, conv_ref)
    for r, state in enumerate(states):
        next_ref[r] = state


def local_query_kernel(stream_hbm, param_ref, signal_ref, start_ref, conv_ref, query_ref, raw_ref, wide_ref, sem):
    copy = pltpu.make_async_copy(stream_hbm.at[0], raw_ref, sem)
    copy.start()
    blocks, steps, _ = raw_ref.shape
    local_steps(conv_ref.shape[0], param_ref, signal_ref, start_ref, conv_ref)
    copy.wait()
    widen(raw_ref, wide_ref, 0, steps)
    lead_in(raw_ref.at[:, pl.ds(steps - 16, 16)], wide_ref, steps)
    taps = [wide(mode_rows(param_ref)[0](j, 0)) for j in range(3)]

    def body(at, carried):
        q2, q1 = carried
        for inner in range(UNROLL):
            step = at * UNROLL + inner
            q0 = row_of(wide_ref, step, steps)
            query_ref[step] = taps[0] * q2 + taps[1] * q1 + taps[2] * q0
            q2, q1 = q1, q0
        return q2, q1

    lax.fori_loop(0, steps // UNROLL, body, (row_of(wide_ref, -2, steps), row_of(wide_ref, -1, steps)))


def pack_kernel(*refs):
    *parts, out_ref = refs
    at = 0
    for part in parts:
        count = 1 if len(part.shape) == 2 else part.shape[0]
        out_ref[at : at + count] = part[...].reshape(count, *out_ref.shape[1:])
        at += count


def gate_kernel(param_ref, query_ref, conv0_ref, conv1_ref, *rest):
    *own_refs, other_ref, out_ref, nat_ref, ends_ref = rest
    rows, chans = out_ref.shape
    steps = rows // SUB
    core = lax.axis_index("core")
    for at, (back, own_ref) in enumerate(zip(BACK, own_refs)):
        pair = 2 * (len(own_refs) - 1 - back)
        ends_ref[pair + core] = own_ref[...]
        ends_ref[pair + 1 - core] = other_ref[at]
    taps, skip, rate, decay, weight = mode_rows(param_ref)
    order = rate.shape[0]
    tap = [[taps(j, s) for s in range(3)] for j in range(3)]

    def head_feat(at, s):
        head, tail = order + 2 * s, order + 6 + 2 * s
        x0, x1 = ends_ref[at, head : head + 1, :], ends_ref[at, head + 1 : head + 2, :]
        if isinstance(at, int) and at == 0:
            m2 = m1 = jnp.zeros_like(x0)
        else:
            m2, m1 = ends_ref[at - 1, tail : tail + 1, :], ends_ref[at - 1, tail + 1 : tail + 2, :]
        first = tap[0][s] * m2 + tap[1][s] * m1 + tap[2][s] * x0
        second = tap[0][s] * m1 + tap[1][s] * x0 + tap[2][s] * x1
        return first, second

    whole = jnp.exp(-rate * rows)
    lead0 = jnp.exp(-rate * (rows - 1))
    lead1 = jnp.exp(-rate * (rows - 2))
    running = jnp.zeros((order, chans), jnp.float32)
    last = ends_ref.shape[0]
    for at in range(last):
        k0, k1 = head_feat(at, 1)
        v0, v1 = head_feat(at, 2)
        h0, h1 = head_feat(at, 0)
        now = (running, k0 * v0, k1 * v1, h0, h1)
        if at == last - 2:
            state, s0, s1, q0, q1 = now
        elif at == last - 1:
            state, s0, s1, q0, q1 = [
                jnp.where(core == 1, new, old) for new, old in zip(now, (state, s0, s1, q0, q1))
            ]
        running = whole * running + ends_ref[at, 0:order, :] + lead0 * now[1] + lead1 * now[2]
    at0 = decay * state + s0
    at1 = decay * at0 + s1
    conv0 = jnp.sum(weight * at0, axis=0, keepdims=True) + skip * s0
    conv1 = jnp.sum(weight * at1, axis=0, keepdims=True) + skip * s1

    block = lax.broadcasted_iota(jnp.int32, (SUB, chans), 0).astype(jnp.float32)
    begin = weight * at1
    decays = [wide(decay[r : r + 1, :]) for r in range(order)]
    terms = [
        wide(begin[r : r + 1, :]) * jnp.exp(-wide(rate[r : r + 1, :]) * (block * steps - 1.0))
        for r in range(order)
    ]

    terms = tuple(terms)
    for which, conv_ref in enumerate((conv0_ref, conv1_ref)):
        count = conv_ref.shape[0]

        def body(at, terms):
            for inner in range(UNROLL):
                local = at * UNROLL + inner
                step = which * count + local
                conv = added([conv_ref[local], *terms])
                nat_ref[pl.ds(step, SUB, stride=steps), :] = query_ref[step] * conv
                terms = [p * a for p, a in zip(terms, decays)]
            return tuple(terms)

        terms = lax.fori_loop(0, count // UNROLL, body, terms)
    nat_ref[0:1, :] = q0 * conv0
    nat_ref[1:2, :] = q1 * conv1
    tile = 128
    for at in range(0, rows, tile):
        out_ref[at : at + tile, :] = nat_ref[at : at + tile, :].astype(jnp.bfloat16)


def pick_kernel(by_owner_ref, near, far):
    peer = peers()
    count = far.shape[0]
    near[...] = by_owner_ref[:, peer[1]]
    far[...] = by_owner_ref[pl.ds(lax.axis_index("core") * count, count), peer[2]]


def weight_kernel(by_owner_ref, near, next_near, far, next_far, weight):
    count, _, depth, _ = by_owner_ref.shape
    half = far.shape[0]
    here, core = lax.axis_index("y"), lax.axis_index("core")
    for j in range(count):
        source = lax.rem(lax.axis_index("z") - j + count, count)
        within = lax.rem(source, half)
        mine = core * half <= source
        mine = mine & (source < core * half + half)
        far_block = jnp.where(mine, far[within], next_far[within])
        rows = slice(j * depth, (j + 1) * depth)
        for s, block in enumerate((by_owner_ref[source, here], far_block, near[source], next_near[source])):
            weight[rows, s * depth : (s + 1) * depth] = block


def project_kernel(here, f1, f2, f3, f4, b1, b2, b3, b4, weight, own, *sent):
    rows, depth = here.shape
    for start in range(0, rows, ROW_TILE):
        span = slice(start, start + ROW_TILE)
        near = [piece[span, :] for piece in (here, f1, f2, f3, b3, b2, b1)]
        half = rows // 2
        far = f4[span, :] if start < half else b4[start - half : start - half + ROW_TILE, :]
        left = jnp.concatenate([*near[:4], far, *near[4:]], axis=1)
        total = jnp.dot(left, weight[...], preferred_element_type=jnp.float32)
        own[span, :] = total[:, 0:depth]
        for s, part in enumerate(sent):
            part[span, :] = total[:, (s + 1) * depth : (s + 2) * depth].astype(jnp.bfloat16)


def finish_kernel(*refs):
    *parts, out = refs
    count = len(parts) // 2
    rows = parts[0].shape[0]
    tile = 128
    for piece in range(2):
        for at in range(0, rows, tile):
            total = parts[piece * count][at : at + tile, :]
            for part in parts[piece * count + 1 : (piece + 1) * count]:
                total = total + part[at : at + tile, :].astype(jnp.float32)
            out[piece * rows + at : piece * rows + at + tile, :] = total.astype(jnp.bfloat16)


def call(kernel, shapes, scratch, flops, args, name, limit=VMEM_LIMIT, **more):
    arrays = [*args, *jax.tree.leaves(shapes, is_leaf=lambda s: hasattr(s, "dtype"))]
    size = sum(math.prod(a.shape) * jnp.dtype(a.dtype).itemsize for a in arrays)
    return pl.pallas_call(
        kernel,
        out_shape=shapes,
        scratch_shapes=scratch,
        compiler_params=pltpu.CompilerParams(vmem_limit_bytes=limit),
        cost_estimate=pl.CostEstimate(flops=flops, bytes_accessed=size, transcendentals=0),
        name=name,
        **more,
    )(*args)


def shards(streams, short_filter, residue, decay_rate, skip_gain, out_weight):
    f32, bf16 = jnp.float32, jnp.bfloat16
    rows, _, chans = streams.shape
    order = residue.shape[0]
    steps = rows // SUB
    z_size, y_size = lax.axis_size("z"), lax.axis_size("y")
    shape = jax.ShapeDtypeStruct

    vmem = pl.BlockSpec(memory_space=pltpu.VMEM)
    def in_hbm(value):
        return pltpu.with_memory_space_constraint(value, pltpu.HBM)

    hbm = pl.BlockSpec(memory_space=pltpu.HBM)
    planes = in_hbm(jnp.transpose(streams, (1, 0, 2)).reshape(3, SUB, steps, chans))
    padded = pltpu.VMEM((SUB * (steps + PAD), chans), f32)
    modes = [in_hbm(m) for m in (short_filter, decay_rate, residue, skip_gain[None, :])]
    signal, start, packed, params = call(
        state_kernel,
        (
            pltpu.VMEM((steps, SUB, chans), f32),
            pltpu.VMEM((order, SUB, chans), f32),
            pltpu.VMEM((order + 16, chans), f32),
            pltpu.VMEM((16 + 3 * order, chans), f32),
        ),
        [
            pltpu.VMEM((2, SUB, steps, chans), bf16),
            pltpu.VMEM((2, SUB, 16, chans), bf16),
            pltpu.VMEM((2, 16, chans), bf16),
            *[pltpu.VMEM(m.shape, f32) for m in modes],
            padded,
            padded,
            pltpu.SemaphoreType.DMA((7 + LOADS,)),
        ],
        rows * chans * 44,
        (planes, *modes),
        "states",
        in_specs=[hbm] * 5,
        out_specs=(vmem,) * 4,
    )
    half_steps = pltpu.VMEM((steps // 2, SUB, chans), f32)
    past = {back: from_behind(packed, "x", back) for back in BACK[1:]}
    conv0, middle = call(
        local_kernel,
        (half_steps, pltpu.VMEM((order, SUB, chans), f32)),
        [],
        rows * chans * 33,
        (params, signal, start),
        "local_conv",
        in_specs=[vmem] * 3,
        out_specs=(vmem,) * 2,
    )
    conv1, query = call(
        local_query_kernel,
        (half_steps, pltpu.VMEM((steps, SUB, chans), f32)),
        [pltpu.VMEM((SUB, steps, chans), bf16), padded, pltpu.SemaphoreType.DMA],
        rows * chans * 40,
        (planes, params, signal, middle),
        "local_conv_query",
        in_specs=[hbm] + [vmem] * 3,
        out_specs=(vmem,) * 2,
    )
    own_ends, _ = lax.optimization_barrier(((packed, *[past[back] for back in BACK[1:]]), conv1))
    ends = call(
        pack_kernel, shape((len(own_ends), *packed.shape), f32), [], 4 * packed.size, own_ends, "pack"
    )
    other_ends = shifted(ends, "core", 1)
    gated = call(
        gate_kernel,
        shape((rows, chans), bf16),
        [pltpu.VMEM((rows, chans), f32), pltpu.VMEM((8, *packed.shape), f32)],
        rows * chans * 34,
        (params, query, conv0, conv1, *own_ends, other_ends),
        "gate",
        in_specs=[vmem] * 9,
        out_specs=vmem,
    )

    by_owner = out_weight.reshape(z_size, y_size, chans, chans)
    near, far = call(
        pick_kernel,
        (shape((z_size, chans, chans), bf16), shape((z_size // 2, chans, chans), bf16)),
        [],
        out_weight.size,
        (lax.optimization_barrier((by_owner, gated))[0],),
        "pick",
    )

    def after(value, *ties):
        return lax.optimization_barrier((value, *ties))[0]

    def hop(piece, *ties, last=False):
        up, down = piece
        front, back, *_ = lax.optimization_barrier((up[-1], down[-1], *ties))
        if last:
            front, back = front[: HALF // 2], back[HALF // 2 :]
        up.append(shifted(front, "z", 1))
        down.append(shifted(back, "z", -1))

    a, b = [([gated[lo : lo + HALF]], [gated[lo : lo + HALF]]) for lo in (0, HALF)]
    hop(a)
    hop(b)
    hop(a)
    far = swapped(far, 2)
    hop(b)
    near = swapped(near, 1)
    hop(a, far)
    next_far = shifted(far, "core", 1)
    hop(b, near)
    next_near = shifted(near, "core", 1)
    hop(a, next_far, last=True)
    weight = call(
        weight_kernel,
        shape((z_size * chans, y_size * chans), bf16),
        [],
        out_weight.size,
        (by_owner, near, next_near, far, next_far),
        "weights",
    )
    hop(b, weight, last=True)

    def project(piece, *ties):
        own, *sent = call(
            project_kernel,
            (shape((HALF, chans), f32),) + (shape((HALF, chans), bf16),) * 3,
            [],
            2 * HALF * z_size * y_size * chans * chans,
            (*piece[0], *piece[1][1:], lax.optimization_barrier((weight, *ties))[0]),
            "project",
        )
        return own, *[swapped(part, kind) for part, kind in zip(sent, KINDS)]

    return call(
        finish_kernel,
        shape((rows, chans), bf16),
        [],
        rows * chans,
        (*project(a, b[1][3]), *project(b)),
        "finish",
    )


def solution(mesh):
    ctx_size, tp_size = mesh.devices.shape
    fine = Mesh(mesh.devices.reshape(ctx_size // 2, 2, tp_size // 4, 4), ("x", "core", "z", "y"))
    tp = ("z", "y")
    in_specs = (
        P(CTX, None, tp),
        P(None, None, tp),
        P(None, tp),
        P(None, tp),
        P(tp),
        P(None, tp),
    )
    return jax.shard_map(shards, mesh=fine, in_specs=in_specs, out_specs=P(CTX, tp), check_vma=False)
```

time: 95.1 us -> 90.3 us (0.950)
  the two profiles are of different devices: /device:TPU:8 before, /device:TPU:2 now
where the time goes in v3:
time: 90.3 us; the launch traced here: 89 us
  starting transfers between devices  50 us (55%)
  waiting for transfers between devices  27.3 us (30%)
  Pallas kernels  11.3 us (13%)
    ppermute x19, starting transfers between devices, shifted(): lax.ppermute(value, axis, [(at, (at + steps) % count) for at in range(cou...  30.2 us
    ppermute x19, waiting for transfers between devices, shifted(): lax.ppermute(value, axis, [(at, (at + steps) % count) for at in range(cou...  15.7 us
    ppermute x8, starting transfers between devices, swapped(): return lax.ppermute(value, ('core', 'y'), pairs)  13.2 us
    ppermute x8, waiting for transfers between devices, swapped(): return lax.ppermute(value, ('core', 'y'), pairs)  11.4 us
    pallas_call x10, Pallas kernels, call(): pl.pallas_call(kernel, out_shape=shapes, scratch_shapes=scratch, compiler...  11.3 us
    ppermute x3, starting transfers between devices, from_behind(): lax.ppermute(value, axis, [(at, at + steps) for at in range(count - steps)])  6.61 us
  transfers between devices with their start and end apart: 30, of which 16 were waited for; matrix products, arithmetic and copies ran while one was open for 0% of the time, Pallas kernels for 6%

profile of v3, /device:TPU:2, one launch (start us, length us, event | category | flops | bytes accessed | tf_op | source)
XLA Modules:
  0.0 89.0 jit_solution(9502311375706689954)
XLA Ops:
  0.0 3.3 %states.1 = (f32[256,8,128]{2,1,0:T(8,128)S(1)}, f32[16,8,128]{2,1,0:T(8,128)S(1)}, f32[32,128]{1,0:T(8,128)S(1)}, f32[64,128]{1,0:T(8,128)S(1)}) custom-call(bf16[3,8,256,128]{3,2,1,0:T(8,128)(2,1)} %bitcast.7, f32[3,3,128]{2,1,0:T(4,128)} %taps_hbm.1, f32[16,128]{1,0:T(8,128)} %rate_hbm.1, f32[16,128]{1,0:T(8,128)} %residue_hbm.1, f32[1,128]{1,0:T(1,128)} %bitcast.9), custom_call_target="tpu_custom_call" | custom-call | flops 11534336 | bytes 2757632 | tf_op jit(solution)/shard_map/states/pallas_call | solution.py:363
  3.3 4.0 %collective-permute-start = (f32[32,128]{1,0:T(8,128)S(1)}, f32[32,128]{1,0:T(8,128)S(1)}, u32[]{:S(2)}, u32[]{:S(2)}) collective-permute-start(f32[32,128]{1,0:T(8,128)S(1)} %get-tuple-element.53.refs_0_.rest_0_), channel_id=1, source_target_pairs={{0,128},{64,192},{1,129},{65,193},{2,130},{66,194},{3,131},{67,195... | collective-permute-start | bytes 49160 | tf_op jit(solution)/shard_map/ppermute | solution.py:43
  7.3 1.9 %collective-permute-start.1 = (f32[32,128]{1,0:T(8,128)S(1)}, f32[32,128]{1,0:T(8,128)S(1)}, u32[]{:S(2)}, u32[]{:S(2)}) collective-permute-start(f32[32,128]{1,0:T(8,128)S(1)} %get-tuple-element.53.refs_0_.rest_0_), channel_id=1, source_target_pairs={{0,64},{64,128},{128,192},{1,65},{65,129},{129,193},{2,66},{66,130... | collective-permute-start | bytes 49160 | tf_op jit(solution)/shard_map/ppermute | solution.py:43
  11.1 1.6 %local_conv_query.1 = (f32[128,8,128]{2,1,0:T(8,128)S(1)}, f32[256,8,128]{2,1,0:T(8,128)S(1)}) custom-call(bf16[3,8,256,128]{3,2,1,0:T(8,128)(2,1)} %bitcast.8, f32[64,128]{1,0:T(8,128)S(1)} %get-tuple-element.45.param_ref, f32[256,8,128]{2,1,0:T(8,128)S(1)} %get-tuple-element.46.signal_ref, f32[16,8,128]{2,1,0:T(8,128)S(1)} %get-tuple-element.48.start_ref), custom_call_target="tpu_custom_call" | custom-call | flops 10485760 | bytes 4292608 | tf_op jit(solution)/shard_map/local_conv_query/pallas_call | solution.py:363
  15.9 2.0 %collective-permute-start.16 = (bf16[1024,128]{1,0:T(8,128)(2,1)S(1)}, bf16[1024,128]{1,0:T(8,128)(2,1)S(1)}, u32[]{:S(2)}, u32[]{:S(2)}) collective-permute-start(bf16[1024,128]{1,0:T(8,128)(2,1)S(1)} %get-tuple-element.69.here), channel_id=1, source_target_pairs={{0,4},{4,8},{8,12},{12,16},{16,20},{20,24},{24,28},{28,0},{1,5},{5... | collective-permute-start | bytes 786440 | tf_op jit(solution)/shard_map/ppermute | solution.py:24
  17.9 4.0 %collective-permute-start.17 = (bf16[1024,128]{1,0:T(8,128)(2,1)S(1)}, bf16[1024,128]{1,0:T(8,128)(2,1)S(1)}, u32[]{:S(2)}, u32[]{:S(2)}) collective-permute-start(bf16[1024,128]{1,0:T(8,128)(2,1)S(1)} %get-tuple-element.69.here), channel_id=1, source_target_pairs={{0,28},{4,0},{8,4},{12,8},{16,12},{20,16},{24,20},{28,24},{1,29},{... | collective-permute-start | bytes 786440 | tf_op jit(solution)/shard_map/ppermute | solution.py:24
  21.9 3.2 %collective-permute-start.5 = (bf16[1024,128]{1,0:T(8,128)(2,1)S(1)}, bf16[1024,128]{1,0:T(8,128)(2,1)S(1)}, u32[]{:S(2)}, u32[]{:S(2)}) collective-permute-start(bf16[1024,128]{1,0:T(8,128)(2,1)S(1)} %get-tuple-element.58.here), channel_id=1, source_target_pairs={{0,28},{4,0},{8,4},{12,8},{16,12},{20,16},{24,20},{28,24},{1,29},{... | collective-permute-start | bytes 786440 | tf_op jit(solution)/shard_map/ppermute | solution.py:24
  25.1 1.7 %collective-permute-start.14 = (bf16[8,128,128]{2,1,0:T(8,128)(2,1)S(1)}, bf16[8,128,128]{2,1,0:T(8,128)(2,1)S(1)}, u32[]{:S(2)}, u32[]{:S(2)}) collective-permute-start(bf16[8,128,128]{2,1,0:T(8,128)(2,1)S(1)} %get-tuple-element.67), channel_id=1, source_target_pairs={{0,1},{1,0},{2,3},{3,2},{32,35},{33,34},{34,33},{35,32},{4,5},{5,4... | collective-permute-start | bytes 786440 | tf_op jit(solution)/shard_map/ppermute | solution.py:33
  26.8 2.1 %collective-permute-done.16.f1 = bf16[1024,128]{1,0:T(8,128)(2,1)S(1)} collective-permute-done((bf16[1024,128]{1,0:T(8,128)(2,1)S(1)}, bf16[1024,128]{1,0:T(8,128)(2,1)S(1)}, u32[]{:S(2)}, u32[]{:S(2)}) %collective-permute-start.16) | collective-permute-done | bytes 262176 | tf_op jit(solution)/shard_map/ppermute | solution.py:24
  28.9 3.3 %collective-permute-start.19 = (bf16[1024,128]{1,0:T(8,128)(2,1)S(1)}, bf16[1024,128]{1,0:T(8,128)(2,1)S(1)}, u32[]{:S(2)}, u32[]{:S(2)}) collective-permute-start(bf16[1024,128]{1,0:T(8,128)(2,1)S(1)} %collective-permute-done.17.b1), channel_id=1, source_target_pairs={{0,28},{4,0},{8,4},{12,8},{16,12},{20,16},{24,20},{28,24},{1,29},{... | collective-permute-start | bytes 786440 | tf_op jit(solution)/shard_map/ppermute | solution.py:24
  32.2 2.3 %collective-permute-done.4.f1 = bf16[1024,128]{1,0:T(8,128)(2,1)S(1)} collective-permute-done((bf16[1024,128]{1,0:T(8,128)(2,1)S(1)}, bf16[1024,128]{1,0:T(8,128)(2,1)S(1)}, u32[]{:S(2)}, u32[]{:S(2)}) %collective-permute-start.4) | collective-permute-done | bytes 262176 | tf_op jit(solution)/shard_map/ppermute | solution.py:24
  34.5 3.2 %collective-permute-start.8 = (bf16[4,128,128]{2,1,0:T(8,128)(2,1)S(1)}, bf16[4,128,128]{2,1,0:T(8,128)(2,1)S(1)}, u32[]{:S(2)}, u32[]{:S(2)}) collective-permute-start(bf16[4,128,128]{2,1,0:T(8,128)(2,1)S(1)} %get-tuple-element.62), channel_id=1, source_target_pairs={{0,2},{1,3},{2,0},{3,1},{32,34},{33,35},{34,32},{35,33},{4,6},{5,7... | collective-permute-start | bytes 393224 | tf_op jit(solution)/shard_map/ppermute | solution.py:33
  37.7 3.4 %collective-permute-start.7 = (bf16[1024,128]{1,0:T(8,128)(2,1)S(1)}, bf16[1024,128]{1,0:T(8,128)(2,1)S(1)}, u32[]{:S(2)}, u32[]{:S(2)}) collective-permute-start(bf16[1024,128]{1,0:T(8,128)(2,1)S(1)} %collective-permute-done.5.b1), channel_id=1, source_target_pairs={{0,28},{4,0},{8,4},{12,8},{16,12},{20,16},{24,20},{28,24},{1,29},{... | collective-permute-start | bytes 786440 | tf_op jit(solution)/shard_map/ppermute | solution.py:24
  41.1 2.1 %collective-permute-start.20 = (bf16[1024,128]{1,0:T(8,128)(2,1)S(1)}, bf16[1024,128]{1,0:T(8,128)(2,1)S(1)}, u32[]{:S(2)}, u32[]{:S(2)}) collective-permute-start(bf16[1024,128]{1,0:T(8,128)(2,1)S(1)} %collective-permute-done.19.b2), channel_id=1, source_target_pairs={{0,28},{4,0},{8,4},{12,8},{16,12},{20,16},{24,20},{28,24},{1,29},{... | collective-permute-start | bytes 786440 | tf_op jit(solution)/shard_map/ppermute | solution.py:24
  45.3 1.5 %collective-permute-done.7.b2 = bf16[1024,128]{1,0:T(8,128)(2,1)S(1)} collective-permute-done((bf16[1024,128]{1,0:T(8,128)(2,1)S(1)}, bf16[1024,128]{1,0:T(8,128)(2,1)S(1)}, u32[]{:S(2)}, u32[]{:S(2)}) %collective-permute-start.7) | collective-permute-done | bytes 262176 | tf_op jit(solution)/shard_map/ppermute | solution.py:24
  46.8 3.7 %collective-permute-start.10 = (bf16[1024,128]{1,0:T(8,128)(2,1)S(1)}, bf16[1024,128]{1,0:T(8,128)(2,1)S(1)}, u32[]{:S(2)}, u32[]{:S(2)}) collective-permute-start(bf16[1024,128]{1,0:T(8,128)(2,1)S(1)} %collective-permute-done.7.b2), channel_id=1, source_target_pairs={{0,28},{4,0},{8,4},{12,8},{16,12},{20,16},{24,20},{28,24},{1,29},{... | collective-permute-start | bytes 786440 | tf_op jit(solution)/shard_map/ppermute | solution.py:24
  53.5 3.3 %collective-permute-start.25 = (bf16[512,128]{1,0:T(8,128)(2,1)S(1)}, bf16[512,128]{1,0:T(8,128)(2,1)S(1)}, u32[]{:S(2)}, u32[]{:S(2)}) collective-permute-start(bf16[512,128]{1,0:T(8,128)(2,1)S(1)} %slice.24), channel_id=1, source_target_pairs={{0,4},{4,8},{8,12},{12,16},{16,20},{20,24},{24,28},{28,0},{1,5},{5... | collective-permute-start | bytes 393224 | tf_op jit(solution)/shard_map/ppermute | solution.py:24
  56.9 4.2 %collective-permute-done.25.f4 = bf16[512,128]{1,0:T(8,128)(2,1)S(1)} collective-permute-done((bf16[512,128]{1,0:T(8,128)(2,1)S(1)}, bf16[512,128]{1,0:T(8,128)(2,1)S(1)}, u32[]{:S(2)}, u32[]{:S(2)}) %collective-permute-start.25) | collective-permute-done | bytes 131104 | tf_op jit(solution)/shard_map/ppermute | solution.py:24
  63.1 1.7 %collective-permute-start.27 = (bf16[1024,128]{1,0:T(8,128)(2,1)S(1)}, bf16[1024,128]{1,0:T(8,128)(2,1)S(1)}, u32[]{:S(2)}, u32[]{:S(2)}) collective-permute-start(bf16[1024,128]{1,0:T(8,128)(2,1)S(1)} %get-tuple-element.82), channel_id=1, source_target_pairs={{0,2},{1,3},{2,0},{3,1},{32,34},{33,35},{34,32},{35,33},{4,6},{5,7... | collective-permute-start | bytes 786440 | tf_op jit(solution)/shard_map/ppermute | solution.py:33
  65.8 2.4 %collective-permute-start.13 = (bf16[512,128]{1,0:T(8,128)(2,1)S(1)}, bf16[512,128]{1,0:T(8,128)(2,1)S(1)}, u32[]{:S(2)}, u32[]{:S(2)}) collective-permute-start(bf16[512,128]{1,0:T(8,128)(2,1)S(1)} %slice.22), channel_id=1, source_target_pairs={{0,28},{4,0},{8,4},{12,8},{16,12},{20,16},{24,20},{28,24},{1,29},{... | collective-permute-start | bytes 393224 | tf_op jit(solution)/shard_map/ppermute | solution.py:24
  68.9 1.8 %collective-permute-start.29 = (bf16[1024,128]{1,0:T(8,128)(2,1)S(1)}, bf16[1024,128]{1,0:T(8,128)(2,1)S(1)}, u32[]{:S(2)}, u32[]{:S(2)}) collective-permute-start(bf16[1024,128]{1,0:T(8,128)(2,1)S(1)} %get-tuple-element.84), channel_id=1, source_target_pairs={{0,3},{1,2},{2,1},{3,0},{32,33},{33,32},{34,35},{35,34},{4,7},{5,6... | collective-permute-start | bytes 786440 | tf_op jit(solution)/shard_map/ppermute | solution.py:33
  72.3 2.8 %collective-permute-start.21 = (bf16[1024,128]{1,0:T(8,128)(2,1)S(1)}, bf16[1024,128]{1,0:T(8,128)(2,1)S(1)}, u32[]{:S(2)}, u32[]{:S(2)}) collective-permute-start(bf16[1024,128]{1,0:T(8,128)(2,1)S(1)} %get-tuple-element.75), channel_id=1, source_target_pairs={{0,2},{1,3},{2,0},{3,1},{32,34},{33,35},{34,32},{35,33},{4,6},{5,7... | collective-permute-start | bytes 786440 | tf_op jit(solution)/shard_map/ppermute | solution.py:33
  77.5 6.6 %collective-permute-done.29.refs_7_ = bf16[1024,128]{1,0:T(8,128)(2,1)S(1)} collective-permute-done((bf16[1024,128]{1,0:T(8,128)(2,1)S(1)}, bf16[1024,128]{1,0:T(8,128)(2,1)S(1)}, u32[]{:S(2)}, u32[]{:S(2)}) %collective-permute-start.29) | collective-permute-done | bytes 262176 | tf_op jit(solution)/shard_map/ppermute | solution.py:33
  84.2 2.5 %collective-permute-done.22.refs_2_ = bf16[1024,128]{1,0:T(8,128)(2,1)S(1)} collective-permute-done((bf16[1024,128]{1,0:T(8,128)(2,1)S(1)}, bf16[1024,128]{1,0:T(8,128)(2,1)S(1)}, u32[]{:S(2)}, u32[]{:S(2)}) %collective-permute-start.22) | collective-permute-done | bytes 262176 | tf_op jit(solution)/shard_map/ppermute | solution.py:33
  (53 shorter events, 20.3 us)
Async XLA Ops:
  3.3 9.5 %collective-permute-start = (f32[32,128]{1,0:T(8,128)S(1)}, f32[32,128]{1,0:T(8,128)S(1)}, u32[]{:S(2)}, u32[]{:S(2)}) collective-permute-start(f32[32,128]{1,0:T(8,128)S(1)} %get-tuple-element.53.refs_0_.rest_0_), channel_id=1, source_target_pairs={{0,128},{64,192},{1,129},{65,193},{2,130},{66,194},{3,131},{67,195... | collective-permute-start | bytes 49160 | tf_op jit(solution)/shard_map/ppermute | solution.py:43
  15.9 13.0 %collective-permute-start.16 = (bf16[1024,128]{1,0:T(8,128)(2,1)S(1)}, bf16[1024,128]{1,0:T(8,128)(2,1)S(1)}, u32[]{:S(2)}, u32[]{:S(2)}) collective-permute-start(bf16[1024,128]{1,0:T(8,128)(2,1)S(1)} %get-tuple-element.69.here), channel_id=1, source_target_pairs={{0,4},{4,8},{8,12},{12,16},{16,20},{20,24},{24,28},{28,0},{1,5},{5... | collective-permute-start | bytes 786440 | tf_op jit(solution)/shard_map/ppermute | solution.py:24
  17.9 11.0 %collective-permute-start.17 = (bf16[1024,128]{1,0:T(8,128)(2,1)S(1)}, bf16[1024,128]{1,0:T(8,128)(2,1)S(1)}, u32[]{:S(2)}, u32[]{:S(2)}) collective-permute-start(bf16[1024,128]{1,0:T(8,128)(2,1)S(1)} %get-tuple-element.69.here), channel_id=1, source_target_pairs={{0,28},{4,0},{8,4},{12,8},{16,12},{20,16},{24,20},{28,24},{1,29},{... | collective-permute-start | bytes 786440 | tf_op jit(solution)/shard_map/ppermute | solution.py:24
  21.9 12.6 %collective-permute-start.4 = (bf16[1024,128]{1,0:T(8,128)(2,1)S(1)}, bf16[1024,128]{1,0:T(8,128)(2,1)S(1)}, u32[]{:S(2)}, u32[]{:S(2)}) collective-permute-start(bf16[1024,128]{1,0:T(8,128)(2,1)S(1)} %get-tuple-element.58.here), channel_id=1, source_target_pairs={{0,4},{4,8},{8,12},{12,16},{16,20},{20,24},{24,28},{28,0},{1,5},{5... | collective-permute-start | bytes 786440 | tf_op jit(solution)/shard_map/ppermute | solution.py:24
  21.9 12.6 %collective-permute-start.5 = (bf16[1024,128]{1,0:T(8,128)(2,1)S(1)}, bf16[1024,128]{1,0:T(8,128)(2,1)S(1)}, u32[]{:S(2)}, u32[]{:S(2)}) collective-permute-start(bf16[1024,128]{1,0:T(8,128)(2,1)S(1)} %get-tuple-element.58.here), channel_id=1, source_target_pairs={{0,28},{4,0},{8,4},{12,8},{16,12},{20,16},{24,20},{28,24},{1,29},{... | collective-permute-start | bytes 786440 | tf_op jit(solution)/shard_map/ppermute | solution.py:24
  25.1 12.6 %collective-permute-start.14 = (bf16[8,128,128]{2,1,0:T(8,128)(2,1)S(1)}, bf16[8,128,128]{2,1,0:T(8,128)(2,1)S(1)}, u32[]{:S(2)}, u32[]{:S(2)}) collective-permute-start(bf16[8,128,128]{2,1,0:T(8,128)(2,1)S(1)} %get-tuple-element.67), channel_id=1, source_target_pairs={{0,1},{1,0},{2,3},{3,2},{32,35},{33,34},{34,33},{35,32},{4,5},{5,4... | collective-permute-start | bytes 786440 | tf_op jit(solution)/shard_map/ppermute | solution.py:33
  28.9 12.2 %collective-permute-start.18 = (bf16[1024,128]{1,0:T(8,128)(2,1)S(1)}, bf16[1024,128]{1,0:T(8,128)(2,1)S(1)}, u32[]{:S(2)}, u32[]{:S(2)}) collective-permute-start(bf16[1024,128]{1,0:T(8,128)(2,1)S(1)} %collective-permute-done.16.f1), channel_id=1, source_target_pairs={{0,4},{4,8},{8,12},{12,16},{16,20},{20,24},{24,28},{28,0},{1,5},{5... | collective-permute-start | bytes 786440 | tf_op jit(solution)/shard_map/ppermute | solution.py:24
  28.9 12.1 %collective-permute-start.19 = (bf16[1024,128]{1,0:T(8,128)(2,1)S(1)}, bf16[1024,128]{1,0:T(8,128)(2,1)S(1)}, u32[]{:S(2)}, u32[]{:S(2)}) collective-permute-start(bf16[1024,128]{1,0:T(8,128)(2,1)S(1)} %collective-permute-done.17.b1), channel_id=1, source_target_pairs={{0,28},{4,0},{8,4},{12,8},{16,12},{20,16},{24,20},{28,24},{1,29},{... | collective-permute-start | bytes 786440 | tf_op jit(solution)/shard_map/ppermute | solution.py:24
  34.5 10.8 %collective-permute-start.6 = (bf16[1024,128]{1,0:T(8,128)(2,1)S(1)}, bf16[1024,128]{1,0:T(8,128)(2,1)S(1)}, u32[]{:S(2)}, u32[]{:S(2)}) collective-permute-start(bf16[1024,128]{1,0:T(8,128)(2,1)S(1)} %collective-permute-done.4.f1), channel_id=1, source_target_pairs={{0,4},{4,8},{8,12},{12,16},{16,20},{20,24},{24,28},{28,0},{1,5},{5... | collective-permute-start | bytes 786440 | tf_op jit(solution)/shard_map/ppermute | solution.py:24
  34.5 8.7 %collective-permute-start.8 = (bf16[4,128,128]{2,1,0:T(8,128)(2,1)S(1)}, bf16[4,128,128]{2,1,0:T(8,128)(2,1)S(1)}, u32[]{:S(2)}, u32[]{:S(2)}) collective-permute-start(bf16[4,128,128]{2,1,0:T(8,128)(2,1)S(1)} %get-tuple-element.62), channel_id=1, source_target_pairs={{0,2},{1,3},{2,0},{3,1},{32,34},{33,35},{34,32},{35,33},{4,6},{5,7... | collective-permute-start | bytes 393224 | tf_op jit(solution)/shard_map/ppermute | solution.py:33
  37.7 9.1 %collective-permute-start.7 = (bf16[1024,128]{1,0:T(8,128)(2,1)S(1)}, bf16[1024,128]{1,0:T(8,128)(2,1)S(1)}, u32[]{:S(2)}, u32[]{:S(2)}) collective-permute-start(bf16[1024,128]{1,0:T(8,128)(2,1)S(1)} %collective-permute-done.5.b1), channel_id=1, source_target_pairs={{0,28},{4,0},{8,4},{12,8},{16,12},{20,16},{24,20},{28,24},{1,29},{... | collective-permute-start | bytes 786440 | tf_op jit(solution)/shard_map/ppermute | solution.py:24
  41.1 10.1 %collective-permute-start.15 = (bf16[8,128,128]{2,1,0:T(8,128)(2,1)S(1)}, bf16[8,128,128]{2,1,0:T(8,128)(2,1)S(1)}, u32[]{:S(2)}, u32[]{:S(2)}) collective-permute-start(bf16[8,128,128]{2,1,0:T(8,128)(2,1)S(1)} %collective-permute-done.14.near), channel_id=1, source_target_pairs={{0,32},{32,0},{1,33},{33,1},{2,34},{34,2},{3,35},{35,3},{4,36},{36... | collective-permute-start | bytes 786440 | tf_op jit(solution)/shard_map/ppermute | solution.py:24
  41.1 11.3 %collective-permute-start.20 = (bf16[1024,128]{1,0:T(8,128)(2,1)S(1)}, bf16[1024,128]{1,0:T(8,128)(2,1)S(1)}, u32[]{:S(2)}, u32[]{:S(2)}) collective-permute-start(bf16[1024,128]{1,0:T(8,128)(2,1)S(1)} %collective-permute-done.19.b2), channel_id=1, source_target_pairs={{0,28},{4,0},{8,4},{12,8},{16,12},{20,16},{24,20},{28,24},{1,29},{... | collective-permute-start | bytes 786440 | tf_op jit(solution)/shard_map/ppermute | solution.py:24
  43.2 10.4 %collective-permute-start.24 = (bf16[1024,128]{1,0:T(8,128)(2,1)S(1)}, bf16[1024,128]{1,0:T(8,128)(2,1)S(1)}, u32[]{:S(2)}, u32[]{:S(2)}) collective-permute-start(bf16[1024,128]{1,0:T(8,128)(2,1)S(1)} %collective-permute-done.18.f2), channel_id=1, source_target_pairs={{0,4},{4,8},{8,12},{12,16},{16,20},{20,24},{24,28},{28,0},{1,5},{5... | collective-permute-start | bytes 786440 | tf_op jit(solution)/shard_map/ppermute | solution.py:24
  46.8 18.0 %collective-permute-start.10 = (bf16[1024,128]{1,0:T(8,128)(2,1)S(1)}, bf16[1024,128]{1,0:T(8,128)(2,1)S(1)}, u32[]{:S(2)}, u32[]{:S(2)}) collective-permute-start(bf16[1024,128]{1,0:T(8,128)(2,1)S(1)} %collective-permute-done.7.b2), channel_id=1, source_target_pairs={{0,28},{4,0},{8,4},{12,8},{16,12},{20,16},{24,20},{28,24},{1,29},{... | collective-permute-start | bytes 786440 | tf_op jit(solution)/shard_map/ppermute | solution.py:24
  50.5 14.3 %collective-permute-start.9 = (bf16[1024,128]{1,0:T(8,128)(2,1)S(1)}, bf16[1024,128]{1,0:T(8,128)(2,1)S(1)}, u32[]{:S(2)}, u32[]{:S(2)}) collective-permute-start(bf16[1024,128]{1,0:T(8,128)(2,1)S(1)} %collective-permute-done.6.f2), channel_id=1, source_target_pairs={{0,4},{4,8},{8,12},{12,16},{16,20},{20,24},{24,28},{28,0},{1,5},{5... | collective-permute-start | bytes 786440 | tf_op jit(solution)/shard_map/ppermute | solution.py:24
  53.5 7.6 %collective-permute-start.25 = (bf16[512,128]{1,0:T(8,128)(2,1)S(1)}, bf16[512,128]{1,0:T(8,128)(2,1)S(1)}, u32[]{:S(2)}, u32[]{:S(2)}) collective-permute-start(bf16[512,128]{1,0:T(8,128)(2,1)S(1)} %slice.24), channel_id=1, source_target_pairs={{0,4},{4,8},{8,12},{12,16},{16,20},{20,24},{24,28},{28,0},{1,5},{5... | collective-permute-start | bytes 393224 | tf_op jit(solution)/shard_map/ppermute | solution.py:24
  63.1 12.7 %collective-permute-start.27 = (bf16[1024,128]{1,0:T(8,128)(2,1)S(1)}, bf16[1024,128]{1,0:T(8,128)(2,1)S(1)}, u32[]{:S(2)}, u32[]{:S(2)}) collective-permute-start(bf16[1024,128]{1,0:T(8,128)(2,1)S(1)} %get-tuple-element.82), channel_id=1, source_target_pairs={{0,2},{1,3},{2,0},{3,1},{32,34},{33,35},{34,32},{35,33},{4,6},{5,7... | collective-permute-start | bytes 786440 | tf_op jit(solution)/shard_map/ppermute | solution.py:33
  64.8 6.3 %collective-permute-start.12 = (bf16[512,128]{1,0:T(8,128)(2,1)S(1)}, bf16[512,128]{1,0:T(8,128)(2,1)S(1)}, u32[]{:S(2)}, u32[]{:S(2)}) collective-permute-start(bf16[512,128]{1,0:T(8,128)(2,1)S(1)} %slice.21), channel_id=1, source_target_pairs={{0,4},{4,8},{8,12},{12,16},{16,20},{20,24},{24,28},{28,0},{1,5},{5... | collective-permute-start | bytes 393224 | tf_op jit(solution)/shard_map/ppermute | solution.py:24
  68.2 9.2 %collective-permute-start.28 = (bf16[1024,128]{1,0:T(8,128)(2,1)S(1)}, bf16[1024,128]{1,0:T(8,128)(2,1)S(1)}, u32[]{:S(2)}, u32[]{:S(2)}) collective-permute-start(bf16[1024,128]{1,0:T(8,128)(2,1)S(1)} %get-tuple-element.83), channel_id=1, source_target_pairs={{0,1},{1,0},{2,3},{3,2},{32,35},{33,34},{34,33},{35,32},{4,5},{5,4... | collective-permute-start | bytes 786440 | tf_op jit(solution)/shard_map/ppermute | solution.py:33
  68.9 15.2 %collective-permute-start.29 = (bf16[1024,128]{1,0:T(8,128)(2,1)S(1)}, bf16[1024,128]{1,0:T(8,128)(2,1)S(1)}, u32[]{:S(2)}, u32[]{:S(2)}) collective-permute-start(bf16[1024,128]{1,0:T(8,128)(2,1)S(1)} %get-tuple-element.84), channel_id=1, source_target_pairs={{0,3},{1,2},{2,1},{3,0},{32,33},{33,32},{34,35},{35,34},{4,7},{5,6... | collective-permute-start | bytes 786440 | tf_op jit(solution)/shard_map/ppermute | solution.py:33
  72.3 11.9 %collective-permute-start.21 = (bf16[1024,128]{1,0:T(8,128)(2,1)S(1)}, bf16[1024,128]{1,0:T(8,128)(2,1)S(1)}, u32[]{:S(2)}, u32[]{:S(2)}) collective-permute-start(bf16[1024,128]{1,0:T(8,128)(2,1)S(1)} %get-tuple-element.75), channel_id=1, source_target_pairs={{0,2},{1,3},{2,0},{3,1},{32,34},{33,35},{34,32},{35,33},{4,6},{5,7... | collective-permute-start | bytes 786440 | tf_op jit(solution)/shard_map/ppermute | solution.py:33
  75.2 11.5 %collective-permute-start.22 = (bf16[1024,128]{1,0:T(8,128)(2,1)S(1)}, bf16[1024,128]{1,0:T(8,128)(2,1)S(1)}, u32[]{:S(2)}, u32[]{:S(2)}) collective-permute-start(bf16[1024,128]{1,0:T(8,128)(2,1)S(1)} %get-tuple-element.76), channel_id=1, source_target_pairs={{0,1},{1,0},{2,3},{3,2},{32,35},{33,34},{34,33},{35,32},{4,5},{5,4... | collective-permute-start | bytes 786440 | tf_op jit(solution)/shard_map/ppermute | solution.py:33
  75.9 12.1 %collective-permute-start.23 = (bf16[1024,128]{1,0:T(8,128)(2,1)S(1)}, bf16[1024,128]{1,0:T(8,128)(2,1)S(1)}, u32[]{:S(2)}, u32[]{:S(2)}) collective-permute-start(bf16[1024,128]{1,0:T(8,128)(2,1)S(1)} %get-tuple-element.77), channel_id=1, source_target_pairs={{0,3},{1,2},{2,1},{3,0},{32,33},{33,32},{34,35},{35,34},{4,7},{5,6... | collective-permute-start | bytes 786440 | tf_op jit(solution)/shard_map/ppermute | solution.py:33
  (7 other events, 37.0 us)

commit v4 on v3

--- a/solution.py
+++ b/solution.py
@@ -1,3 +1,4 @@
+import functools
 import math
 
 import jax
@@ -14,7 +15,7 @@
 HALF = 1024
 KINDS = (2, 1, 3)
 LOADS = 4
-BACK = (0, 2, 1, 3)
+BACK = (0, 2, 3, 1)
 VMEM_LIMIT = 16 * 1024 * 1024
 ROW_TILE = 256
 
@@ -103,18 +104,16 @@
     small, large = copies[:-LOADS], copies[-LOADS:]
     for copy in small[:3] + large + small[3:]:
         copy.start()
-    for copy in small:
+    for copy in small[:3]:
         copy.wait()
 
     for j in range(3):
         for s in range(3):
             param_ref[3 * j + s : 3 * j + s + 1, :] = taps_ref[j, s : s + 1, :]
-    param_ref[9:10, :] = skip_ref[...]
     param_ref[10:16, :] = jnp.zeros((6, chans), jnp.float32)
     rates = rate_ref[...]
     param_ref[16 : 16 + order, :] = rates
     param_ref[16 + order : 16 + 2 * order, :] = jnp.exp(-rates)
-    param_ref[16 + 2 * order : 16 + 3 * order, :] = residue_ref[...] * jnp.sqrt(2.0 * rates)
     taps, _, _, fade, _ = mode_rows(param_ref)
     lead_in(tail_ref.at[0], key_ref, steps)
     lead_in(tail_ref.at[1], val_ref, steps)
@@ -155,6 +154,10 @@
                 carried = advance(step, carried, step < 2)
             begin = 1
         carried = lax.fori_loop(begin, (at + 1) * part // UNROLL, body, tuple(carried))
+    for copy in small[3:]:
+        copy.wait()
+    param_ref[9:10, :] = skip_ref[...]
+    param_ref[16 + 2 * order : 16 + 3 * order, :] = residue_ref[...] * jnp.sqrt(2.0 * rates)
     states = carried[4:]
     for r in range(order):
         rate = wide(rates[r : r + 1, :])
@@ -344,17 +347,18 @@
             part[span, :] = total[:, (s + 1) * depth : (s + 2) * depth].astype(jnp.bfloat16)
 
 
-def finish_kernel(*refs):
-    *parts, out = refs
-    count = len(parts) // 2
-    rows = parts[0].shape[0]
+def finish_kernel(piece, own, one, two, three, *rest):
+    *_, out_hbm, half_ref, sem = rest
+    rows = own.shape[0]
     tile = 128
-    for piece in range(2):
-        for at in range(0, rows, tile):
-            total = parts[piece * count][at : at + tile, :]
-            for part in parts[piece * count + 1 : (piece + 1) * count]:
-                total = total + part[at : at + tile, :].astype(jnp.float32)
-            out[piece * rows + at : piece * rows + at + tile, :] = total.astype(jnp.bfloat16)
+    for at in range(0, rows, tile):
+        total = own[at : at + tile, :]
+        for part in (one, two, three):
+            total = total + part[at : at + tile, :].astype(jnp.float32)
+        half_ref[at : at + tile, :] = total.astype(jnp.bfloat16)
+    copy = pltpu.make_async_copy(half_ref, out_hbm.at[pl.ds(piece * rows, rows)], sem)
+    copy.start()
+    copy.wait()
 
 
 def call(kernel, shapes, scratch, flops, args, name, limit=VMEM_LIMIT, **more):
@@ -502,14 +506,23 @@
         )
         return own, *[swapped(part, kind) for part, kind in zip(sent, KINDS)]
 
-    return call(
-        finish_kernel,
-        shape((rows, chans), bf16),
-        [],
-        rows * chans,
-        (*project(a, b[1][3]), *project(b)),
-        "finish",
-    )
+    def finish(piece, parts, *earlier):
+        earlier = tuple(in_hbm(e) for e in earlier)
+        return call(
+            functools.partial(finish_kernel, piece),
+            pltpu.HBM((rows, chans), bf16),
+            [pltpu.VMEM((HALF, chans), bf16), pltpu.SemaphoreType.DMA],
+            HALF * chans,
+            (*parts, *earlier),
+            "finish",
+            in_specs=[vmem] * 4 + [hbm] * len(earlier),
+            out_specs=hbm,
+            input_output_aliases={4 + at: at for at in range(len(earlier))},
+        )
+
+    first = project(b)
+    second = project(a, b[1][3])
+    return finish(0, second, finish(1, first))
 
 
 def solution(mesh):

time: 90.3 us -> 89.6 us (level); the launches traced: 89 us -> 89.4 us
    pallas_call x10 -> x11, Pallas kernels: 11.3 us -> 11.9 us  [call(): pl.pallas_call(kernel, out_shape=shapes, scratch_shapes=scratch, compiler...]
  transfers between devices with their start and end apart: 30 -> 30, of which waited for: 16 -> 15; matrix products, arithmetic and copies ran while one was open for 0% -> 0% of each run, Pallas kernels for 6% -> 7%
where the time goes in v4:
time: 89.6 us; the launch traced here: 89.4 us
  starting transfers between devices  50 us (56%)
  waiting for transfers between devices  27.2 us (30%)
  Pallas kernels  11.9 us (13%)
    ppermute x19, starting transfers between devices, shifted(): lax.ppermute(value, axis, [(at, (at + steps) % count) for at in range(cou...  30.1 us
    ppermute x19, waiting for transfers between devices, shifted(): lax.ppermute(value, axis, [(at, (at + steps) % count) for at in range(cou...  15.7 us
    ppermute x8, starting transfers between devices, swapped(): return lax.ppermute(value, ('core', 'y'), pairs)  13.2 us
    pallas_call x11, Pallas kernels, call(): pl.pallas_call(kernel, out_shape=shapes, scratch_shapes=scratch, compiler...  11.9 us
    ppermute x8, waiting for transfers between devices, swapped(): return lax.ppermute(value, ('core', 'y'), pairs)  10.6 us
    ppermute x3, starting transfers between devices, from_behind(): lax.ppermute(value, axis, [(at, at + steps) for at in range(count - steps)])  6.61 us
  transfers between devices with their start and end apart: 30, of which 15 were waited for; matrix products, arithmetic and copies ran while one was open for 0% of the time, Pallas kernels for 7%

profile of v4, /device:TPU:2, one launch (start us, length us, event | category | flops | bytes accessed | tf_op | source)
XLA Modules:
  0.0 89.4 jit_solution(10043052119529857676)
XLA Ops:
  0.0 3.2 %states.1 = (f32[256,8,128]{2,1,0:T(8,128)S(1)}, f32[16,8,128]{2,1,0:T(8,128)S(1)}, f32[32,128]{1,0:T(8,128)S(1)}, f32[64,128]{1,0:T(8,128)S(1)}) custom-call(bf16[3,8,256,128]{3,2,1,0:T(8,128)(2,1)} %bitcast.7, f32[3,3,128]{2,1,0:T(4,128)} %taps_hbm.1, f32[16,128]{1,0:T(8,128)} %rate_hbm.1, f32[16,128]{1,0:T(8,128)} %residue_hbm.1, f32[1,128]{1,0:T(1,128)} %bitcast.9), custom_call_target="tpu_custom_call" | custom-call | flops 11534336 | bytes 2757632 | tf_op jit(solution)/shard_map/states/pallas_call | solution.py:367
  3.2 4.0 %collective-permute-start = (f32[32,128]{1,0:T(8,128)S(1)}, f32[32,128]{1,0:T(8,128)S(1)}, u32[]{:S(2)}, u32[]{:S(2)}) collective-permute-start(f32[32,128]{1,0:T(8,128)S(1)} %get-tuple-element.53.refs_0_.rest_0_), channel_id=1, source_target_pairs={{0,128},{64,192},{1,129},{65,193},{2,130},{66,194},{3,131},{67,195... | collective-permute-start | bytes 49160 | tf_op jit(solution)/shard_map/ppermute | solution.py:44
  7.9 1.9 %collective-permute-start.2 = (f32[32,128]{1,0:T(8,128)S(1)}, f32[32,128]{1,0:T(8,128)S(1)}, u32[]{:S(2)}, u32[]{:S(2)}) collective-permute-start(f32[32,128]{1,0:T(8,128)S(1)} %get-tuple-element.53.refs_0_.rest_0_), channel_id=1, source_target_pairs={{0,64},{64,128},{128,192},{1,65},{65,129},{129,193},{2,66},{66,130... | collective-permute-start | bytes 49160 | tf_op jit(solution)/shard_map/ppermute | solution.py:44
  11.0 1.6 %local_conv_query.1 = (f32[128,8,128]{2,1,0:T(8,128)S(1)}, f32[256,8,128]{2,1,0:T(8,128)S(1)}) custom-call(bf16[3,8,256,128]{3,2,1,0:T(8,128)(2,1)} %bitcast.8, f32[64,128]{1,0:T(8,128)S(1)} %get-tuple-element.45.param_ref, f32[256,8,128]{2,1,0:T(8,128)S(1)} %get-tuple-element.46.signal_ref, f32[16,8,128]{2,1,0:T(8,128)S(1)} %get-tuple-element.48.start_ref), custom_call_target="tpu_custom_call" | custom-call | flops 10485760 | bytes 4292608 | tf_op jit(solution)/shard_map/local_conv_query/pallas_call | solution.py:367
  14.8 1.5 %gate.1 = bf16[2048,128]{1,0:T(8,128)(2,1)S(1)} custom-call(f32[64,128]{1,0:T(8,128)S(1)} %get-tuple-element.45.param_ref, f32[256,8,128]{2,1,0:T(8,128)S(1)} %get-tuple-element.49.query_ref, f32[128,8,128]{2,1,0:T(8,128)S(1)} %get-tuple-element.50.conv0_ref, f32[128,8,128]{2,1,0:T(8,128)S(1)} %get-tuple-element.51.conv1_ref, ...), custom_call_target="tpu_custom_call" | custom-call | flops 8912896 | bytes 2785280 | tf_op jit(solution)/shard_map/gate/pallas_call | solution.py:367
  16.3 2.0 %collective-permute-start.16 = (bf16[1024,128]{1,0:T(8,128)(2,1)S(1)}, bf16[1024,128]{1,0:T(8,128)(2,1)S(1)}, u32[]{:S(2)}, u32[]{:S(2)}) collective-permute-start(bf16[1024,128]{1,0:T(8,128)(2,1)S(1)} %get-tuple-element.69.here), channel_id=1, source_target_pairs={{0,4},{4,8},{8,12},{12,16},{16,20},{20,24},{24,28},{28,0},{1,5},{5... | collective-permute-start | bytes 786440 | tf_op jit(solution)/shard_map/ppermute | solution.py:25
  18.3 4.0 %collective-permute-start.17 = (bf16[1024,128]{1,0:T(8,128)(2,1)S(1)}, bf16[1024,128]{1,0:T(8,128)(2,1)S(1)}, u32[]{:S(2)}, u32[]{:S(2)}) collective-permute-start(bf16[1024,128]{1,0:T(8,128)(2,1)S(1)} %get-tuple-element.69.here), channel_id=1, source_target_pairs={{0,28},{4,0},{8,4},{12,8},{16,12},{20,16},{24,20},{28,24},{1,29},{... | collective-permute-start | bytes 786440 | tf_op jit(solution)/shard_map/ppermute | solution.py:25
  22.4 3.2 %collective-permute-start.5 = (bf16[1024,128]{1,0:T(8,128)(2,1)S(1)}, bf16[1024,128]{1,0:T(8,128)(2,1)S(1)}, u32[]{:S(2)}, u32[]{:S(2)}) collective-permute-start(bf16[1024,128]{1,0:T(8,128)(2,1)S(1)} %get-tuple-element.58.here), channel_id=1, source_target_pairs={{0,28},{4,0},{8,4},{12,8},{16,12},{20,16},{24,20},{28,24},{1,29},{... | collective-permute-start | bytes 786440 | tf_op jit(solution)/shard_map/ppermute | solution.py:25
  25.6 1.7 %collective-permute-start.14 = (bf16[8,128,128]{2,1,0:T(8,128)(2,1)S(1)}, bf16[8,128,128]{2,1,0:T(8,128)(2,1)S(1)}, u32[]{:S(2)}, u32[]{:S(2)}) collective-permute-start(bf16[8,128,128]{2,1,0:T(8,128)(2,1)S(1)} %get-tuple-element.67), channel_id=1, source_target_pairs={{0,1},{1,0},{2,3},{3,2},{32,35},{33,34},{34,33},{35,32},{4,5},{5,4... | collective-permute-start | bytes 786440 | tf_op jit(solution)/shard_map/ppermute | solution.py:34
  27.3 2.1 %collective-permute-done.16.f1 = bf16[1024,128]{1,0:T(8,128)(2,1)S(1)} collective-permute-done((bf16[1024,128]{1,0:T(8,128)(2,1)S(1)}, bf16[1024,128]{1,0:T(8,128)(2,1)S(1)}, u32[]{:S(2)}, u32[]{:S(2)}) %collective-permute-start.16) | collective-permute-done | bytes 262176 | tf_op jit(solution)/shard_map/ppermute | solution.py:25
  29.4 3.3 %collective-permute-start.19 = (bf16[1024,128]{1,0:T(8,128)(2,1)S(1)}, bf16[1024,128]{1,0:T(8,128)(2,1)S(1)}, u32[]{:S(2)}, u32[]{:S(2)}) collective-permute-start(bf16[1024,128]{1,0:T(8,128)(2,1)S(1)} %collective-permute-done.17.b1), channel_id=1, source_target_pairs={{0,28},{4,0},{8,4},{12,8},{16,12},{20,16},{24,20},{28,24},{1,29},{... | collective-permute-start | bytes 786440 | tf_op jit(solution)/shard_map/ppermute | solution.py:25
  32.7 2.3 %collective-permute-done.4.f1 = bf16[1024,128]{1,0:T(8,128)(2,1)S(1)} collective-permute-done((bf16[1024,128]{1,0:T(8,128)(2,1)S(1)}, bf16[1024,128]{1,0:T(8,128)(2,1)S(1)}, u32[]{:S(2)}, u32[]{:S(2)}) %collective-permute-start.4) | collective-permute-done | bytes 262176 | tf_op jit(solution)/shard_map/ppermute | solution.py:25
  35.0 3.2 %collective-permute-start.8 = (bf16[4,128,128]{2,1,0:T(8,128)(2,1)S(1)}, bf16[4,128,128]{2,1,0:T(8,128)(2,1)S(1)}, u32[]{:S(2)}, u32[]{:S(2)}) collective-permute-start(bf16[4,128,128]{2,1,0:T(8,128)(2,1)S(1)} %get-tuple-element.62), channel_id=1, source_target_pairs={{0,2},{1,3},{2,0},{3,1},{32,34},{33,35},{34,32},{35,33},{4,6},{5,7... | collective-permute-start | bytes 393224 | tf_op jit(solution)/shard_map/ppermute | solution.py:34
  38.2 3.4 %collective-permute-start.7 = (bf16[1024,128]{1,0:T(8,128)(2,1)S(1)}, bf16[1024,128]{1,0:T(8,128)(2,1)S(1)}, u32[]{:S(2)}, u32[]{:S(2)}) collective-permute-start(bf16[1024,128]{1,0:T(8,128)(2,1)S(1)} %collective-permute-done.5.b1), channel_id=1, source_target_pairs={{0,28},{4,0},{8,4},{12,8},{16,12},{20,16},{24,20},{28,24},{1,29},{... | collective-permute-start | bytes 786440 | tf_op jit(solution)/shard_map/ppermute | solution.py:25
  41.6 2.1 %collective-permute-start.20 = (bf16[1024,128]{1,0:T(8,128)(2,1)S(1)}, bf16[1024,128]{1,0:T(8,128)(2,1)S(1)}, u32[]{:S(2)}, u32[]{:S(2)}) collective-permute-start(bf16[1024,128]{1,0:T(8,128)(2,1)S(1)} %collective-permute-done.19.b2), channel_id=1, source_target_pairs={{0,28},{4,0},{8,4},{12,8},{16,12},{20,16},{24,20},{28,24},{1,29},{... | collective-permute-start | bytes 786440 | tf_op jit(solution)/shard_map/ppermute | solution.py:25
  47.3 3.7 %collective-permute-start.10 = (bf16[1024,128]{1,0:T(8,128)(2,1)S(1)}, bf16[1024,128]{1,0:T(8,128)(2,1)S(1)}, u32[]{:S(2)}, u32[]{:S(2)}) collective-permute-start(bf16[1024,128]{1,0:T(8,128)(2,1)S(1)} %collective-permute-done.7.b2), channel_id=1, source_target_pairs={{0,28},{4,0},{8,4},{12,8},{16,12},{20,16},{24,20},{28,24},{1,29},{... | collective-permute-start | bytes 786440 | tf_op jit(solution)/shard_map/ppermute | solution.py:25
  54.0 3.3 %collective-permute-start.25 = (bf16[512,128]{1,0:T(8,128)(2,1)S(1)}, bf16[512,128]{1,0:T(8,128)(2,1)S(1)}, u32[]{:S(2)}, u32[]{:S(2)}) collective-permute-start(bf16[512,128]{1,0:T(8,128)(2,1)S(1)} %slice.24), channel_id=1, source_target_pairs={{0,4},{4,8},{8,12},{12,16},{16,20},{20,24},{24,28},{28,0},{1,5},{5... | collective-permute-start | bytes 393224 | tf_op jit(solution)/shard_map/ppermute | solution.py:25
  57.4 4.2 %collective-permute-done.25.f4 = bf16[512,128]{1,0:T(8,128)(2,1)S(1)} collective-permute-done((bf16[512,128]{1,0:T(8,128)(2,1)S(1)}, bf16[512,128]{1,0:T(8,128)(2,1)S(1)}, u32[]{:S(2)}, u32[]{:S(2)}) %collective-permute-start.25) | collective-permute-done | bytes 131104 | tf_op jit(solution)/shard_map/ppermute | solution.py:25
  63.6 1.7 %collective-permute-start.27 = (bf16[1024,128]{1,0:T(8,128)(2,1)S(1)}, bf16[1024,128]{1,0:T(8,128)(2,1)S(1)}, u32[]{:S(2)}, u32[]{:S(2)}) collective-permute-start(bf16[1024,128]{1,0:T(8,128)(2,1)S(1)} %get-tuple-element.82), channel_id=1, source_target_pairs={{0,2},{1,3},{2,0},{3,1},{32,34},{33,35},{34,32},{35,33},{4,6},{5,7... | collective-permute-start | bytes 786440 | tf_op jit(solution)/shard_map/ppermute | solution.py:34
  66.3 2.4 %collective-permute-start.13 = (bf16[512,128]{1,0:T(8,128)(2,1)S(1)}, bf16[512,128]{1,0:T(8,128)(2,1)S(1)}, u32[]{:S(2)}, u32[]{:S(2)}) collective-permute-start(bf16[512,128]{1,0:T(8,128)(2,1)S(1)} %slice.22), channel_id=1, source_target_pairs={{0,28},{4,0},{8,4},{12,8},{16,12},{20,16},{24,20},{28,24},{1,29},{... | collective-permute-start | bytes 393224 | tf_op jit(solution)/shard_map/ppermute | solution.py:25
  69.4 1.8 %collective-permute-start.29 = (bf16[1024,128]{1,0:T(8,128)(2,1)S(1)}, bf16[1024,128]{1,0:T(8,128)(2,1)S(1)}, u32[]{:S(2)}, u32[]{:S(2)}) collective-permute-start(bf16[1024,128]{1,0:T(8,128)(2,1)S(1)} %get-tuple-element.84), channel_id=1, source_target_pairs={{0,3},{1,2},{2,1},{3,0},{32,33},{33,32},{34,35},{35,34},{4,7},{5,6... | collective-permute-start | bytes 786440 | tf_op jit(solution)/shard_map/ppermute | solution.py:34
  72.8 2.8 %collective-permute-start.21 = (bf16[1024,128]{1,0:T(8,128)(2,1)S(1)}, bf16[1024,128]{1,0:T(8,128)(2,1)S(1)}, u32[]{:S(2)}, u32[]{:S(2)}) collective-permute-start(bf16[1024,128]{1,0:T(8,128)(2,1)S(1)} %get-tuple-element.75), channel_id=1, source_target_pairs={{0,2},{1,3},{2,0},{3,1},{32,34},{33,35},{34,32},{35,33},{4,6},{5,7... | collective-permute-start | bytes 786440 | tf_op jit(solution)/shard_map/ppermute | solution.py:34
  78.0 6.6 %collective-permute-done.29.three = bf16[1024,128]{1,0:T(8,128)(2,1)S(1)} collective-permute-done((bf16[1024,128]{1,0:T(8,128)(2,1)S(1)}, bf16[1024,128]{1,0:T(8,128)(2,1)S(1)}, u32[]{:S(2)}, u32[]{:S(2)}) %collective-permute-start.29) | collective-permute-done | bytes 262176 | tf_op jit(solution)/shard_map/ppermute | solution.py:34
  85.4 1.8 %collective-permute-done.22.two = bf16[1024,128]{1,0:T(8,128)(2,1)S(1)} collective-permute-done((bf16[1024,128]{1,0:T(8,128)(2,1)S(1)}, bf16[1024,128]{1,0:T(8,128)(2,1)S(1)}, u32[]{:S(2)}, u32[]{:S(2)}) %collective-permute-start.22) | collective-permute-done | bytes 262176 | tf_op jit(solution)/shard_map/ppermute | solution.py:34
  (54 shorter events, 21.3 us)
Async XLA Ops:
  3.2 9.5 %collective-permute-start = (f32[32,128]{1,0:T(8,128)S(1)}, f32[32,128]{1,0:T(8,128)S(1)}, u32[]{:S(2)}, u32[]{:S(2)}) collective-permute-start(f32[32,128]{1,0:T(8,128)S(1)} %get-tuple-element.53.refs_0_.rest_0_), channel_id=1, source_target_pairs={{0,128},{64,192},{1,129},{65,193},{2,130},{66,194},{3,131},{67,195... | collective-permute-start | bytes 49160 | tf_op jit(solution)/shard_map/ppermute | solution.py:44
  16.3 13.0 %collective-permute-start.16 = (bf16[1024,128]{1,0:T(8,128)(2,1)S(1)}, bf16[1024,128]{1,0:T(8,128)(2,1)S(1)}, u32[]{:S(2)}, u32[]{:S(2)}) collective-permute-start(bf16[1024,128]{1,0:T(8,128)(2,1)S(1)} %get-tuple-element.69.here), channel_id=1, source_target_pairs={{0,4},{4,8},{8,12},{12,16},{16,20},{20,24},{24,28},{28,0},{1,5},{5... | collective-permute-start | bytes 786440 | tf_op jit(solution)/shard_map/ppermute | solution.py:25
  18.3 11.0 %collective-permute-start.17 = (bf16[1024,128]{1,0:T(8,128)(2,1)S(1)}, bf16[1024,128]{1,0:T(8,128)(2,1)S(1)}, u32[]{:S(2)}, u32[]{:S(2)}) collective-permute-start(bf16[1024,128]{1,0:T(8,128)(2,1)S(1)} %get-tuple-element.69.here), channel_id=1, source_target_pairs={{0,28},{4,0},{8,4},{12,8},{16,12},{20,16},{24,20},{28,24},{1,29},{... | collective-permute-start | bytes 786440 | tf_op jit(solution)/shard_map/ppermute | solution.py:25
  22.4 12.6 %collective-permute-start.4 = (bf16[1024,128]{1,0:T(8,128)(2,1)S(1)}, bf16[1024,128]{1,0:T(8,128)(2,1)S(1)}, u32[]{:S(2)}, u32[]{:S(2)}) collective-permute-start(bf16[1024,128]{1,0:T(8,128)(2,1)S(1)} %get-tuple-element.58.here), channel_id=1, source_target_pairs={{0,4},{4,8},{8,12},{12,16},{16,20},{20,24},{24,28},{28,0},{1,5},{5... | collective-permute-start | bytes 786440 | tf_op jit(solution)/shard_map/ppermute | solution.py:25
  22.4 12.6 %collective-permute-start.5 = (bf16[1024,128]{1,0:T(8,128)(2,1)S(1)}, bf16[1024,128]{1,0:T(8,128)(2,1)S(1)}, u32[]{:S(2)}, u32[]{:S(2)}) collective-permute-start(bf16[1024,128]{1,0:T(8,128)(2,1)S(1)} %get-tuple-element.58.here), channel_id=1, source_target_pairs={{0,28},{4,0},{8,4},{12,8},{16,12},{20,16},{24,20},{28,24},{1,29},{... | collective-permute-start | bytes 786440 | tf_op jit(solution)/shard_map/ppermute | solution.py:25
  25.6 12.6 %collective-permute-start.14 = (bf16[8,128,128]{2,1,0:T(8,128)(2,1)S(1)}, bf16[8,128,128]{2,1,0:T(8,128)(2,1)S(1)}, u32[]{:S(2)}, u32[]{:S(2)}) collective-permute-start(bf16[8,128,128]{2,1,0:T(8,128)(2,1)S(1)} %get-tuple-element.67), channel_id=1, source_target_pairs={{0,1},{1,0},{2,3},{3,2},{32,35},{33,34},{34,33},{35,32},{4,5},{5,4... | collective-permute-start | bytes 786440 | tf_op jit(solution)/shard_map/ppermute | solution.py:34
  29.4 12.2 %collective-permute-start.18 = (bf16[1024,128]{1,0:T(8,128)(2,1)S(1)}, bf16[1024,128]{1,0:T(8,128)(2,1)S(1)}, u32[]{:S(2)}, u32[]{:S(2)}) collective-permute-start(bf16[1024,128]{1,0:T(8,128)(2,1)S(1)} %collective-permute-done.16.f1), channel_id=1, source_target_pairs={{0,4},{4,8},{8,12},{12,16},{16,20},{20,24},{24,28},{28,0},{1,5},{5... | collective-permute-start | bytes 786440 | tf_op jit(solution)/shard_map/ppermute | solution.py:25
  29.4 12.1 %collective-permute-start.19 = (bf16[1024,128]{1,0:T(8,128)(2,1)S(1)}, bf16[1024,128]{1,0:T(8,128)(2,1)S(1)}, u32[]{:S(2)}, u32[]{:S(2)}) collective-permute-start(bf16[1024,128]{1,0:T(8,128)(2,1)S(1)} %collective-permute-done.17.b1), channel_id=1, source_target_pairs={{0,28},{4,0},{8,4},{12,8},{16,12},{20,16},{24,20},{28,24},{1,29},{... | collective-permute-start | bytes 786440 | tf_op jit(solution)/shard_map/ppermute | solution.py:25
  35.0 10.8 %collective-permute-start.6 = (bf16[1024,128]{1,0:T(8,128)(2,1)S(1)}, bf16[1024,128]{1,0:T(8,128)(2,1)S(1)}, u32[]{:S(2)}, u32[]{:S(2)}) collective-permute-start(bf16[1024,128]{1,0:T(8,128)(2,1)S(1)} %collective-permute-done.4.f1), channel_id=1, source_target_pairs={{0,4},{4,8},{8,12},{12,16},{16,20},{20,24},{24,28},{28,0},{1,5},{5... | collective-permute-start | bytes 786440 | tf_op jit(solution)/shard_map/ppermute | solution.py:25
  35.0 8.7 %collective-permute-start.8 = (bf16[4,128,128]{2,1,0:T(8,128)(2,1)S(1)}, bf16[4,128,128]{2,1,0:T(8,128)(2,1)S(1)}, u32[]{:S(2)}, u32[]{:S(2)}) collective-permute-start(bf16[4,128,128]{2,1,0:T(8,128)(2,1)S(1)} %get-tuple-element.62), channel_id=1, source_target_pairs={{0,2},{1,3},{2,0},{3,1},{32,34},{33,35},{34,32},{35,33},{4,6},{5,7... | collective-permute-start | bytes 393224 | tf_op jit(solution)/shard_map/ppermute | solution.py:34
  38.2 9.1 %collective-permute-start.7 = (bf16[1024,128]{1,0:T(8,128)(2,1)S(1)}, bf16[1024,128]{1,0:T(8,128)(2,1)S(1)}, u32[]{:S(2)}, u32[]{:S(2)}) collective-permute-start(bf16[1024,128]{1,0:T(8,128)(2,1)S(1)} %collective-permute-done.5.b1), channel_id=1, source_target_pairs={{0,28},{4,0},{8,4},{12,8},{16,12},{20,16},{24,20},{28,24},{1,29},{... | collective-permute-start | bytes 786440 | tf_op jit(solution)/shard_map/ppermute | solution.py:25
  41.6 10.1 %collective-permute-start.15 = (bf16[8,128,128]{2,1,0:T(8,128)(2,1)S(1)}, bf16[8,128,128]{2,1,0:T(8,128)(2,1)S(1)}, u32[]{:S(2)}, u32[]{:S(2)}) collective-permute-start(bf16[8,128,128]{2,1,0:T(8,128)(2,1)S(1)} %collective-permute-done.14.near), channel_id=1, source_target_pairs={{0,32},{32,0},{1,33},{33,1},{2,34},{34,2},{3,35},{35,3},{4,36},{36... | collective-permute-start | bytes 786440 | tf_op jit(solution)/shard_map/ppermute | solution.py:25
  41.6 11.3 %collective-permute-start.20 = (bf16[1024,128]{1,0:T(8,128)(2,1)S(1)}, bf16[1024,128]{1,0:T(8,128)(2,1)S(1)}, u32[]{:S(2)}, u32[]{:S(2)}) collective-permute-start(bf16[1024,128]{1,0:T(8,128)(2,1)S(1)} %collective-permute-done.19.b2), channel_id=1, source_target_pairs={{0,28},{4,0},{8,4},{12,8},{16,12},{20,16},{24,20},{28,24},{1,29},{... | collective-permute-start | bytes 786440 | tf_op jit(solution)/shard_map/ppermute | solution.py:25
  43.7 10.4 %collective-permute-start.24 = (bf16[1024,128]{1,0:T(8,128)(2,1)S(1)}, bf16[1024,128]{1,0:T(8,128)(2,1)S(1)}, u32[]{:S(2)}, u32[]{:S(2)}) collective-permute-start(bf16[1024,128]{1,0:T(8,128)(2,1)S(1)} %collective-permute-done.18.f2), channel_id=1, source_target_pairs={{0,4},{4,8},{8,12},{12,16},{16,20},{20,24},{24,28},{28,0},{1,5},{5... | collective-permute-start | bytes 786440 | tf_op jit(solution)/shard_map/ppermute | solution.py:25
  47.3 18.0 %collective-permute-start.10 = (bf16[1024,128]{1,0:T(8,128)(2,1)S(1)}, bf16[1024,128]{1,0:T(8,128)(2,1)S(1)}, u32[]{:S(2)}, u32[]{:S(2)}) collective-permute-start(bf16[1024,128]{1,0:T(8,128)(2,1)S(1)} %collective-permute-done.7.b2), channel_id=1, source_target_pairs={{0,28},{4,0},{8,4},{12,8},{16,12},{20,16},{24,20},{28,24},{1,29},{... | collective-permute-start | bytes 786440 | tf_op jit(solution)/shard_map/ppermute | solution.py:25
  51.0 14.3 %collective-permute-start.9 = (bf16[1024,128]{1,0:T(8,128)(2,1)S(1)}, bf16[1024,128]{1,0:T(8,128)(2,1)S(1)}, u32[]{:S(2)}, u32[]{:S(2)}) collective-permute-start(bf16[1024,128]{1,0:T(8,128)(2,1)S(1)} %collective-permute-done.6.f2), channel_id=1, source_target_pairs={{0,4},{4,8},{8,12},{12,16},{16,20},{20,24},{24,28},{28,0},{1,5},{5... | collective-permute-start | bytes 786440 | tf_op jit(solution)/shard_map/ppermute | solution.py:25
  54.0 7.6 %collective-permute-start.25 = (bf16[512,128]{1,0:T(8,128)(2,1)S(1)}, bf16[512,128]{1,0:T(8,128)(2,1)S(1)}, u32[]{:S(2)}, u32[]{:S(2)}) collective-permute-start(bf16[512,128]{1,0:T(8,128)(2,1)S(1)} %slice.24), channel_id=1, source_target_pairs={{0,4},{4,8},{8,12},{12,16},{16,20},{20,24},{24,28},{28,0},{1,5},{5... | collective-permute-start | bytes 393224 | tf_op jit(solution)/shard_map/ppermute | solution.py:25
  63.6 12.7 %collective-permute-start.27 = (bf16[1024,128]{1,0:T(8,128)(2,1)S(1)}, bf16[1024,128]{1,0:T(8,128)(2,1)S(1)}, u32[]{:S(2)}, u32[]{:S(2)}) collective-permute-start(bf16[1024,128]{1,0:T(8,128)(2,1)S(1)} %get-tuple-element.82), channel_id=1, source_target_pairs={{0,2},{1,3},{2,0},{3,1},{32,34},{33,35},{34,32},{35,33},{4,6},{5,7... | collective-permute-start | bytes 786440 | tf_op jit(solution)/shard_map/ppermute | solution.py:34
  65.3 6.3 %collective-permute-start.12 = (bf16[512,128]{1,0:T(8,128)(2,1)S(1)}, bf16[512,128]{1,0:T(8,128)(2,1)S(1)}, u32[]{:S(2)}, u32[]{:S(2)}) collective-permute-start(bf16[512,128]{1,0:T(8,128)(2,1)S(1)} %slice.21), channel_id=1, source_target_pairs={{0,4},{4,8},{8,12},{12,16},{16,20},{20,24},{24,28},{28,0},{1,5},{5... | collective-permute-start | bytes 393224 | tf_op jit(solution)/shard_map/ppermute | solution.py:25
  68.7 9.2 %collective-permute-start.28 = (bf16[1024,128]{1,0:T(8,128)(2,1)S(1)}, bf16[1024,128]{1,0:T(8,128)(2,1)S(1)}, u32[]{:S(2)}, u32[]{:S(2)}) collective-permute-start(bf16[1024,128]{1,0:T(8,128)(2,1)S(1)} %get-tuple-element.83), channel_id=1, source_target_pairs={{0,1},{1,0},{2,3},{3,2},{32,35},{33,34},{34,33},{35,32},{4,5},{5,4... | collective-permute-start | bytes 786440 | tf_op jit(solution)/shard_map/ppermute | solution.py:34
  69.4 15.2 %collective-permute-start.29 = (bf16[1024,128]{1,0:T(8,128)(2,1)S(1)}, bf16[1024,128]{1,0:T(8,128)(2,1)S(1)}, u32[]{:S(2)}, u32[]{:S(2)}) collective-permute-start(bf16[1024,128]{1,0:T(8,128)(2,1)S(1)} %get-tuple-element.84), channel_id=1, source_target_pairs={{0,3},{1,2},{2,1},{3,0},{32,33},{33,32},{34,35},{35,34},{4,7},{5,6... | collective-permute-start | bytes 786440 | tf_op jit(solution)/shard_map/ppermute | solution.py:34
  72.8 12.6 %collective-permute-start.21 = (bf16[1024,128]{1,0:T(8,128)(2,1)S(1)}, bf16[1024,128]{1,0:T(8,128)(2,1)S(1)}, u32[]{:S(2)}, u32[]{:S(2)}) collective-permute-start(bf16[1024,128]{1,0:T(8,128)(2,1)S(1)} %get-tuple-element.75), channel_id=1, source_target_pairs={{0,2},{1,3},{2,0},{3,1},{32,34},{33,35},{34,32},{35,33},{4,6},{5,7... | collective-permute-start | bytes 786440 | tf_op jit(solution)/shard_map/ppermute | solution.py:34
  75.7 11.5 %collective-permute-start.22 = (bf16[1024,128]{1,0:T(8,128)(2,1)S(1)}, bf16[1024,128]{1,0:T(8,128)(2,1)S(1)}, u32[]{:S(2)}, u32[]{:S(2)}) collective-permute-start(bf16[1024,128]{1,0:T(8,128)(2,1)S(1)} %get-tuple-element.76), channel_id=1, source_target_pairs={{0,1},{1,0},{2,3},{3,2},{32,35},{33,34},{34,33},{35,32},{4,5},{5,4... | collective-permute-start | bytes 786440 | tf_op jit(solution)/shard_map/ppermute | solution.py:34
  76.4 12.1 %collective-permute-start.23 = (bf16[1024,128]{1,0:T(8,128)(2,1)S(1)}, bf16[1024,128]{1,0:T(8,128)(2,1)S(1)}, u32[]{:S(2)}, u32[]{:S(2)}) collective-permute-start(bf16[1024,128]{1,0:T(8,128)(2,1)S(1)} %get-tuple-element.77), channel_id=1, source_target_pairs={{0,3},{1,2},{2,1},{3,0},{32,33},{33,32},{34,35},{35,34},{4,7},{5,6... | collective-permute-start | bytes 786440 | tf_op jit(solution)/shard_map/ppermute | solution.py:34
  (7 other events, 38.7 us)

commit v5 on v4

--- a/solution.py
+++ b/solution.py
@@ -11,7 +11,7 @@
 CTX = ("x", "core")
 SUB = 8
 PAD = 8
-UNROLL = 8
+UNROLL = 16
 HALF = 1024
 KINDS = (2, 1, 3)
 LOADS = 4
@@ -389,7 +389,7 @@
 
     hbm = pl.BlockSpec(memory_space=pltpu.HBM)
     planes = in_hbm(jnp.transpose(streams, (1, 0, 2)).reshape(3, SUB, steps, chans))
-    padded = pltpu.VMEM((SUB * (steps + PAD), chans), f32)
+    padded = pltpu.VMEM(((SUB + 1) * (steps + PAD), chans), f32)
     modes = [in_hbm(m) for m in (short_filter, decay_rate, residue, skip_gain[None, :])]
     signal, start, packed, params = call(
         state_kernel,
@@ -444,7 +444,7 @@
     gated = call(
         gate_kernel,
         shape((rows, chans), bf16),
-        [pltpu.VMEM((rows, chans), f32), pltpu.VMEM((8, *packed.shape), f32)],
+        [pltpu.VMEM((rows + steps, chans), f32), pltpu.VMEM((8, *packed.shape), f32)],
         rows * chans * 34,
         (params, query, conv0, conv1, *own_ends, other_ends),
         "gate",

time: 89.6 us -> 89.3 us (level)
  no operation moved by 1% of the time
where the time goes in v5:
time: 89.3 us; the launch traced here: 89.2 us
  starting transfers between devices  50 us (56%)
  waiting for transfers between devices  27.3 us (31%)
  Pallas kernels  11.5 us (13%)
    ppermute x19, starting transfers between devices, shifted(): lax.ppermute(value, axis, [(at, (at + steps) % count) for at in range(cou...  30.1 us
    ppermute x19, waiting for transfers between devices, shifted(): lax.ppermute(value, axis, [(at, (at + steps) % count) for at in range(cou...  15.7 us
    ppermute x8, starting transfers between devices, swapped(): return lax.ppermute(value, ('core', 'y'), pairs)  13.2 us
    pallas_call x11, Pallas kernels, call(): pl.pallas_call(kernel, out_shape=shapes, scratch_shapes=scratch, compiler...  11.5 us
    ppermute x8, waiting for transfers between devices, swapped(): return lax.ppermute(value, ('core', 'y'), pairs)  10.6 us
    ppermute x3, starting transfers between devices, from_behind(): lax.ppermute(value, axis, [(at, at + steps) for at in range(count - steps)])  6.61 us
  transfers between devices with their start and end apart: 30, of which 15 were waited for; matrix products, arithmetic and copies ran while one was open for 0% of the time, Pallas kernels for 7%

profile of v5, /device:TPU:2, one launch (start us, length us, event | category | flops | bytes accessed | tf_op | source)
XLA Modules:
  0.0 89.2 jit_solution(17034757652608151209)
XLA Ops:
  0.0 3.0 %states.1 = (f32[256,8,128]{2,1,0:T(8,128)S(1)}, f32[16,8,128]{2,1,0:T(8,128)S(1)}, f32[32,128]{1,0:T(8,128)S(1)}, f32[64,128]{1,0:T(8,128)S(1)}) custom-call(bf16[3,8,256,128]{3,2,1,0:T(8,128)(2,1)} %bitcast.7, f32[3,3,128]{2,1,0:T(4,128)} %taps_hbm.1, f32[16,128]{1,0:T(8,128)} %rate_hbm.1, f32[16,128]{1,0:T(8,128)} %residue_hbm.1, f32[1,128]{1,0:T(1,128)} %bitcast.9), custom_call_target="tpu_custom_call" | custom-call | flops 11534336 | bytes 2757632 | tf_op jit(solution)/shard_map/states/pallas_call | solution.py:367
  3.0 4.0 %collective-permute-start = (f32[32,128]{1,0:T(8,128)S(1)}, f32[32,128]{1,0:T(8,128)S(1)}, u32[]{:S(2)}, u32[]{:S(2)}) collective-permute-start(f32[32,128]{1,0:T(8,128)S(1)} %get-tuple-element.53.refs_0_.rest_0_), channel_id=1, source_target_pairs={{0,128},{64,192},{1,129},{65,193},{2,130},{66,194},{3,131},{67,195... | collective-permute-start | bytes 49160 | tf_op jit(solution)/shard_map/ppermute | solution.py:44
  7.7 1.9 %collective-permute-start.2 = (f32[32,128]{1,0:T(8,128)S(1)}, f32[32,128]{1,0:T(8,128)S(1)}, u32[]{:S(2)}, u32[]{:S(2)}) collective-permute-start(f32[32,128]{1,0:T(8,128)S(1)} %get-tuple-element.53.refs_0_.rest_0_), channel_id=1, source_target_pairs={{0,64},{64,128},{128,192},{1,65},{65,129},{129,193},{2,66},{66,130... | collective-permute-start | bytes 49160 | tf_op jit(solution)/shard_map/ppermute | solution.py:44
  10.8 1.5 %local_conv_query.1 = (f32[128,8,128]{2,1,0:T(8,128)S(1)}, f32[256,8,128]{2,1,0:T(8,128)S(1)}) custom-call(bf16[3,8,256,128]{3,2,1,0:T(8,128)(2,1)} %bitcast.8, f32[64,128]{1,0:T(8,128)S(1)} %get-tuple-element.45.param_ref, f32[256,8,128]{2,1,0:T(8,128)S(1)} %get-tuple-element.46.signal_ref, f32[16,8,128]{2,1,0:T(8,128)S(1)} %get-tuple-element.48.start_ref), custom_call_target="tpu_custom_call" | custom-call | flops 10485760 | bytes 4292608 | tf_op jit(solution)/shard_map/local_conv_query/pallas_call | solution.py:367
  16.1 2.0 %collective-permute-start.16 = (bf16[1024,128]{1,0:T(8,128)(2,1)S(1)}, bf16[1024,128]{1,0:T(8,128)(2,1)S(1)}, u32[]{:S(2)}, u32[]{:S(2)}) collective-permute-start(bf16[1024,128]{1,0:T(8,128)(2,1)S(1)} %get-tuple-element.69.here), channel_id=1, source_target_pairs={{0,4},{4,8},{8,12},{12,16},{16,20},{20,24},{24,28},{28,0},{1,5},{5... | collective-permute-start | bytes 786440 | tf_op jit(solution)/shard_map/ppermute | solution.py:25
  18.1 4.0 %collective-permute-start.17 = (bf16[1024,128]{1,0:T(8,128)(2,1)S(1)}, bf16[1024,128]{1,0:T(8,128)(2,1)S(1)}, u32[]{:S(2)}, u32[]{:S(2)}) collective-permute-start(bf16[1024,128]{1,0:T(8,128)(2,1)S(1)} %get-tuple-element.69.here), channel_id=1, source_target_pairs={{0,28},{4,0},{8,4},{12,8},{16,12},{20,16},{24,20},{28,24},{1,29},{... | collective-permute-start | bytes 786440 | tf_op jit(solution)/shard_map/ppermute | solution.py:25
  22.1 3.2 %collective-permute-start.5 = (bf16[1024,128]{1,0:T(8,128)(2,1)S(1)}, bf16[1024,128]{1,0:T(8,128)(2,1)S(1)}, u32[]{:S(2)}, u32[]{:S(2)}) collective-permute-start(bf16[1024,128]{1,0:T(8,128)(2,1)S(1)} %get-tuple-element.58.here), channel_id=1, source_target_pairs={{0,28},{4,0},{8,4},{12,8},{16,12},{20,16},{24,20},{28,24},{1,29},{... | collective-permute-start | bytes 786440 | tf_op jit(solution)/shard_map/ppermute | solution.py:25
  25.4 1.7 %collective-permute-start.14 = (bf16[8,128,128]{2,1,0:T(8,128)(2,1)S(1)}, bf16[8,128,128]{2,1,0:T(8,128)(2,1)S(1)}, u32[]{:S(2)}, u32[]{:S(2)}) collective-permute-start(bf16[8,128,128]{2,1,0:T(8,128)(2,1)S(1)} %get-tuple-element.67), channel_id=1, source_target_pairs={{0,1},{1,0},{2,3},{3,2},{32,35},{33,34},{34,33},{35,32},{4,5},{5,4... | collective-permute-start | bytes 786440 | tf_op jit(solution)/shard_map/ppermute | solution.py:34
  27.1 2.1 %collective-permute-done.16.f1 = bf16[1024,128]{1,0:T(8,128)(2,1)S(1)} collective-permute-done((bf16[1024,128]{1,0:T(8,128)(2,1)S(1)}, bf16[1024,128]{1,0:T(8,128)(2,1)S(1)}, u32[]{:S(2)}, u32[]{:S(2)}) %collective-permute-start.16) | collective-permute-done | bytes 262176 | tf_op jit(solution)/shard_map/ppermute | solution.py:25
  29.2 3.3 %collective-permute-start.19 = (bf16[1024,128]{1,0:T(8,128)(2,1)S(1)}, bf16[1024,128]{1,0:T(8,128)(2,1)S(1)}, u32[]{:S(2)}, u32[]{:S(2)}) collective-permute-start(bf16[1024,128]{1,0:T(8,128)(2,1)S(1)} %collective-permute-done.17.b1), channel_id=1, source_target_pairs={{0,28},{4,0},{8,4},{12,8},{16,12},{20,16},{24,20},{28,24},{1,29},{... | collective-permute-start | bytes 786440 | tf_op jit(solution)/shard_map/ppermute | solution.py:25
  32.5 2.3 %collective-permute-done.4.f1 = bf16[1024,128]{1,0:T(8,128)(2,1)S(1)} collective-permute-done((bf16[1024,128]{1,0:T(8,128)(2,1)S(1)}, bf16[1024,128]{1,0:T(8,128)(2,1)S(1)}, u32[]{:S(2)}, u32[]{:S(2)}) %collective-permute-start.4) | collective-permute-done | bytes 262176 | tf_op jit(solution)/shard_map/ppermute | solution.py:25
  34.8 3.2 %collective-permute-start.8 = (bf16[4,128,128]{2,1,0:T(8,128)(2,1)S(1)}, bf16[4,128,128]{2,1,0:T(8,128)(2,1)S(1)}, u32[]{:S(2)}, u32[]{:S(2)}) collective-permute-start(bf16[4,128,128]{2,1,0:T(8,128)(2,1)S(1)} %get-tuple-element.62), channel_id=1, source_target_pairs={{0,2},{1,3},{2,0},{3,1},{32,34},{33,35},{34,32},{35,33},{4,6},{5,7... | collective-permute-start | bytes 393224 | tf_op jit(solution)/shard_map/ppermute | solution.py:34
  38.0 3.4 %collective-permute-start.7 = (bf16[1024,128]{1,0:T(8,128)(2,1)S(1)}, bf16[1024,128]{1,0:T(8,128)(2,1)S(1)}, u32[]{:S(2)}, u32[]{:S(2)}) collective-permute-start(bf16[1024,128]{1,0:T(8,128)(2,1)S(1)} %collective-permute-done.5.b1), channel_id=1, source_target_pairs={{0,28},{4,0},{8,4},{12,8},{16,12},{20,16},{24,20},{28,24},{1,29},{... | collective-permute-start | bytes 786440 | tf_op jit(solution)/shard_map/ppermute | solution.py:25
  41.3 2.1 %collective-permute-start.20 = (bf16[1024,128]{1,0:T(8,128)(2,1)S(1)}, bf16[1024,128]{1,0:T(8,128)(2,1)S(1)}, u32[]{:S(2)}, u32[]{:S(2)}) collective-permute-start(bf16[1024,128]{1,0:T(8,128)(2,1)S(1)} %collective-permute-done.19.b2), channel_id=1, source_target_pairs={{0,28},{4,0},{8,4},{12,8},{16,12},{20,16},{24,20},{28,24},{1,29},{... | collective-permute-start | bytes 786440 | tf_op jit(solution)/shard_map/ppermute | solution.py:25
  45.5 1.5 %collective-permute-done.7.b2 = bf16[1024,128]{1,0:T(8,128)(2,1)S(1)} collective-permute-done((bf16[1024,128]{1,0:T(8,128)(2,1)S(1)}, bf16[1024,128]{1,0:T(8,128)(2,1)S(1)}, u32[]{:S(2)}, u32[]{:S(2)}) %collective-permute-start.7) | collective-permute-done | bytes 262176 | tf_op jit(solution)/shard_map/ppermute | solution.py:25
  47.0 3.7 %collective-permute-start.10 = (bf16[1024,128]{1,0:T(8,128)(2,1)S(1)}, bf16[1024,128]{1,0:T(8,128)(2,1)S(1)}, u32[]{:S(2)}, u32[]{:S(2)}) collective-permute-start(bf16[1024,128]{1,0:T(8,128)(2,1)S(1)} %collective-permute-done.7.b2), channel_id=1, source_target_pairs={{0,28},{4,0},{8,4},{12,8},{16,12},{20,16},{24,20},{28,24},{1,29},{... | collective-permute-start | bytes 786440 | tf_op jit(solution)/shard_map/ppermute | solution.py:25
  53.8 3.3 %collective-permute-start.25 = (bf16[512,128]{1,0:T(8,128)(2,1)S(1)}, bf16[512,128]{1,0:T(8,128)(2,1)S(1)}, u32[]{:S(2)}, u32[]{:S(2)}) collective-permute-start(bf16[512,128]{1,0:T(8,128)(2,1)S(1)} %slice.24), channel_id=1, source_target_pairs={{0,4},{4,8},{8,12},{12,16},{16,20},{20,24},{24,28},{28,0},{1,5},{5... | collective-permute-start | bytes 393224 | tf_op jit(solution)/shard_map/ppermute | solution.py:25
  57.2 4.2 %collective-permute-done.25.f4 = bf16[512,128]{1,0:T(8,128)(2,1)S(1)} collective-permute-done((bf16[512,128]{1,0:T(8,128)(2,1)S(1)}, bf16[512,128]{1,0:T(8,128)(2,1)S(1)}, u32[]{:S(2)}, u32[]{:S(2)}) %collective-permute-start.25) | collective-permute-done | bytes 131104 | tf_op jit(solution)/shard_map/ppermute | solution.py:25
  63.4 1.7 %collective-permute-start.27 = (bf16[1024,128]{1,0:T(8,128)(2,1)S(1)}, bf16[1024,128]{1,0:T(8,128)(2,1)S(1)}, u32[]{:S(2)}, u32[]{:S(2)}) collective-permute-start(bf16[1024,128]{1,0:T(8,128)(2,1)S(1)} %get-tuple-element.82), channel_id=1, source_target_pairs={{0,2},{1,3},{2,0},{3,1},{32,34},{33,35},{34,32},{35,33},{4,6},{5,7... | collective-permute-start | bytes 786440 | tf_op jit(solution)/shard_map/ppermute | solution.py:34
  66.1 2.4 %collective-permute-start.13 = (bf16[512,128]{1,0:T(8,128)(2,1)S(1)}, bf16[512,128]{1,0:T(8,128)(2,1)S(1)}, u32[]{:S(2)}, u32[]{:S(2)}) collective-permute-start(bf16[512,128]{1,0:T(8,128)(2,1)S(1)} %slice.22), channel_id=1, source_target_pairs={{0,28},{4,0},{8,4},{12,8},{16,12},{20,16},{24,20},{28,24},{1,29},{... | collective-permute-start | bytes 393224 | tf_op jit(solution)/shard_map/ppermute | solution.py:25
  69.2 1.8 %collective-permute-start.29 = (bf16[1024,128]{1,0:T(8,128)(2,1)S(1)}, bf16[1024,128]{1,0:T(8,128)(2,1)S(1)}, u32[]{:S(2)}, u32[]{:S(2)}) collective-permute-start(bf16[1024,128]{1,0:T(8,128)(2,1)S(1)} %get-tuple-element.84), channel_id=1, source_target_pairs={{0,3},{1,2},{2,1},{3,0},{32,33},{33,32},{34,35},{35,34},{4,7},{5,6... | collective-permute-start | bytes 786440 | tf_op jit(solution)/shard_map/ppermute | solution.py:34
  72.6 2.8 %collective-permute-start.21 = (bf16[1024,128]{1,0:T(8,128)(2,1)S(1)}, bf16[1024,128]{1,0:T(8,128)(2,1)S(1)}, u32[]{:S(2)}, u32[]{:S(2)}) collective-permute-start(bf16[1024,128]{1,0:T(8,128)(2,1)S(1)} %get-tuple-element.75), channel_id=1, source_target_pairs={{0,2},{1,3},{2,0},{3,1},{32,34},{33,35},{34,32},{35,33},{4,6},{5,7... | collective-permute-start | bytes 786440 | tf_op jit(solution)/shard_map/ppermute | solution.py:34
  77.7 6.6 %collective-permute-done.29.three = bf16[1024,128]{1,0:T(8,128)(2,1)S(1)} collective-permute-done((bf16[1024,128]{1,0:T(8,128)(2,1)S(1)}, bf16[1024,128]{1,0:T(8,128)(2,1)S(1)}, u32[]{:S(2)}, u32[]{:S(2)}) %collective-permute-start.29) | collective-permute-done | bytes 262176 | tf_op jit(solution)/shard_map/ppermute | solution.py:34
  85.2 1.8 %collective-permute-done.22.two = bf16[1024,128]{1,0:T(8,128)(2,1)S(1)} collective-permute-done((bf16[1024,128]{1,0:T(8,128)(2,1)S(1)}, bf16[1024,128]{1,0:T(8,128)(2,1)S(1)}, u32[]{:S(2)}, u32[]{:S(2)}) %collective-permute-start.22) | collective-permute-done | bytes 262176 | tf_op jit(solution)/shard_map/ppermute | solution.py:34
  (54 shorter events, 21.3 us)
Async XLA Ops:
  3.0 9.3 %collective-permute-start = (f32[32,128]{1,0:T(8,128)S(1)}, f32[32,128]{1,0:T(8,128)S(1)}, u32[]{:S(2)}, u32[]{:S(2)}) collective-permute-start(f32[32,128]{1,0:T(8,128)S(1)} %get-tuple-element.53.refs_0_.rest_0_), channel_id=1, source_target_pairs={{0,128},{64,192},{1,129},{65,193},{2,130},{66,194},{3,131},{67,195... | collective-permute-start | bytes 49160 | tf_op jit(solution)/shard_map/ppermute | solution.py:44
  16.1 13.0 %collective-permute-start.16 = (bf16[1024,128]{1,0:T(8,128)(2,1)S(1)}, bf16[1024,128]{1,0:T(8,128)(2,1)S(1)}, u32[]{:S(2)}, u32[]{:S(2)}) collective-permute-start(bf16[1024,128]{1,0:T(8,128)(2,1)S(1)} %get-tuple-element.69.here), channel_id=1, source_target_pairs={{0,4},{4,8},{8,12},{12,16},{16,20},{20,24},{24,28},{28,0},{1,5},{5... | collective-permute-start | bytes 786440 | tf_op jit(solution)/shard_map/ppermute | solution.py:25
  18.1 11.0 %collective-permute-start.17 = (bf16[1024,128]{1,0:T(8,128)(2,1)S(1)}, bf16[1024,128]{1,0:T(8,128)(2,1)S(1)}, u32[]{:S(2)}, u32[]{:S(2)}) collective-permute-start(bf16[1024,128]{1,0:T(8,128)(2,1)S(1)} %get-tuple-element.69.here), channel_id=1, source_target_pairs={{0,28},{4,0},{8,4},{12,8},{16,12},{20,16},{24,20},{28,24},{1,29},{... | collective-permute-start | bytes 786440 | tf_op jit(solution)/shard_map/ppermute | solution.py:25
  22.1 12.6 %collective-permute-start.4 = (bf16[1024,128]{1,0:T(8,128)(2,1)S(1)}, bf16[1024,128]{1,0:T(8,128)(2,1)S(1)}, u32[]{:S(2)}, u32[]{:S(2)}) collective-permute-start(bf16[1024,128]{1,0:T(8,128)(2,1)S(1)} %get-tuple-element.58.here), channel_id=1, source_target_pairs={{0,4},{4,8},{8,12},{12,16},{16,20},{20,24},{24,28},{28,0},{1,5},{5... | collective-permute-start | bytes 786440 | tf_op jit(solution)/shard_map/ppermute | solution.py:25
  22.1 12.6 %collective-permute-start.5 = (bf16[1024,128]{1,0:T(8,128)(2,1)S(1)}, bf16[1024,128]{1,0:T(8,128)(2,1)S(1)}, u32[]{:S(2)}, u32[]{:S(2)}) collective-permute-start(bf16[1024,128]{1,0:T(8,128)(2,1)S(1)} %get-tuple-element.58.here), channel_id=1, source_target_pairs={{0,28},{4,0},{8,4},{12,8},{16,12},{20,16},{24,20},{28,24},{1,29},{... | collective-permute-start | bytes 786440 | tf_op jit(solution)/shard_map/ppermute | solution.py:25
  25.4 12.6 %collective-permute-start.14 = (bf16[8,128,128]{2,1,0:T(8,128)(2,1)S(1)}, bf16[8,128,128]{2,1,0:T(8,128)(2,1)S(1)}, u32[]{:S(2)}, u32[]{:S(2)}) collective-permute-start(bf16[8,128,128]{2,1,0:T(8,128)(2,1)S(1)} %get-tuple-element.67), channel_id=1, source_target_pairs={{0,1},{1,0},{2,3},{3,2},{32,35},{33,34},{34,33},{35,32},{4,5},{5,4... | collective-permute-start | bytes 786440 | tf_op jit(solution)/shard_map/ppermute | solution.py:34
  29.2 12.2 %collective-permute-start.18 = (bf16[1024,128]{1,0:T(8,128)(2,1)S(1)}, bf16[1024,128]{1,0:T(8,128)(2,1)S(1)}, u32[]{:S(2)}, u32[]{:S(2)}) collective-permute-start(bf16[1024,128]{1,0:T(8,128)(2,1)S(1)} %collective-permute-done.16.f1), channel_id=1, source_target_pairs={{0,4},{4,8},{8,12},{12,16},{16,20},{20,24},{24,28},{28,0},{1,5},{5... | collective-permute-start | bytes 786440 | tf_op jit(solution)/shard_map/ppermute | solution.py:25
  29.2 12.1 %collective-permute-start.19 = (bf16[1024,128]{1,0:T(8,128)(2,1)S(1)}, bf16[1024,128]{1,0:T(8,128)(2,1)S(1)}, u32[]{:S(2)}, u32[]{:S(2)}) collective-permute-start(bf16[1024,128]{1,0:T(8,128)(2,1)S(1)} %collective-permute-done.17.b1), channel_id=1, source_target_pairs={{0,28},{4,0},{8,4},{12,8},{16,12},{20,16},{24,20},{28,24},{1,29},{... | collective-permute-start | bytes 786440 | tf_op jit(solution)/shard_map/ppermute | solution.py:25
  34.8 10.8 %collective-permute-start.6 = (bf16[1024,128]{1,0:T(8,128)(2,1)S(1)}, bf16[1024,128]{1,0:T(8,128)(2,1)S(1)}, u32[]{:S(2)}, u32[]{:S(2)}) collective-permute-start(bf16[1024,128]{1,0:T(8,128)(2,1)S(1)} %collective-permute-done.4.f1), channel_id=1, source_target_pairs={{0,4},{4,8},{8,12},{12,16},{16,20},{20,24},{24,28},{28,0},{1,5},{5... | collective-permute-start | bytes 786440 | tf_op jit(solution)/shard_map/ppermute | solution.py:25
  34.8 8.7 %collective-permute-start.8 = (bf16[4,128,128]{2,1,0:T(8,128)(2,1)S(1)}, bf16[4,128,128]{2,1,0:T(8,128)(2,1)S(1)}, u32[]{:S(2)}, u32[]{:S(2)}) collective-permute-start(bf16[4,128,128]{2,1,0:T(8,128)(2,1)S(1)} %get-tuple-element.62), channel_id=1, source_target_pairs={{0,2},{1,3},{2,0},{3,1},{32,34},{33,35},{34,32},{35,33},{4,6},{5,7... | collective-permute-start | bytes 393224 | tf_op jit(solution)/shard_map/ppermute | solution.py:34
  38.0 9.1 %collective-permute-start.7 = (bf16[1024,128]{1,0:T(8,128)(2,1)S(1)}, bf16[1024,128]{1,0:T(8,128)(2,1)S(1)}, u32[]{:S(2)}, u32[]{:S(2)}) collective-permute-start(bf16[1024,128]{1,0:T(8,128)(2,1)S(1)} %collective-permute-done.5.b1), channel_id=1, source_target_pairs={{0,28},{4,0},{8,4},{12,8},{16,12},{20,16},{24,20},{28,24},{1,29},{... | collective-permute-start | bytes 786440 | tf_op jit(solution)/shard_map/ppermute | solution.py:25
  41.3 10.1 %collective-permute-start.15 = (bf16[8,128,128]{2,1,0:T(8,128)(2,1)S(1)}, bf16[8,128,128]{2,1,0:T(8,128)(2,1)S(1)}, u32[]{:S(2)}, u32[]{:S(2)}) collective-permute-start(bf16[8,128,128]{2,1,0:T(8,128)(2,1)S(1)} %collective-permute-done.14.near), channel_id=1, source_target_pairs={{0,32},{32,0},{1,33},{33,1},{2,34},{34,2},{3,35},{35,3},{4,36},{36... | collective-permute-start | bytes 786440 | tf_op jit(solution)/shard_map/ppermute | solution.py:25
  41.3 11.3 %collective-permute-start.20 = (bf16[1024,128]{1,0:T(8,128)(2,1)S(1)}, bf16[1024,128]{1,0:T(8,128)(2,1)S(1)}, u32[]{:S(2)}, u32[]{:S(2)}) collective-permute-start(bf16[1024,128]{1,0:T(8,128)(2,1)S(1)} %collective-permute-done.19.b2), channel_id=1, source_target_pairs={{0,28},{4,0},{8,4},{12,8},{16,12},{20,16},{24,20},{28,24},{1,29},{... | collective-permute-start | bytes 786440 | tf_op jit(solution)/shard_map/ppermute | solution.py:25
  43.4 10.4 %collective-permute-start.24 = (bf16[1024,128]{1,0:T(8,128)(2,1)S(1)}, bf16[1024,128]{1,0:T(8,128)(2,1)S(1)}, u32[]{:S(2)}, u32[]{:S(2)}) collective-permute-start(bf16[1024,128]{1,0:T(8,128)(2,1)S(1)} %collective-permute-done.18.f2), channel_id=1, source_target_pairs={{0,4},{4,8},{8,12},{12,16},{16,20},{20,24},{24,28},{28,0},{1,5},{5... | collective-permute-start | bytes 786440 | tf_op jit(solution)/shard_map/ppermute | solution.py:25
  47.0 18.0 %collective-permute-start.10 = (bf16[1024,128]{1,0:T(8,128)(2,1)S(1)}, bf16[1024,128]{1,0:T(8,128)(2,1)S(1)}, u32[]{:S(2)}, u32[]{:S(2)}) collective-permute-start(bf16[1024,128]{1,0:T(8,128)(2,1)S(1)} %collective-permute-done.7.b2), channel_id=1, source_target_pairs={{0,28},{4,0},{8,4},{12,8},{16,12},{20,16},{24,20},{28,24},{1,29},{... | collective-permute-start | bytes 786440 | tf_op jit(solution)/shard_map/ppermute | solution.py:25
  50.7 14.3 %collective-permute-start.9 = (bf16[1024,128]{1,0:T(8,128)(2,1)S(1)}, bf16[1024,128]{1,0:T(8,128)(2,1)S(1)}, u32[]{:S(2)}, u32[]{:S(2)}) collective-permute-start(bf16[1024,128]{1,0:T(8,128)(2,1)S(1)} %collective-permute-done.6.f2), channel_id=1, source_target_pairs={{0,4},{4,8},{8,12},{12,16},{16,20},{20,24},{24,28},{28,0},{1,5},{5... | collective-permute-start | bytes 786440 | tf_op jit(solution)/shard_map/ppermute | solution.py:25
  53.8 7.6 %collective-permute-start.25 = (bf16[512,128]{1,0:T(8,128)(2,1)S(1)}, bf16[512,128]{1,0:T(8,128)(2,1)S(1)}, u32[]{:S(2)}, u32[]{:S(2)}) collective-permute-start(bf16[512,128]{1,0:T(8,128)(2,1)S(1)} %slice.24), channel_id=1, source_target_pairs={{0,4},{4,8},{8,12},{12,16},{16,20},{20,24},{24,28},{28,0},{1,5},{5... | collective-permute-start | bytes 393224 | tf_op jit(solution)/shard_map/ppermute | solution.py:25
  63.4 12.7 %collective-permute-start.27 = (bf16[1024,128]{1,0:T(8,128)(2,1)S(1)}, bf16[1024,128]{1,0:T(8,128)(2,1)S(1)}, u32[]{:S(2)}, u32[]{:S(2)}) collective-permute-start(bf16[1024,128]{1,0:T(8,128)(2,1)S(1)} %get-tuple-element.82), channel_id=1, source_target_pairs={{0,2},{1,3},{2,0},{3,1},{32,34},{33,35},{34,32},{35,33},{4,6},{5,7... | collective-permute-start | bytes 786440 | tf_op jit(solution)/shard_map/ppermute | solution.py:34
  65.1 6.3 %collective-permute-start.12 = (bf16[512,128]{1,0:T(8,128)(2,1)S(1)}, bf16[512,128]{1,0:T(8,128)(2,1)S(1)}, u32[]{:S(2)}, u32[]{:S(2)}) collective-permute-start(bf16[512,128]{1,0:T(8,128)(2,1)S(1)} %slice.21), channel_id=1, source_target_pairs={{0,4},{4,8},{8,12},{12,16},{16,20},{20,24},{24,28},{28,0},{1,5},{5... | collective-permute-start | bytes 393224 | tf_op jit(solution)/shard_map/ppermute | solution.py:25
  68.5 9.2 %collective-permute-start.28 = (bf16[1024,128]{1,0:T(8,128)(2,1)S(1)}, bf16[1024,128]{1,0:T(8,128)(2,1)S(1)}, u32[]{:S(2)}, u32[]{:S(2)}) collective-permute-start(bf16[1024,128]{1,0:T(8,128)(2,1)S(1)} %get-tuple-element.83), channel_id=1, source_target_pairs={{0,1},{1,0},{2,3},{3,2},{32,35},{33,34},{34,33},{35,32},{4,5},{5,4... | collective-permute-start | bytes 786440 | tf_op jit(solution)/shard_map/ppermute | solution.py:34
  69.2 15.2 %collective-permute-start.29 = (bf16[1024,128]{1,0:T(8,128)(2,1)S(1)}, bf16[1024,128]{1,0:T(8,128)(2,1)S(1)}, u32[]{:S(2)}, u32[]{:S(2)}) collective-permute-start(bf16[1024,128]{1,0:T(8,128)(2,1)S(1)} %get-tuple-element.84), channel_id=1, source_target_pairs={{0,3},{1,2},{2,1},{3,0},{32,33},{33,32},{34,35},{35,34},{4,7},{5,6... | collective-permute-start | bytes 786440 | tf_op jit(solution)/shard_map/ppermute | solution.py:34
  72.6 12.6 %collective-permute-start.21 = (bf16[1024,128]{1,0:T(8,128)(2,1)S(1)}, bf16[1024,128]{1,0:T(8,128)(2,1)S(1)}, u32[]{:S(2)}, u32[]{:S(2)}) collective-permute-start(bf16[1024,128]{1,0:T(8,128)(2,1)S(1)} %get-tuple-element.75), channel_id=1, source_target_pairs={{0,2},{1,3},{2,0},{3,1},{32,34},{33,35},{34,32},{35,33},{4,6},{5,7... | collective-permute-start | bytes 786440 | tf_op jit(solution)/shard_map/ppermute | solution.py:34
  75.4 11.5 %collective-permute-start.22 = (bf16[1024,128]{1,0:T(8,128)(2,1)S(1)}, bf16[1024,128]{1,0:T(8,128)(2,1)S(1)}, u32[]{:S(2)}, u32[]{:S(2)}) collective-permute-start(bf16[1024,128]{1,0:T(8,128)(2,1)S(1)} %get-tuple-element.76), channel_id=1, source_target_pairs={{0,1},{1,0},{2,3},{3,2},{32,35},{33,34},{34,33},{35,32},{4,5},{5,4... | collective-permute-start | bytes 786440 | tf_op jit(solution)/shard_map/ppermute | solution.py:34
  76.1 12.1 %collective-permute-start.23 = (bf16[1024,128]{1,0:T(8,128)(2,1)S(1)}, bf16[1024,128]{1,0:T(8,128)(2,1)S(1)}, u32[]{:S(2)}, u32[]{:S(2)}) collective-permute-start(bf16[1024,128]{1,0:T(8,128)(2,1)S(1)} %get-tuple-element.77), channel_id=1, source_target_pairs={{0,3},{1,2},{2,1},{3,0},{32,33},{33,32},{34,35},{35,34},{4,7},{5,6... | collective-permute-start | bytes 786440 | tf_op jit(solution)/shard_map/ppermute | solution.py:34
  (7 other events, 38.4 us)

commit v6 on v5

--- a/solution.py
+++ b/solution.py
@@ -17,7 +17,7 @@
 LOADS = 4
 BACK = (0, 2, 3, 1)
 VMEM_LIMIT = 16 * 1024 * 1024
-ROW_TILE = 256
+ROW_TILE = 512
 
 
 def shifted(value, axis, steps):

time: 89.3 us -> 89.3 us (level)
  no operation moved by 1% of the time
where the time goes in v6:
time: 89.3 us; the launch traced here: 89.2 us
  starting transfers between devices  50 us (56%)
  waiting for transfers between devices  27.3 us (31%)
  Pallas kernels  11.5 us (13%)
    ppermute x19, starting transfers between devices, shifted(): lax.ppermute(value, axis, [(at, (at + steps) % count) for at in range(cou...  30.1 us
    ppermute x19, waiting for transfers between devices, shifted(): lax.ppermute(value, axis, [(at, (at + steps) % count) for at in range(cou...  15.7 us
    ppermute x8, starting transfers between devices, swapped(): return lax.ppermute(value, ('core', 'y'), pairs)  13.2 us
    pallas_call x11, Pallas kernels, call(): pl.pallas_call(kernel, out_shape=shapes, scratch_shapes=scratch, compiler...  11.5 us
    ppermute x8, waiting for transfers between devices, swapped(): return lax.ppermute(value, ('core', 'y'), pairs)  10.6 us
    ppermute x3, starting transfers between devices, from_behind(): lax.ppermute(value, axis, [(at, at + steps) for at in range(count - steps)])  6.61 us
  transfers between devices with their start and end apart: 30, of which 15 were waited for; matrix products, arithmetic and copies ran while one was open for 0% of the time, Pallas kernels for 7%

profile of v6, /device:TPU:2, one launch (start us, length us, event | category | flops | bytes accessed | tf_op | source)
XLA Modules:
  0.0 89.2 jit_solution(1075415975458612809)
XLA Ops:
  0.0 3.0 %states.1 = (f32[256,8,128]{2,1,0:T(8,128)S(1)}, f32[16,8,128]{2,1,0:T(8,128)S(1)}, f32[32,128]{1,0:T(8,128)S(1)}, f32[64,128]{1,0:T(8,128)S(1)}) custom-call(bf16[3,8,256,128]{3,2,1,0:T(8,128)(2,1)} %bitcast.7, f32[3,3,128]{2,1,0:T(4,128)} %taps_hbm.1, f32[16,128]{1,0:T(8,128)} %rate_hbm.1, f32[16,128]{1,0:T(8,128)} %residue_hbm.1, f32[1,128]{1,0:T(1,128)} %bitcast.9), custom_call_target="tpu_custom_call" | custom-call | flops 11534336 | bytes 2757632 | tf_op jit(solution)/shard_map/states/pallas_call | solution.py:367
  3.0 4.0 %collective-permute-start = (f32[32,128]{1,0:T(8,128)S(1)}, f32[32,128]{1,0:T(8,128)S(1)}, u32[]{:S(2)}, u32[]{:S(2)}) collective-permute-start(f32[32,128]{1,0:T(8,128)S(1)} %get-tuple-element.53.refs_0_.rest_0_), channel_id=1, source_target_pairs={{0,128},{64,192},{1,129},{65,193},{2,130},{66,194},{3,131},{67,195... | collective-permute-start | bytes 49160 | tf_op jit(solution)/shard_map/ppermute | solution.py:44
  7.7 1.9 %collective-permute-start.2 = (f32[32,128]{1,0:T(8,128)S(1)}, f32[32,128]{1,0:T(8,128)S(1)}, u32[]{:S(2)}, u32[]{:S(2)}) collective-permute-start(f32[32,128]{1,0:T(8,128)S(1)} %get-tuple-element.53.refs_0_.rest_0_), channel_id=1, source_target_pairs={{0,64},{64,128},{128,192},{1,65},{65,129},{129,193},{2,66},{66,130... | collective-permute-start | bytes 49160 | tf_op jit(solution)/shard_map/ppermute | solution.py:44
  10.8 1.5 %local_conv_query.1 = (f32[128,8,128]{2,1,0:T(8,128)S(1)}, f32[256,8,128]{2,1,0:T(8,128)S(1)}) custom-call(bf16[3,8,256,128]{3,2,1,0:T(8,128)(2,1)} %bitcast.8, f32[64,128]{1,0:T(8,128)S(1)} %get-tuple-element.45.param_ref, f32[256,8,128]{2,1,0:T(8,128)S(1)} %get-tuple-element.46.signal_ref, f32[16,8,128]{2,1,0:T(8,128)S(1)} %get-tuple-element.48.start_ref), custom_call_target="tpu_custom_call" | custom-call | flops 10485760 | bytes 4292608 | tf_op jit(solution)/shard_map/local_conv_query/pallas_call | solution.py:367
  16.1 2.0 %collective-permute-start.16 = (bf16[1024,128]{1,0:T(8,128)(2,1)S(1)}, bf16[1024,128]{1,0:T(8,128)(2,1)S(1)}, u32[]{:S(2)}, u32[]{:S(2)}) collective-permute-start(bf16[1024,128]{1,0:T(8,128)(2,1)S(1)} %get-tuple-element.69.here), channel_id=1, source_target_pairs={{0,4},{4,8},{8,12},{12,16},{16,20},{20,24},{24,28},{28,0},{1,5},{5... | collective-permute-start | bytes 786440 | tf_op jit(solution)/shard_map/ppermute | solution.py:25
  18.1 4.0 %collective-permute-start.17 = (bf16[1024,128]{1,0:T(8,128)(2,1)S(1)}, bf16[1024,128]{1,0:T(8,128)(2,1)S(1)}, u32[]{:S(2)}, u32[]{:S(2)}) collective-permute-start(bf16[1024,128]{1,0:T(8,128)(2,1)S(1)} %get-tuple-element.69.here), channel_id=1, source_target_pairs={{0,28},{4,0},{8,4},{12,8},{16,12},{20,16},{24,20},{28,24},{1,29},{... | collective-permute-start | bytes 786440 | tf_op jit(solution)/shard_map/ppermute | solution.py:25
  22.1 3.2 %collective-permute-start.5 = (bf16[1024,128]{1,0:T(8,128)(2,1)S(1)}, bf16[1024,128]{1,0:T(8,128)(2,1)S(1)}, u32[]{:S(2)}, u32[]{:S(2)}) collective-permute-start(bf16[1024,128]{1,0:T(8,128)(2,1)S(1)} %get-tuple-element.58.here), channel_id=1, source_target_pairs={{0,28},{4,0},{8,4},{12,8},{16,12},{20,16},{24,20},{28,24},{1,29},{... | collective-permute-start | bytes 786440 | tf_op jit(solution)/shard_map/ppermute | solution.py:25
  25.4 1.7 %collective-permute-start.14 = (bf16[8,128,128]{2,1,0:T(8,128)(2,1)S(1)}, bf16[8,128,128]{2,1,0:T(8,128)(2,1)S(1)}, u32[]{:S(2)}, u32[]{:S(2)}) collective-permute-start(bf16[8,128,128]{2,1,0:T(8,128)(2,1)S(1)} %get-tuple-element.67), channel_id=1, source_target_pairs={{0,1},{1,0},{2,3},{3,2},{32,35},{33,34},{34,33},{35,32},{4,5},{5,4... | collective-permute-start | bytes 786440 | tf_op jit(solution)/shard_map/ppermute | solution.py:34
  27.1 2.1 %collective-permute-done.16.f1 = bf16[1024,128]{1,0:T(8,128)(2,1)S(1)} collective-permute-done((bf16[1024,128]{1,0:T(8,128)(2,1)S(1)}, bf16[1024,128]{1,0:T(8,128)(2,1)S(1)}, u32[]{:S(2)}, u32[]{:S(2)}) %collective-permute-start.16) | collective-permute-done | bytes 262176 | tf_op jit(solution)/shard_map/ppermute | solution.py:25
  29.2 3.3 %collective-permute-start.19 = (bf16[1024,128]{1,0:T(8,128)(2,1)S(1)}, bf16[1024,128]{1,0:T(8,128)(2,1)S(1)}, u32[]{:S(2)}, u32[]{:S(2)}) collective-permute-start(bf16[1024,128]{1,0:T(8,128)(2,1)S(1)} %collective-permute-done.17.b1), channel_id=1, source_target_pairs={{0,28},{4,0},{8,4},{12,8},{16,12},{20,16},{24,20},{28,24},{1,29},{... | collective-permute-start | bytes 786440 | tf_op jit(solution)/shard_map/ppermute | solution.py:25
  32.5 2.3 %collective-permute-done.4.f1 = bf16[1024,128]{1,0:T(8,128)(2,1)S(1)} collective-permute-done((bf16[1024,128]{1,0:T(8,128)(2,1)S(1)}, bf16[1024,128]{1,0:T(8,128)(2,1)S(1)}, u32[]{:S(2)}, u32[]{:S(2)}) %collective-permute-start.4) | collective-permute-done | bytes 262176 | tf_op jit(solution)/shard_map/ppermute | solution.py:25
  34.8 3.2 %collective-permute-start.8 = (bf16[4,128,128]{2,1,0:T(8,128)(2,1)S(1)}, bf16[4,128,128]{2,1,0:T(8,128)(2,1)S(1)}, u32[]{:S(2)}, u32[]{:S(2)}) collective-permute-start(bf16[4,128,128]{2,1,0:T(8,128)(2,1)S(1)} %get-tuple-element.62), channel_id=1, source_target_pairs={{0,2},{1,3},{2,0},{3,1},{32,34},{33,35},{34,32},{35,33},{4,6},{5,7... | collective-permute-start | bytes 393224 | tf_op jit(solution)/shard_map/ppermute | solution.py:34
  38.0 3.4 %collective-permute-start.7 = (bf16[1024,128]{1,0:T(8,128)(2,1)S(1)}, bf16[1024,128]{1,0:T(8,128)(2,1)S(1)}, u32[]{:S(2)}, u32[]{:S(2)}) collective-permute-start(bf16[1024,128]{1,0:T(8,128)(2,1)S(1)} %collective-permute-done.5.b1), channel_id=1, source_target_pairs={{0,28},{4,0},{8,4},{12,8},{16,12},{20,16},{24,20},{28,24},{1,29},{... | collective-permute-start | bytes 786440 | tf_op jit(solution)/shard_map/ppermute | solution.py:25
  41.3 2.1 %collective-permute-start.20 = (bf16[1024,128]{1,0:T(8,128)(2,1)S(1)}, bf16[1024,128]{1,0:T(8,128)(2,1)S(1)}, u32[]{:S(2)}, u32[]{:S(2)}) collective-permute-start(bf16[1024,128]{1,0:T(8,128)(2,1)S(1)} %collective-permute-done.19.b2), channel_id=1, source_target_pairs={{0,28},{4,0},{8,4},{12,8},{16,12},{20,16},{24,20},{28,24},{1,29},{... | collective-permute-start | bytes 786440 | tf_op jit(solution)/shard_map/ppermute | solution.py:25
  45.5 1.5 %collective-permute-done.7.b2 = bf16[1024,128]{1,0:T(8,128)(2,1)S(1)} collective-permute-done((bf16[1024,128]{1,0:T(8,128)(2,1)S(1)}, bf16[1024,128]{1,0:T(8,128)(2,1)S(1)}, u32[]{:S(2)}, u32[]{:S(2)}) %collective-permute-start.7) | collective-permute-done | bytes 262176 | tf_op jit(solution)/shard_map/ppermute | solution.py:25
  47.0 3.7 %collective-permute-start.10 = (bf16[1024,128]{1,0:T(8,128)(2,1)S(1)}, bf16[1024,128]{1,0:T(8,128)(2,1)S(1)}, u32[]{:S(2)}, u32[]{:S(2)}) collective-permute-start(bf16[1024,128]{1,0:T(8,128)(2,1)S(1)} %collective-permute-done.7.b2), channel_id=1, source_target_pairs={{0,28},{4,0},{8,4},{12,8},{16,12},{20,16},{24,20},{28,24},{1,29},{... | collective-permute-start | bytes 786440 | tf_op jit(solution)/shard_map/ppermute | solution.py:25
  53.8 3.3 %collective-permute-start.25 = (bf16[512,128]{1,0:T(8,128)(2,1)S(1)}, bf16[512,128]{1,0:T(8,128)(2,1)S(1)}, u32[]{:S(2)}, u32[]{:S(2)}) collective-permute-start(bf16[512,128]{1,0:T(8,128)(2,1)S(1)} %slice.24), channel_id=1, source_target_pairs={{0,4},{4,8},{8,12},{12,16},{16,20},{20,24},{24,28},{28,0},{1,5},{5... | collective-permute-start | bytes 393224 | tf_op jit(solution)/shard_map/ppermute | solution.py:25
  57.2 4.2 %collective-permute-done.25.f4 = bf16[512,128]{1,0:T(8,128)(2,1)S(1)} collective-permute-done((bf16[512,128]{1,0:T(8,128)(2,1)S(1)}, bf16[512,128]{1,0:T(8,128)(2,1)S(1)}, u32[]{:S(2)}, u32[]{:S(2)}) %collective-permute-start.25) | collective-permute-done | bytes 131104 | tf_op jit(solution)/shard_map/ppermute | solution.py:25
  63.4 1.7 %collective-permute-start.27 = (bf16[1024,128]{1,0:T(8,128)(2,1)S(1)}, bf16[1024,128]{1,0:T(8,128)(2,1)S(1)}, u32[]{:S(2)}, u32[]{:S(2)}) collective-permute-start(bf16[1024,128]{1,0:T(8,128)(2,1)S(1)} %get-tuple-element.82), channel_id=1, source_target_pairs={{0,2},{1,3},{2,0},{3,1},{32,34},{33,35},{34,32},{35,33},{4,6},{5,7... | collective-permute-start | bytes 786440 | tf_op jit(solution)/shard_map/ppermute | solution.py:34
  66.1 2.4 %collective-permute-start.13 = (bf16[512,128]{1,0:T(8,128)(2,1)S(1)}, bf16[512,128]{1,0:T(8,128)(2,1)S(1)}, u32[]{:S(2)}, u32[]{:S(2)}) collective-permute-start(bf16[512,128]{1,0:T(8,128)(2,1)S(1)} %slice.22), channel_id=1, source_target_pairs={{0,28},{4,0},{8,4},{12,8},{16,12},{20,16},{24,20},{28,24},{1,29},{... | collective-permute-start | bytes 393224 | tf_op jit(solution)/shard_map/ppermute | solution.py:25
  69.2 1.8 %collective-permute-start.29 = (bf16[1024,128]{1,0:T(8,128)(2,1)S(1)}, bf16[1024,128]{1,0:T(8,128)(2,1)S(1)}, u32[]{:S(2)}, u32[]{:S(2)}) collective-permute-start(bf16[1024,128]{1,0:T(8,128)(2,1)S(1)} %get-tuple-element.84), channel_id=1, source_target_pairs={{0,3},{1,2},{2,1},{3,0},{32,33},{33,32},{34,35},{35,34},{4,7},{5,6... | collective-permute-start | bytes 786440 | tf_op jit(solution)/shard_map/ppermute | solution.py:34
  72.6 2.8 %collective-permute-start.21 = (bf16[1024,128]{1,0:T(8,128)(2,1)S(1)}, bf16[1024,128]{1,0:T(8,128)(2,1)S(1)}, u32[]{:S(2)}, u32[]{:S(2)}) collective-permute-start(bf16[1024,128]{1,0:T(8,128)(2,1)S(1)} %get-tuple-element.75), channel_id=1, source_target_pairs={{0,2},{1,3},{2,0},{3,1},{32,34},{33,35},{34,32},{35,33},{4,6},{5,7... | collective-permute-start | bytes 786440 | tf_op jit(solution)/shard_map/ppermute | solution.py:34
  77.7 6.6 %collective-permute-done.29.three = bf16[1024,128]{1,0:T(8,128)(2,1)S(1)} collective-permute-done((bf16[1024,128]{1,0:T(8,128)(2,1)S(1)}, bf16[1024,128]{1,0:T(8,128)(2,1)S(1)}, u32[]{:S(2)}, u32[]{:S(2)}) %collective-permute-start.29) | collective-permute-done | bytes 262176 | tf_op jit(solution)/shard_map/ppermute | solution.py:34
  85.2 1.8 %collective-permute-done.22.two = bf16[1024,128]{1,0:T(8,128)(2,1)S(1)} collective-permute-done((bf16[1024,128]{1,0:T(8,128)(2,1)S(1)}, bf16[1024,128]{1,0:T(8,128)(2,1)S(1)}, u32[]{:S(2)}, u32[]{:S(2)}) %collective-permute-start.22) | collective-permute-done | bytes 262176 | tf_op jit(solution)/shard_map/ppermute | solution.py:34
  (54 shorter events, 21.3 us)
Async XLA Ops:
  3.0 9.3 %collective-permute-start = (f32[32,128]{1,0:T(8,128)S(1)}, f32[32,128]{1,0:T(8,128)S(1)}, u32[]{:S(2)}, u32[]{:S(2)}) collective-permute-start(f32[32,128]{1,0:T(8,128)S(1)} %get-tuple-element.53.refs_0_.rest_0_), channel_id=1, source_target_pairs={{0,128},{64,192},{1,129},{65,193},{2,130},{66,194},{3,131},{67,195... | collective-permute-start | bytes 49160 | tf_op jit(solution)/shard_map/ppermute | solution.py:44
  16.1 13.0 %collective-permute-start.16 = (bf16[1024,128]{1,0:T(8,128)(2,1)S(1)}, bf16[1024,128]{1,0:T(8,128)(2,1)S(1)}, u32[]{:S(2)}, u32[]{:S(2)}) collective-permute-start(bf16[1024,128]{1,0:T(8,128)(2,1)S(1)} %get-tuple-element.69.here), channel_id=1, source_target_pairs={{0,4},{4,8},{8,12},{12,16},{16,20},{20,24},{24,28},{28,0},{1,5},{5... | collective-permute-start | bytes 786440 | tf_op jit(solution)/shard_map/ppermute | solution.py:25
  18.1 11.0 %collective-permute-start.17 = (bf16[1024,128]{1,0:T(8,128)(2,1)S(1)}, bf16[1024,128]{1,0:T(8,128)(2,1)S(1)}, u32[]{:S(2)}, u32[]{:S(2)}) collective-permute-start(bf16[1024,128]{1,0:T(8,128)(2,1)S(1)} %get-tuple-element.69.here), channel_id=1, source_target_pairs={{0,28},{4,0},{8,4},{12,8},{16,12},{20,16},{24,20},{28,24},{1,29},{... | collective-permute-start | bytes 786440 | tf_op jit(solution)/shard_map/ppermute | solution.py:25
  22.1 12.6 %collective-permute-start.4 = (bf16[1024,128]{1,0:T(8,128)(2,1)S(1)}, bf16[1024,128]{1,0:T(8,128)(2,1)S(1)}, u32[]{:S(2)}, u32[]{:S(2)}) collective-permute-start(bf16[1024,128]{1,0:T(8,128)(2,1)S(1)} %get-tuple-element.58.here), channel_id=1, source_target_pairs={{0,4},{4,8},{8,12},{12,16},{16,20},{20,24},{24,28},{28,0},{1,5},{5... | collective-permute-start | bytes 786440 | tf_op jit(solution)/shard_map/ppermute | solution.py:25
  22.1 12.6 %collective-permute-start.5 = (bf16[1024,128]{1,0:T(8,128)(2,1)S(1)}, bf16[1024,128]{1,0:T(8,128)(2,1)S(1)}, u32[]{:S(2)}, u32[]{:S(2)}) collective-permute-start(bf16[1024,128]{1,0:T(8,128)(2,1)S(1)} %get-tuple-element.58.here), channel_id=1, source_target_pairs={{0,28},{4,0},{8,4},{12,8},{16,12},{20,16},{24,20},{28,24},{1,29},{... | collective-permute-start | bytes 786440 | tf_op jit(solution)/shard_map/ppermute | solution.py:25
  25.4 12.6 %collective-permute-start.14 = (bf16[8,128,128]{2,1,0:T(8,128)(2,1)S(1)}, bf16[8,128,128]{2,1,0:T(8,128)(2,1)S(1)}, u32[]{:S(2)}, u32[]{:S(2)}) collective-permute-start(bf16[8,128,128]{2,1,0:T(8,128)(2,1)S(1)} %get-tuple-element.67), channel_id=1, source_target_pairs={{0,1},{1,0},{2,3},{3,2},{32,35},{33,34},{34,33},{35,32},{4,5},{5,4... | collective-permute-start | bytes 786440 | tf_op jit(solution)/shard_map/ppermute | solution.py:34
  29.2 12.2 %collective-permute-start.18 = (bf16[1024,128]{1,0:T(8,128)(2,1)S(1)}, bf16[1024,128]{1,0:T(8,128)(2,1)S(1)}, u32[]{:S(2)}, u32[]{:S(2)}) collective-permute-start(bf16[1024,128]{1,0:T(8,128)(2,1)S(1)} %collective-permute-done.16.f1), channel_id=1, source_target_pairs={{0,4},{4,8},{8,12},{12,16},{16,20},{20,24},{24,28},{28,0},{1,5},{5... | collective-permute-start | bytes 786440 | tf_op jit(solution)/shard_map/ppermute | solution.py:25
  29.2 12.1 %collective-permute-start.19 = (bf16[1024,128]{1,0:T(8,128)(2,1)S(1)}, bf16[1024,128]{1,0:T(8,128)(2,1)S(1)}, u32[]{:S(2)}, u32[]{:S(2)}) collective-permute-start(bf16[1024,128]{1,0:T(8,128)(2,1)S(1)} %collective-permute-done.17.b1), channel_id=1, source_target_pairs={{0,28},{4,0},{8,4},{12,8},{16,12},{20,16},{24,20},{28,24},{1,29},{... | collective-permute-start | bytes 786440 | tf_op jit(solution)/shard_map/ppermute | solution.py:25
  34.8 10.8 %collective-permute-start.6 = (bf16[1024,128]{1,0:T(8,128)(2,1)S(1)}, bf16[1024,128]{1,0:T(8,128)(2,1)S(1)}, u32[]{:S(2)}, u32[]{:S(2)}) collective-permute-start(bf16[1024,128]{1,0:T(8,128)(2,1)S(1)} %collective-permute-done.4.f1), channel_id=1, source_target_pairs={{0,4},{4,8},{8,12},{12,16},{16,20},{20,24},{24,28},{28,0},{1,5},{5... | collective-permute-start | bytes 786440 | tf_op jit(solution)/shard_map/ppermute | solution.py:25
  34.8 8.7 %collective-permute-start.8 = (bf16[4,128,128]{2,1,0:T(8,128)(2,1)S(1)}, bf16[4,128,128]{2,1,0:T(8,128)(2,1)S(1)}, u32[]{:S(2)}, u32[]{:S(2)}) collective-permute-start(bf16[4,128,128]{2,1,0:T(8,128)(2,1)S(1)} %get-tuple-element.62), channel_id=1, source_target_pairs={{0,2},{1,3},{2,0},{3,1},{32,34},{33,35},{34,32},{35,33},{4,6},{5,7... | collective-permute-start | bytes 393224 | tf_op jit(solution)/shard_map/ppermute | solution.py:34
  38.0 9.1 %collective-permute-start.7 = (bf16[1024,128]{1,0:T(8,128)(2,1)S(1)}, bf16[1024,128]{1,0:T(8,128)(2,1)S(1)}, u32[]{:S(2)}, u32[]{:S(2)}) collective-permute-start(bf16[1024,128]{1,0:T(8,128)(2,1)S(1)} %collective-permute-done.5.b1), channel_id=1, source_target_pairs={{0,28},{4,0},{8,4},{12,8},{16,12},{20,16},{24,20},{28,24},{1,29},{... | collective-permute-start | bytes 786440 | tf_op jit(solution)/shard_map/ppermute | solution.py:25
  41.3 10.1 %collective-permute-start.15 = (bf16[8,128,128]{2,1,0:T(8,128)(2,1)S(1)}, bf16[8,128,128]{2,1,0:T(8,128)(2,1)S(1)}, u32[]{:S(2)}, u32[]{:S(2)}) collective-permute-start(bf16[8,128,128]{2,1,0:T(8,128)(2,1)S(1)} %collective-permute-done.14.near), channel_id=1, source_target_pairs={{0,32},{32,0},{1,33},{33,1},{2,34},{34,2},{3,35},{35,3},{4,36},{36... | collective-permute-start | bytes 786440 | tf_op jit(solution)/shard_map/ppermute | solution.py:25
  41.3 11.3 %collective-permute-start.20 = (bf16[1024,128]{1,0:T(8,128)(2,1)S(1)}, bf16[1024,128]{1,0:T(8,128)(2,1)S(1)}, u32[]{:S(2)}, u32[]{:S(2)}) collective-permute-start(bf16[1024,128]{1,0:T(8,128)(2,1)S(1)} %collective-permute-done.19.b2), channel_id=1, source_target_pairs={{0,28},{4,0},{8,4},{12,8},{16,12},{20,16},{24,20},{28,24},{1,29},{... | collective-permute-start | bytes 786440 | tf_op jit(solution)/shard_map/ppermute | solution.py:25
  43.4 10.4 %collective-permute-start.24 = (bf16[1024,128]{1,0:T(8,128)(2,1)S(1)}, bf16[1024,128]{1,0:T(8,128)(2,1)S(1)}, u32[]{:S(2)}, u32[]{:S(2)}) collective-permute-start(bf16[1024,128]{1,0:T(8,128)(2,1)S(1)} %collective-permute-done.18.f2), channel_id=1, source_target_pairs={{0,4},{4,8},{8,12},{12,16},{16,20},{20,24},{24,28},{28,0},{1,5},{5... | collective-permute-start | bytes 786440 | tf_op jit(solution)/shard_map/ppermute | solution.py:25
  47.0 18.0 %collective-permute-start.10 = (bf16[1024,128]{1,0:T(8,128)(2,1)S(1)}, bf16[1024,128]{1,0:T(8,128)(2,1)S(1)}, u32[]{:S(2)}, u32[]{:S(2)}) collective-permute-start(bf16[1024,128]{1,0:T(8,128)(2,1)S(1)} %collective-permute-done.7.b2), channel_id=1, source_target_pairs={{0,28},{4,0},{8,4},{12,8},{16,12},{20,16},{24,20},{28,24},{1,29},{... | collective-permute-start | bytes 786440 | tf_op jit(solution)/shard_map/ppermute | solution.py:25
  50.7 14.3 %collective-permute-start.9 = (bf16[1024,128]{1,0:T(8,128)(2,1)S(1)}, bf16[1024,128]{1,0:T(8,128)(2,1)S(1)}, u32[]{:S(2)}, u32[]{:S(2)}) collective-permute-start(bf16[1024,128]{1,0:T(8,128)(2,1)S(1)} %collective-permute-done.6.f2), channel_id=1, source_target_pairs={{0,4},{4,8},{8,12},{12,16},{16,20},{20,24},{24,28},{28,0},{1,5},{5... | collective-permute-start | bytes 786440 | tf_op jit(solution)/shard_map/ppermute | solution.py:25
  53.8 7.6 %collective-permute-start.25 = (bf16[512,128]{1,0:T(8,128)(2,1)S(1)}, bf16[512,128]{1,0:T(8,128)(2,1)S(1)}, u32[]{:S(2)}, u32[]{:S(2)}) collective-permute-start(bf16[512,128]{1,0:T(8,128)(2,1)S(1)} %slice.24), channel_id=1, source_target_pairs={{0,4},{4,8},{8,12},{12,16},{16,20},{20,24},{24,28},{28,0},{1,5},{5... | collective-permute-start | bytes 393224 | tf_op jit(solution)/shard_map/ppermute | solution.py:25
  63.4 12.7 %collective-permute-start.27 = (bf16[1024,128]{1,0:T(8,128)(2,1)S(1)}, bf16[1024,128]{1,0:T(8,128)(2,1)S(1)}, u32[]{:S(2)}, u32[]{:S(2)}) collective-permute-start(bf16[1024,128]{1,0:T(8,128)(2,1)S(1)} %get-tuple-element.82), channel_id=1, source_target_pairs={{0,2},{1,3},{2,0},{3,1},{32,34},{33,35},{34,32},{35,33},{4,6},{5,7... | collective-permute-start | bytes 786440 | tf_op jit(solution)/shard_map/ppermute | solution.py:34
  65.1 6.3 %collective-permute-start.12 = (bf16[512,128]{1,0:T(8,128)(2,1)S(1)}, bf16[512,128]{1,0:T(8,128)(2,1)S(1)}, u32[]{:S(2)}, u32[]{:S(2)}) collective-permute-start(bf16[512,128]{1,0:T(8,128)(2,1)S(1)} %slice.21), channel_id=1, source_target_pairs={{0,4},{4,8},{8,12},{12,16},{16,20},{20,24},{24,28},{28,0},{1,5},{5... | collective-permute-start | bytes 393224 | tf_op jit(solution)/shard_map/ppermute | solution.py:25
  68.5 9.2 %collective-permute-start.28 = (bf16[1024,128]{1,0:T(8,128)(2,1)S(1)}, bf16[1024,128]{1,0:T(8,128)(2,1)S(1)}, u32[]{:S(2)}, u32[]{:S(2)}) collective-permute-start(bf16[1024,128]{1,0:T(8,128)(2,1)S(1)} %get-tuple-element.83), channel_id=1, source_target_pairs={{0,1},{1,0},{2,3},{3,2},{32,35},{33,34},{34,33},{35,32},{4,5},{5,4... | collective-permute-start | bytes 786440 | tf_op jit(solution)/shard_map/ppermute | solution.py:34
  69.2 15.2 %collective-permute-start.29 = (bf16[1024,128]{1,0:T(8,128)(2,1)S(1)}, bf16[1024,128]{1,0:T(8,128)(2,1)S(1)}, u32[]{:S(2)}, u32[]{:S(2)}) collective-permute-start(bf16[1024,128]{1,0:T(8,128)(2,1)S(1)} %get-tuple-element.84), channel_id=1, source_target_pairs={{0,3},{1,2},{2,1},{3,0},{32,33},{33,32},{34,35},{35,34},{4,7},{5,6... | collective-permute-start | bytes 786440 | tf_op jit(solution)/shard_map/ppermute | solution.py:34
  72.6 12.6 %collective-permute-start.21 = (bf16[1024,128]{1,0:T(8,128)(2,1)S(1)}, bf16[1024,128]{1,0:T(8,128)(2,1)S(1)}, u32[]{:S(2)}, u32[]{:S(2)}) collective-permute-start(bf16[1024,128]{1,0:T(8,128)(2,1)S(1)} %get-tuple-element.75), channel_id=1, source_target_pairs={{0,2},{1,3},{2,0},{3,1},{32,34},{33,35},{34,32},{35,33},{4,6},{5,7... | collective-permute-start | bytes 786440 | tf_op jit(solution)/shard_map/ppermute | solution.py:34
  75.4 11.5 %collective-permute-start.22 = (bf16[1024,128]{1,0:T(8,128)(2,1)S(1)}, bf16[1024,128]{1,0:T(8,128)(2,1)S(1)}, u32[]{:S(2)}, u32[]{:S(2)}) collective-permute-start(bf16[1024,128]{1,0:T(8,128)(2,1)S(1)} %get-tuple-element.76), channel_id=1, source_target_pairs={{0,1},{1,0},{2,3},{3,2},{32,35},{33,34},{34,33},{35,32},{4,5},{5,4... | collective-permute-start | bytes 786440 | tf_op jit(solution)/shard_map/ppermute | solution.py:34
  76.1 12.1 %collective-permute-start.23 = (bf16[1024,128]{1,0:T(8,128)(2,1)S(1)}, bf16[1024,128]{1,0:T(8,128)(2,1)S(1)}, u32[]{:S(2)}, u32[]{:S(2)}) collective-permute-start(bf16[1024,128]{1,0:T(8,128)(2,1)S(1)} %get-tuple-element.77), channel_id=1, source_target_pairs={{0,3},{1,2},{2,1},{3,0},{32,33},{33,32},{34,35},{35,34},{4,7},{5,6... | collective-permute-start | bytes 786440 | tf_op jit(solution)/shard_map/ppermute | solution.py:34
  (7 other events, 38.4 us)
